TPU v7x, 32 devices: a whole 2x2x4 slice. The times are simulated.
32 devices in a mesh: dp: 8 (over y, x, core), seq: 4 (over z).
Axes of the slice: x: 2, y: 2, z: 4, core: 2. Of those that a mesh axis runs over, the one named last changes fastest.
Arguments:
- features: bfloat16 [4, 8, 2048, 512], P(None, 'dp', 'seq'), may hold values from -6 to 6
- lengths: int32 [4, 8], P(None, 'dp'), may hold values from 512 to 2048, as said below
- dw_weight: bfloat16 [2, 7, 512], P(None, None, 'dp'), may hold values from -2 to 2
- block_gains: bfloat16 [2, 2, 512], P(None, None, 'dp'), may hold values from 0.5 to 1.5
- block_biases: bfloat16 [2, 3, 512], P(None, None, 'dp'), may hold values from -1.75 to 1.75
- up_weight: bfloat16 [2, 512, 1536], P(None, 'dp'), may hold values from -0.25 to 0.25
- up_bias: bfloat16 [2, 1536], P(None, 'dp'), may hold values from -1.75 to 1.75
- down_weight: bfloat16 [2, 1536, 512], P(None, 'dp'), may hold values from -0.15625 to 0.15625
- head_gain: float32 [512], P('dp'), may hold values from 0.5 to 1.5
- head_shift: float32 [512], P('dp'), may hold values from -1.75 to 1.75
- head_weight: float32 [512, 1026], P('dp'), may hold values from -0.25 to 0.25
- head_bias: float32 [1026], replicated
- audio_grad: float32 [4, 8, 2048, 256], P(None, 'dp', 'seq'), may hold values from -6 to 6
Outputs:
- audio: float32 [4, 8, 2048, 256], P(None, 'dp', 'seq')
- feature_grad: float32 [4, 8, 2048, 512], P(None, 'dp', 'seq')
- dw_grad: float32 [2, 7, 512], P(None, None, 'dp')
- gains_grad: float32 [2, 2, 512], P(None, None, 'dp')
- biases_grad: float32 [2, 3, 512], P(None, None, 'dp')
- up_grad: float32 [2, 512, 1536], P(None, 'dp')
- up_bias_grad: float32 [2, 1536], P(None, 'dp')
- down_grad: float32 [2, 1536, 512], P(None, 'dp')
- head_gain_grad: float32 [512], P('dp')
- head_shift_grad: float32 [512], P('dp')
- head_weight_grad: float32 [512, 1026], P('dp')
- head_bias_grad: float32 [1026], replicated
Inputs may be any that keep to these rules, and one draw needn't show every extreme that they name: `lengths`: some utterance of each draw fills all 2048 frames.
All inputs are finite; a program needn't handle non-finite values.
Results may differ from a plain program's by a relative error of at most 0.018.
Values may be sent and summed in bfloat16 or wider, within the bound.
No kernel may reach another device: no remote copies, remote signals or barrier semaphores. Data moves between devices by JAX's collectives and lax.ppermute only.
A program may use at most 168 MiB of HBM per device.

v0:
```python
import math

import jax
import jax.numpy as jnp
from jax import lax
from jax.sharding import PartitionSpec as P

NFFT = 1024
HOP = 256
BINS = 513
KERNEL = 7
BLOCKS = 2


exact_mode = lax.Precision.HIGHEST
norm_eps = 1e-06
contract_rows = (((0,), (0,)), ((), ()))
contract_cols = (((1,), (1,)), ((), ()))


def padded_2(cells, sides, width):
    for axis, dim in sides:
        count = lax.axis_size(axis)
        ends = count - 1
        head = lax.slice_in_dim(cells, 0, width, axis=dim)
        tail = lax.slice_in_dim(cells, cells.shape[dim] - width, cells.shape[dim], axis=dim)
        cells = jnp.concatenate(
            [
                lax.ppermute(tail, axis, [(i, (i + 1) % count) for i in range(ends)]),
                cells,
                lax.ppermute(head, axis, [((i + 1) % count, i) for i in range(ends)]),
            ],
            axis=dim,
        )
    return cells


def for_sending(array):
    return jax.tree.map(lambda a: a.astype(jnp.bfloat16) if a.dtype == jnp.float32 else a, array)


def dft_tables():
    frequency = jnp.arange(BINS, dtype=jnp.int32)
    sample = jnp.arange(NFFT, dtype=jnp.int32)
    product = frequency[:, None] * sample[None, :] % NFFT
    angles = product.astype(jnp.float32) * (2.0 * math.pi / NFFT)
    edge = (frequency == 0) | (frequency == NFFT // 2)
    weight_row = jnp.where(edge, 1.0, 2.0).astype(jnp.float32) / NFFT
    return (jnp.cos(angles) * weight_row[:, None], -jnp.sin(angles) * weight_row[:, None])


def hann_window():
    sample = jnp.arange(NFFT, dtype=jnp.int32).astype(jnp.float32)
    return 0.5 - 0.5 * jnp.cos(sample * (2.0 * math.pi / NFFT))


def envelope_rows(row_ids, seq_rows, window):
    squared = window * window
    total = jnp.zeros((row_ids.shape[0], HOP), jnp.float32)
    for q in range(4):
        source = row_ids + 2 - q
        valid = ((source >= 0) & (source < seq_rows)).astype(jnp.float32)[:, None]
        total = total + valid * squared[q * HOP : (q + 1) * HOP][None, :]
    return total


def norm_forward(values, norm_gain, norm_shift):
    row_mean = jnp.mean(values, axis=-1, keepdims=True)
    centred = values - row_mean
    inv_std = lax.rsqrt(jnp.mean(centred * centred, axis=-1, keepdims=True) + norm_eps)
    unit_rows = centred * inv_std
    return (unit_rows * norm_gain + norm_shift, unit_rows, inv_std)


def norm_backward(normed_grad, unit_rows, inv_std, norm_gain):
    unit_grad = normed_grad * norm_gain
    inner = jnp.mean(unit_grad * unit_rows, axis=-1, keepdims=True)
    values_grad = inv_std * (
        unit_grad - jnp.mean(unit_grad, axis=-1, keepdims=True) - unit_rows * inner
    )
    return (values_grad, jnp.sum(normed_grad * unit_rows, axis=0), jnp.sum(normed_grad, axis=0))


def gelu_parts(pre_act):
    cumulative = 0.5 * (1.0 + lax.erf(pre_act * (1.0 / math.sqrt(2.0))))
    density = jnp.exp(-0.5 * pre_act * pre_act) * (1.0 / math.sqrt(2.0 * math.pi))
    return (pre_act * cumulative, cumulative + pre_act * density)


def block_forward(hidden, convnext_block_list, convnext_block):
    conv_taps = convnext_block_list[0][convnext_block]
    gains = convnext_block_list[1][convnext_block].astype(jnp.float32)
    biases = convnext_block_list[2][convnext_block].astype(jnp.float32)
    rows_here = hidden.shape[0]
    block_in = hidden.astype(jnp.bfloat16)
    padded = padded_2(block_in, (("seq", 0),), 3)
    padded_wide = padded.astype(jnp.float32)
    conv_out = jnp.zeros_like(hidden) + biases[0]
    for k in range(KERNEL):
        conv_out = conv_out + conv_taps[k].astype(jnp.float32) * padded_wide[k : k + rows_here]
    normed, unit_rows, inv_std = norm_forward(conv_out, gains[0], biases[1])
    normed_low = normed.astype(jnp.bfloat16)
    pre_act = jnp.dot(
        normed_low, convnext_block_list[3][convnext_block], preferred_element_type=jnp.float32
    ) + convnext_block_list[4][convnext_block].astype(jnp.float32)
    activated, gelu_slope = gelu_parts(pre_act)
    act_low = activated.astype(jnp.bfloat16)
    branch = (
        jnp.dot(act_low, convnext_block_list[5][convnext_block], preferred_element_type=jnp.float32)
        + biases[2]
    )
    saved_residuals = (padded_wide, unit_rows, inv_std, normed_low, gelu_slope, act_low, branch)
    return (hidden + gains[1] * branch, saved_residuals)


def convnext_block_reverse(incoming_gradient, convnext_block_list, convnext_block, saved_residuals):
    padded_wide, unit_rows, inv_std, normed_low, gelu_slope, act_low, branch = saved_residuals
    conv_taps = convnext_block_list[0][convnext_block].astype(jnp.float32)
    gains = convnext_block_list[1][convnext_block].astype(jnp.float32)
    rows_here = incoming_gradient.shape[0]
    scale_grad = jnp.sum(branch * incoming_gradient, axis=0)
    branch_grad = (gains[1] * incoming_gradient).astype(jnp.bfloat16)
    down_grad = lax.dot_general(
        act_low, branch_grad, contract_rows, preferred_element_type=jnp.float32
    )
    down_bias_grad = jnp.sum(branch_grad.astype(jnp.float32), axis=0)
    act_grad = lax.dot_general(
        branch_grad,
        convnext_block_list[5][convnext_block],
        contract_cols,
        preferred_element_type=jnp.float32,
    )
    pre_grad = (act_grad * gelu_slope).astype(jnp.bfloat16)
    up_grad = lax.dot_general(
        normed_low, pre_grad, contract_rows, preferred_element_type=jnp.float32
    )
    up_bias_grad = jnp.sum(pre_grad.astype(jnp.float32), axis=0)
    normed_grad = lax.dot_general(
        pre_grad,
        convnext_block_list[3][convnext_block],
        contract_cols,
        preferred_element_type=jnp.float32,
    )
    conv_wide, gain_grad, shift_grad = norm_backward(normed_grad, unit_rows, inv_std, gains[0])
    conv_grad = conv_wide.astype(jnp.bfloat16)
    grad_padded = padded_2(conv_grad, (("seq", 0),), 3).astype(jnp.float32)
    conv_low = conv_grad.astype(jnp.float32)
    tap_grads = jnp.stack(
        [jnp.sum(padded_wide[k : k + rows_here] * conv_low, axis=0) for k in range(KERNEL)]
    )
    input_grad = incoming_gradient
    for k in range(KERNEL):
        start = KERNEL - 1 - k
        input_grad = input_grad + conv_taps[k] * grad_padded[start : start + rows_here]
    grads = (
        tap_grads,
        jnp.stack([gain_grad, scale_grad]),
        jnp.stack([jnp.sum(conv_low, axis=0), shift_grad, down_bias_grad]),
        up_grad,
        up_bias_grad,
        down_grad,
    )
    return (input_grad, grads)


def head_forward(hidden, head, head_bias, tables, window, envelope, frame_mask):
    cos_table, sin_table = tables
    rows_here = hidden.shape[0]
    normed, unit_rows, inv_std = norm_forward(hidden, head[0], head[1])
    logits = (
        jnp.dot(normed, head[2], precision=exact_mode, preferred_element_type=jnp.float32)
        + head_bias
    )
    magnitude = jnp.exp(logits[:, :BINS])
    phase = logits[:, BINS:]
    real_part = magnitude * jnp.cos(phase)
    imag_part = magnitude * jnp.sin(phase)
    framed = jnp.dot(real_part, cos_table, precision=exact_mode, preferred_element_type=jnp.float32)
    framed = (
        framed
        + jnp.dot(imag_part, sin_table, precision=exact_mode, preferred_element_type=jnp.float32)
    ) * window
    summed_rows = jnp.zeros((rows_here + 4, HOP), jnp.float32)
    for q in range(4):
        quarter = framed[:, q * HOP : (q + 1) * HOP]
        summed_rows = summed_rows + jnp.pad(quarter, ((q, 4 - q), (0, 0)))
    rims = padded_2(summed_rows.astype(jnp.bfloat16), (("seq", 0),), 2).astype(summed_rows.dtype)
    own_rows = rims[4 : rows_here + 4]
    own_rows = own_rows + jnp.pad(rims[0:2], ((0, rows_here - 2), (0, 0)))
    own_rows = own_rows + jnp.pad(rims[rows_here + 6 : rows_here + 8], ((rows_here - 2, 0), (0, 0)))
    audio = own_rows / envelope * frame_mask
    return (audio, (normed, unit_rows, inv_std, real_part, imag_part))


def head_backward(cotangent, head, saved_residuals, tables, window, envelope, frame_mask):
    normed, unit_rows, inv_std, real_part, imag_part = saved_residuals
    cos_table, sin_table = tables
    rows_here = cotangent.shape[0]
    own_grad = cotangent * frame_mask / envelope
    grad_rows = padded_2(own_grad, (("seq", 0),), 2)
    framed_grad = jnp.concatenate([grad_rows[q : q + rows_here] for q in range(4)], axis=1) * window
    real_grad = lax.dot_general(
        framed_grad,
        cos_table,
        contract_cols,
        precision=exact_mode,
        preferred_element_type=jnp.float32,
    )
    imag_grad = lax.dot_general(
        framed_grad,
        sin_table,
        contract_cols,
        precision=exact_mode,
        preferred_element_type=jnp.float32,
    )
    log_grad = real_grad * real_part + imag_grad * imag_part
    phase_grad = imag_grad * real_part - real_grad * imag_part
    logit_grad = jnp.concatenate([log_grad, phase_grad], axis=1)
    weight_grad = lax.dot_general(
        normed, logit_grad, contract_rows, precision=exact_mode, preferred_element_type=jnp.float32
    )
    bias_sum = jnp.sum(logit_grad, axis=0)
    normed_grad = lax.dot_general(
        logit_grad, head[2], contract_cols, precision=exact_mode, preferred_element_type=jnp.float32
    )
    hidden_grad, gain_grad, shift_grad = norm_backward(normed_grad, unit_rows, inv_std, head[0])
    return (hidden_grad, (gain_grad, shift_grad, weight_grad), bias_sum)


def per_device(
    features,
    lengths,
    dw_weight,
    block_gains,
    block_biases,
    up_weight,
    up_bias,
    down_weight,
    head_gain,
    head_shift,
    head_weight,
    head_bias,
    audio_grad,
):
    micro_count = features.shape[0]
    rows_here = features.shape[2]
    seq_rows = rows_here * lax.axis_size("seq")
    row_ids = lax.axis_index("seq") * rows_here + jnp.arange(rows_here, dtype=jnp.int32)
    tables = dft_tables()
    window = hann_window()
    envelope = envelope_rows(row_ids, seq_rows, window)
    block_pack = (dw_weight, block_gains, block_biases, up_weight, up_bias, down_weight)
    head_pack = (head_gain, head_shift, head_weight)
    totals = None
    bias_total = jnp.zeros((2 * BINS,), jnp.float32)
    audio_list = []
    input_list = []
    for micro in range(micro_count):
        convnext_block_list = (
            lax.all_gather(block_pack[0], "dp", axis=2, tiled=True),
            lax.all_gather(block_pack[1], "dp", axis=2, tiled=True),
            lax.all_gather(block_pack[2], "dp", axis=2, tiled=True),
            lax.all_gather(block_pack[3], "dp", axis=1, tiled=True),
            lax.all_gather(block_pack[4], "dp", axis=1, tiled=True),
            lax.all_gather(block_pack[5], "dp", axis=1, tiled=True),
        )
        head = (
            lax.all_gather(head_pack[0], "dp", axis=0, tiled=True),
            lax.all_gather(head_pack[1], "dp", axis=0, tiled=True),
            lax.all_gather(head_pack[2], "dp", axis=0, tiled=True),
        )
        frame_mask = (row_ids < lengths[micro, 0]).astype(jnp.float32)[:, None]
        hidden = features[micro, 0].astype(jnp.float32) * frame_mask
        saved_residual_list = []
        for convnext_block in range(BLOCKS):
            hidden, saved_residuals = block_forward(hidden, convnext_block_list, convnext_block)
            saved_residual_list.append(saved_residuals)
        audio, head_stash = head_forward(
            hidden, head, head_bias, tables, window, envelope, frame_mask
        )
        audio_list.append(audio)
        incoming_gradient, head_grads, bias_sum = head_backward(
            audio_grad[micro, 0], head, head_stash, tables, window, envelope, frame_mask
        )
        convnext_block_gradients = [None] * BLOCKS
        for convnext_block in reversed(range(BLOCKS)):
            incoming_gradient, convnext_block_gradients[convnext_block] = convnext_block_reverse(
                incoming_gradient,
                convnext_block_list,
                convnext_block,
                saved_residual_list[convnext_block],
            )
        input_list.append(incoming_gradient * frame_mask)
        stacked = tuple(
            (jnp.stack([convnext_block_gradients[b][i] for b in range(BLOCKS)]) for i in range(6))
        )
        micro_grads = stacked + head_grads
        totals = micro_grads if totals is None else jax.tree.map(jnp.add, totals, micro_grads)
        bias_total = bias_total + bias_sum
    shards = (
        lax.psum_scatter(
            totals[0].astype(jnp.bfloat16), "dp", scatter_dimension=2, tiled=True
        ).astype(jnp.float32),
        lax.psum_scatter(
            totals[1].astype(jnp.bfloat16), "dp", scatter_dimension=2, tiled=True
        ).astype(jnp.float32),
        lax.psum_scatter(
            totals[2].astype(jnp.bfloat16), "dp", scatter_dimension=2, tiled=True
        ).astype(jnp.float32),
        lax.psum_scatter(
            totals[3].astype(jnp.bfloat16), "dp", scatter_dimension=1, tiled=True
        ).astype(jnp.float32),
        lax.psum_scatter(
            totals[4].astype(jnp.bfloat16), "dp", scatter_dimension=1, tiled=True
        ).astype(jnp.float32),
        lax.psum_scatter(
            totals[5].astype(jnp.bfloat16), "dp", scatter_dimension=1, tiled=True
        ).astype(jnp.float32),
        lax.psum_scatter(
            totals[6].astype(jnp.bfloat16), "dp", scatter_dimension=0, tiled=True
        ).astype(jnp.float32),
        lax.psum_scatter(
            totals[7].astype(jnp.bfloat16), "dp", scatter_dimension=0, tiled=True
        ).astype(jnp.float32),
        lax.psum_scatter(
            totals[8].astype(jnp.bfloat16), "dp", scatter_dimension=0, tiled=True
        ).astype(jnp.float32),
    )
    shards = jax.tree.map(
        lambda part: part.astype(jnp.float32), lax.psum(for_sending(shards), "seq")
    )
    bias_grad = lax.psum(bias_total, ("dp", "seq"))
    audio_out = jnp.stack(audio_list)[:, None]
    input_out = jnp.stack(input_list)[:, None]
    return (
        audio_out,
        input_out,
        shards[0],
        shards[1],
        shards[2],
        shards[3],
        shards[4],
        shards[5],
        shards[6],
        shards[7],
        shards[8],
        bias_grad,
    )


def solution(mesh):
    return jax.shard_map(
        per_device,
        mesh=mesh,
        in_specs=(
            P(None, "dp", "seq", None),
            P(None, "dp"),
            P(None, None, "dp"),
            P(None, None, "dp"),
            P(None, None, "dp"),
            P(None, "dp", None),
            P(None, "dp"),
            P(None, "dp", None),
            P("dp"),
            P("dp"),
            P("dp", None),
            P(),
            P(None, "dp", "seq", None),
        ),
        out_specs=(
            P(None, "dp", "seq", None),
            P(None, "dp", "seq", None),
            P(None, None, "dp"),
            P(None, None, "dp"),
            P(None, None, "dp"),
            P(None, "dp", None),
            P(None, "dp"),
            P(None, "dp", None),
            P("dp"),
            P("dp"),
            P("dp", None),
            P(),
        ),
        check_vma=False,
    )
```

profile of v0, /device:TPU:0, one launch (start us, length us, event | category | flops | bytes accessed | tf_op | source)
XLA Modules:
  0.0 1161.9 jit_solution(13383971009714512672)
XLA Ops:
  15.1 4.9 collective-permute-start.36
  21.4 4.5 collective-permute-start.42
  27.2 4.5 collective-permute-start.30
  33.2 10.3 all_gather.20
  43.5 24.3 %fusion.312 = (f32[512]{0:T(512)S(1)}, f32[512]{0:T(512)S(1)}, f32[512]{0:T(512)S(1)}, f32[512]{0:T(512)S(1)}, f32[512]{0:T(512)S(1)}, /*index=5*/f32[512]{0:T(5...) fusion(bf16[2,7,512]{1,0,2:T(2,128)(2,1)S(1)} %all_gather.20), kind=kLoop, calls=%fused_computation.743 | loop fusion | flops 7168 | bytes 43008 | tf_op jit(solution)/shard_map/convert_element_type | solution.py:100
  68.2 8.9 all-gather
  77.5 8.3 all_gather.19
  85.9 10.1 all_gather.18
  102.1 5.4 slice_reduce_fusion.14
  107.5 5.0 slice_reduce_fusion.19
  112.6 14.7 %slice_reduce_fusion.6 = (f32[512]{0:T(512)}, f32[512]{0:T(512)}, f32[512]{0:T(512)}, f32[512]{0:T(512)}, f32[512]{0:T(512)}, /*index=5*/f32[512]{0:T(512)}, f32[512]{0:T(512)}) fusion(f32[1,7,512]{1,0,2:T(1,128)S(1)} %get-tuple-element.379), kind=kLoop, calls=%fused_computation.717 | loop fusion | bytes 28672 | tf_op jit(solution)/shard_map/slice | solution.py:154
  127.3 15.1 %slice_reduce_fusion.13 = (f32[512]{0:T(512)}, f32[512]{0:T(512)}, f32[512]{0:T(512)}, f32[512]{0:T(512)}, f32[512]{0:T(512)}, /*index=5*/f32[512]{0:T(512)}, f32[512]{0:T(512)}) fusion(f32[1,7,512]{1,0,2:T(1,128)S(1)} %get-tuple-element.380), kind=kLoop, calls=%fused_computation.725 | loop fusion | bytes 28672 | tf_op jit(solution)/shard_map/slice | solution.py:154
  146.1 13.2 %all-reduce.24 = (f32[512]{0:T(512)S(1)}, f32[512]{0:T(512)S(1)}) all-reduce(f32[512]{0:T(512)S(1)} %dynamic-update-slice.1, f32[512]{0:T(512)S(1)} %dynamic-update-slice), channel_id=1, replica_groups=mesh['dp'=8,'seq'=4] {'dp'}, use_global_device_ids=true, to_apply=%add.21 | all-reduce | flops 1024 | bytes 8192
  160.7 4.7 collective-permute-start.24
  165.4 13.6 %fusion.88 = f32[512,513]{0,1:T(8,128)} fusion(f32[2,256]{1,0:T(2,128)S(1)} %collective-permute-done.37, f32[512,256]{1,0:T(8,128)S(1)} %get-tuple-element.300, f32[2,256]{1,0:T(2,128)S(1)} %collective-permute-done.36, f32[512,256]{1,0:T(8,128)S(1)} %fusion.239, f32[513]{0:T(1024)} %select_multiply_fusion, f32[1024]{0:T(1024)} %multiply_subtract_fusion.4), kind=kOutput, calls=%fused_computation.255 | convolution fusion | flops 3238542336 | bytes 2109444 | tf_op jit(solution)/shard_map/dot_general | solution.py:202
  180.4 4.7 collective-permute-start.12
  185.1 13.4 %fusion.92 = f32[512,513]{0,1:T(8,128)} fusion(f32[2,256]{1,0:T(2,128)S(1)} %collective-permute-done.43, f32[512,256]{1,0:T(8,128)S(1)} %get-tuple-element.299, f32[2,256]{1,0:T(2,128)S(1)} %collective-permute-done.42, f32[512,256]{1,0:T(8,128)S(1)} %fusion.238, f32[513]{0:T(1024)} %select_multiply_fusion, f32[1024]{0:T(1024)} %multiply_subtract_fusion.4), kind=kOutput, calls=%fused_computation.257 | convolution fusion | flops 3238542336 | bytes 2109444 | tf_op jit(solution)/shard_map/dot_general | solution.py:202
  199.9 4.7 collective-permute-start.18
  204.6 13.6 %fusion.84 = f32[512,513]{0,1:T(8,128)} fusion(f32[2,256]{1,0:T(2,128)S(1)} %collective-permute-done.31, f32[512,256]{1,0:T(8,128)S(1)} %copy-done.118, f32[2,256]{1,0:T(2,128)S(1)} %collective-permute-done.30, f32[512,256]{1,0:T(8,128)S(1)} %fusion.240, f32[513]{0:T(1024)} %select_multiply_fusion, f32[1024]{0:T(1024)} %multiply_subtract_fusion.4), kind=kOutput, calls=%fused_computation.253 | convolution fusion | flops 3238542336 | bytes 2109444 | tf_op jit(solution)/shard_map/dot_general | solution.py:202
  219.5 4.5 collective-permute-start.6
  224.1 13.3 %fusion.80 = f32[512,513]{0,1:T(8,128)} fusion(f32[2,256]{1,0:T(2,128)S(1)} %collective-permute-done.25, f32[512,256]{1,0:T(8,128)S(1)} %copy-done.121, f32[2,256]{1,0:T(2,128)S(1)} %collective-permute-done.24, f32[512,256]{1,0:T(8,128)S(1)} %fusion.241, f32[513]{0:T(1024)} %select_multiply_fusion, f32[1024]{0:T(1024)} %multiply_subtract_fusion.4), kind=kOutput, calls=%fused_computation.251 | convolution fusion | flops 3238542336 | bytes 2109444 | tf_op jit(solution)/shard_map/dot_general | solution.py:202
  238.7 4.5 collective-permute-start
  252.8 5.2 multiply_convert_fusion.7
  281.3 4.5 collective-permute-start.14
  287.1 4.8 collective-permute-start.8
  293.2 4.5 collective-permute-start.2
  328.8 6.4 convolution_add_fusion.3
  335.2 17.3 %fusion.97 = f32[512,1024]{1,0:T(8,128)S(1)} fusion(f32[513]{0:T(1024)} %select_multiply_fusion, f32[512,1026]{0,1:T(8,128)S(1)} %convolution_add_fusion.3), kind=kOutput, calls=%fused_computation.280 | convolution fusion | flops 3235659264 | bytes 4229124 | tf_op jit(solution)/shard_map/dot_general | solution.py:178
  352.5 16.9 %multiply_add_fusion.3 = (f32[512,513]{0,1:T(8,128)S(1)}, f32[512,513]{0,1:T(8,128)S(1)}) fusion(f32[512,513]{0,1:T(8,128)S(1)} %copy-done.305, f32[512,1026]{0,1:T(8,128)S(1)} %convolution_add_fusion.3, f32[513]{0:T(1024)} %select_multiply_fusion, f32[2,256]{1,0:T(2,128)S(1)} %collective-permute-done.25, f32[512,256]{1,0:T(8,128)S(1)} %copy-done.122, ...), kind=kOutput, calls=%fused_computation.269 | convolution fusion | flops 3241168896 | bytes 6311940 | tf_op jit(solution)/shard_map/dot_general | solution.py:209
  370.6 8.5 fusion.76
  380.1 17.7 %add_multiply_fusion.11 = f32[512,1024]{1,0:T(8,128)S(1)} fusion(f32[512,1024]{1,0:T(8,128)S(1)} %fusion.97, f32[513]{0:T(1024)} %select_multiply_fusion, f32[1024]{0:T(1024)} %multiply_subtract_fusion.4, f32[512,1026]{0,1:T(8,128)S(1)} %convolution_add_fusion.3), kind=kOutput, calls=%fused_computation.228 | convolution fusion | flops 3237233152 | bytes 6330372 | tf_op jit(solution)/shard_map/dot_general | solution.py:181
  409.3 17.3 %fusion.96 = f32[512,1024]{1,0:T(8,128)S(1)} fusion(f32[513]{0:T(1024)} %select_multiply_fusion, f32[512,1026]{0,1:T(8,128)S(1)} %convolution_add_fusion.2), kind=kOutput, calls=%fused_computation.279 | convolution fusion | flops 3235659264 | bytes 4229124 | tf_op jit(solution)/shard_map/dot_general | solution.py:178
  426.6 16.9 %multiply_add_fusion.2 = (f32[512,513]{0,1:T(8,128)S(1)}, f32[512,513]{0,1:T(8,128)S(1)}) fusion(f32[512,513]{0,1:T(8,128)S(1)} %copy-done.304, f32[512,1026]{0,1:T(8,128)S(1)} %convolution_add_fusion.2, f32[513]{0:T(1024)} %select_multiply_fusion, f32[2,256]{1,0:T(2,128)S(1)} %collective-permute-done.31, f32[512,256]{1,0:T(8,128)S(1)} %copy-done.119, ...), kind=kOutput, calls=%fused_computation.267 | convolution fusion | flops 3241168896 | bytes 6311940 | tf_op jit(solution)/shard_map/dot_general | solution.py:209
  443.8 7.6 fusion.74
  451.4 9.9 multiply_reduce_fusion.3
  461.3 8.9 convolution_add_fusion.6
  470.1 17.8 %add_multiply_fusion.10 = f32[512,1024]{1,0:T(8,128)S(1)} fusion(f32[512,1024]{1,0:T(8,128)S(1)} %fusion.96, f32[513]{0:T(1024)} %select_multiply_fusion, f32[1024]{0:T(1024)} %multiply_subtract_fusion.4, f32[512,1026]{0,1:T(8,128)S(1)} %convolution_add_fusion.2), kind=kOutput, calls=%fused_computation.227 | convolution fusion | flops 3237233152 | bytes 6330372 | tf_op jit(solution)/shard_map/dot_general | solution.py:181
  488.9 5.1 collective-permute-start.10
  499.8 17.5 %fusion.95 = f32[512,1024]{1,0:T(8,128)S(1)} fusion(f32[513]{0:T(1024)} %select_multiply_fusion, f32[512,1026]{0,1:T(8,128)S(1)} %convolution_add_fusion.1), kind=kOutput, calls=%fused_computation.278 | convolution fusion | flops 3235659264 | bytes 4229124 | tf_op jit(solution)/shard_map/dot_general | solution.py:178
  517.4 16.6 %multiply_add_fusion.1 = (f32[512,513]{0,1:T(8,128)S(1)}, f32[512,513]{0,1:T(8,128)S(1)}) fusion(f32[512,513]{0,1:T(8,128)S(1)} %copy-done.303, f32[512,1026]{0,1:T(8,128)S(1)} %convolution_add_fusion.1, f32[513]{0:T(1024)} %select_multiply_fusion, f32[2,256]{1,0:T(2,128)S(1)} %copy-done.271, f32[512,256]{1,0:T(8,128)S(1)} %copy-done.116, ...), kind=kOutput, calls=%fused_computation.265 | convolution fusion | flops 3241168896 | bytes 6311940 | tf_op jit(solution)/shard_map/dot_general | solution.py:209
  534.3 8.6 convolution_add_fusion.5
  542.9 17.9 %add_multiply_fusion.9 = f32[512,1024]{1,0:T(8,128)S(1)} fusion(f32[512,1024]{1,0:T(8,128)S(1)} %fusion.95, f32[513]{0:T(1024)} %select_multiply_fusion, f32[1024]{0:T(1024)} %multiply_subtract_fusion.4, f32[512,1026]{0,1:T(8,128)S(1)} %convolution_add_fusion.1), kind=kOutput, calls=%fused_computation.226 | convolution fusion | flops 3237233152 | bytes 6330372 | tf_op jit(solution)/shard_map/dot_general | solution.py:181
  562.5 5.1 collective-permute-start.16
  572.1 18.9 %fusion.94 = f32[512,1024]{1,0:T(8,128)} fusion(f32[513]{0:T(1024)} %select_multiply_fusion, f32[512,1026]{0,1:T(8,128)S(1)} %convolution_add_fusion), kind=kOutput, calls=%fused_computation.277 | convolution fusion | flops 3235659264 | bytes 4229124 | tf_op jit(solution)/shard_map/dot_general | solution.py:178
  591.1 16.6 %multiply_add_fusion = (f32[512,513]{0,1:T(8,128)S(1)}, f32[512,513]{0,1:T(8,128)S(1)}) fusion(f32[512,513]{0,1:T(8,128)S(1)} %copy-done.302, f32[512,1026]{0,1:T(8,128)S(1)} %convolution_add_fusion, f32[513]{0:T(1024)} %select_multiply_fusion, f32[2,256]{1,0:T(2,128)S(1)} %copy-done.269, f32[512,256]{1,0:T(8,128)S(1)} %copy-done.114, ...), kind=kOutput, calls=%fused_computation.263 | convolution fusion | flops 3241168896 | bytes 6311940 | tf_op jit(solution)/shard_map/dot_general | solution.py:209
  609.0 9.6 fusion.46
  618.6 9.7 fusion.72
  628.5 11.4 multiply_reduce_fusion.16
  639.9 11.8 %all-reduce.25 = (bf16[512]{0:T(512)(128)(2,1)S(1)}, bf16[512]{0:T(512)(128)(2,1)S(1)}) all-reduce(bf16[512]{0:T(512)(128)(2,1)S(1)} %add_convert_fusion.13, bf16[512]{0:T(512)(128)(2,1)S(1)} %add_convert_fusion.12), channel_id=8, replica_groups=mesh['dp'=8,'seq'=4] {'dp'}, use_global_device_ids=true, to_apply=%region_168.169.clone | all-reduce | flops 1024 | bytes 4096
  653.2 19.2 %add_multiply_fusion.8 = f32[512,1024]{1,0:T(8,128)S(1)} fusion(f32[512,1024]{1,0:T(8,128)} %fusion.94, f32[513]{0:T(1024)} %select_multiply_fusion, f32[1024]{0:T(1024)} %multiply_subtract_fusion.4, f32[512,1026]{0,1:T(8,128)} %copy-done.123), kind=kOutput, calls=%fused_computation.225 | convolution fusion | flops 3237233152 | bytes 6332416 | tf_op jit(solution)/shard_map/dot_general | solution.py:181
  733.5 39.0 %psum.79 = f32[1026]{0:T(1024)} all-reduce(f32[1026]{0:T(1024)S(1)} %add_add_fusion), channel_id=1, replica_groups=mesh['dp'=8,'seq'=4] {'dp','seq'}, use_global_device_ids=true, to_apply=%region_182.183 | all-reduce | flops 1026 | bytes 8208 | tf_op jit(solution)/shard_map/psum | solution.py:332
  773.9 5.1 collective-permute-start.22
  783.4 4.5 collective-permute-start.26
  804.2 4.7 collective-permute-start.44
  848.2 4.9 fusion.2
  877.4 5.2 fusion.5
  883.9 6.8 fusion.104
  931.8 18.8 %reduce-scatter.18.cloned.1.call-done = bf16[2,192,512]{2,1,0:T(8,128)(2,1)} async-done(((bf16[2,1536,512]{2,1,0:T(8,128)(2,1)}), bf16[2,192,512]{2,1,0:T(8,128)(2,1)}) %reduce-scatter.18.cloned.1.call-update) | async-done | bytes 393232 | tf_op jit(solution)/shard_map/reduce_scatter | solution.py:316
  956.5 30.7 %reduce-scatter.24.cloned.1.call-done = bf16[64,4]{1,0:T(8,128)(2,1)} async-done(((bf16[512,4]{1,0:T(8,128)(2,1)}), bf16[64,4]{1,0:T(8,128)(2,1)}) %reduce-scatter.24.cloned.1.call-update) | async-done | bytes 528
  988.1 36.0 %reduce-scatter.28.cloned.1.call-done = bf16[192,2]{1,0:T(8,128)(2,1)} async-done(((bf16[1536,2]{1,0:T(8,128)(2,1)}), bf16[192,2]{1,0:T(8,128)(2,1)}) %reduce-scatter.28.cloned.1.call-update) | async-done | bytes 784
  1025.0 35.5 %reduce-scatter.26.cloned.1.call-done = bf16[64,6]{1,0:T(8,128)(2,1)} async-done(((bf16[512,6]{1,0:T(8,128)(2,1)}), bf16[64,6]{1,0:T(8,128)(2,1)}) %reduce-scatter.26.cloned.1.call-update) | async-done | bytes 784
  1061.4 36.2 %reduce-scatter.22.cloned.1.call-done = bf16[64,14]{1,0:T(8,128)(2,1)} async-done(((bf16[512,14]{1,0:T(8,128)(2,1)}), bf16[64,14]{1,0:T(8,128)(2,1)}) %reduce-scatter.22.cloned.1.call-update) | async-done | bytes 1808
  1098.5 12.1 %all-reduce.26 = (bf16[2,7,64]{2,1,0:T(8,128)(2,1)S(1)}, bf16[2,3,64]{2,1,0:T(4,128)(2,1)S(1)}, bf16[2,2,64]{2,1,0:T(2,128)(2,1)S(1)}, bf16[2,192]{1,0:T(2,128)(...) all-reduce(bf16[2,7,64]{2,1,0:T(8,128)(2,1)S(1)} %copy.49, ...), channel_id=1, replica_groups=mesh['dp'=8,'seq'=4] {'seq'}, use_global_device_ids=true, to_apply=%region_105.106 | all-reduce | flops 2048 | bytes 8192 | tf_op jit(solution)/shard_map/psum | solution.py:330
  1114.0 35.5 %all-reduce.30.cloned.1.call-done = (bf16[2,64,1536]{2,1,0:T(8,128)(2,1)}, bf16[2,192,512]{2,1,0:T(8,128)(2,1)}, bf16[64,1026]{1,0:T(8,128)(2,1)}) async-done(((bf16[2,64,1536]{2,1,0:T(8,128)(2,1)}, bf16[2,192,512]{2,1,0:T(8,128)(2,1)}, bf16[64,1026]{1,0:T(8,128)(2,1)}), (bf16[2,64,1536]{2,1,0:T(8,128)(2,1)}, bf16[2,192,512]{2,1,0:T(8,128)(2,1)}, bf16[64,1026]{1,0:T(8,128)(2,1)})) %all-reduce.30.cloned.1.call-update) | async-done | bytes 917776 | tf_op jit(solution)/shard_map/psum | solution.py:330
  (1013 shorter events, 327.8 us)
Async XLA Ops:
  7.2 245.6 %all-gather.5.cloned.1.call-start = ((), (), s32[]{:S(2)}) async-start(), calls=%async_computation.7 | async-start | bytes 3538944 | tf_op jit(solution)/shard_map/all_gather | solution.py:263
  7.9 256.2 %all-gather.7.cloned.1.call-start = ((), (), s32[]{:S(2)}) async-start(), calls=%async_computation.8 | async-start | bytes 3538944 | tf_op jit(solution)/shard_map/all_gather | solution.py:265
  8.7 320.1 %all-gather.9.cloned.1.call-start = ((), (), s32[]{:S(2)}) async-start(), calls=%async_computation.9 | async-start | bytes 2654208 | tf_op jit(solution)/shard_map/all_gather | solution.py:270
  11.5 313.3 %copy-start.153 = (f32[512]{0:T(512)}, f32[512]{0:T(512)S(1)}, u32[]{:S(2)}) copy-start(f32[512]{0:T(512)S(1)} %get-tuple-element.493) | copy-start | bytes 6148
  11.5 313.3 %copy-start.159 = (f32[512]{0:T(512)}, f32[512]{0:T(512)S(1)}, u32[]{:S(2)}) copy-start(f32[512]{0:T(512)S(1)} %get-tuple-element.494) | copy-start | bytes 6148
  12.9 312.0 %copy-start.155 = (f32[512]{0:T(512)}, f32[512]{0:T(512)S(1)}, u32[]{:S(2)}) copy-start(f32[512]{0:T(512)S(1)} %get-tuple-element.496) | copy-start | bytes 6148
  12.9 312.0 %copy-start.157 = (f32[512]{0:T(512)}, f32[512]{0:T(512)S(1)}, u32[]{:S(2)}) copy-start(f32[512]{0:T(512)S(1)} %get-tuple-element.495) | copy-start | bytes 6148
  15.1 144.3 %collective-permute-start.36 = (f32[2,256]{1,0:T(2,128)S(1)}, f32[2,256]{1,0:T(2,128)S(1)}, u32[]{:S(2)}, u32[]{:S(2)}) collective-permute-start(f32[2,256]{1,0:T(2,128)S(1)} %get-tuple-element.347), channel_id=1, source_target_pairs={{0,1},{1,2},{2,3},{4,5},{5,6},{6,7},{8,9},{9,10},{10,11},{12,13},{... | collective-permute-start | bytes 6152 | tf_op jit(solution)/shard_map/ppermute | solution.py:29
  20.0 140.7 %collective-permute-start.37 = (f32[2,256]{1,0:T(2,128)S(1)}, f32[2,256]{1,0:T(2,128)S(1)}, u32[]{:S(2)}, u32[]{:S(2)}) collective-permute-start(f32[2,256]{1,0:T(2,128)S(1)} %get-tuple-element.348), channel_id=1, source_target_pairs={{1,0},{2,1},{3,2},{5,4},{6,5},{7,6},{9,8},{10,9},{11,10},{13,12},{... | collective-permute-start | bytes 6152 | tf_op jit(solution)/shard_map/ppermute | solution.py:31
  21.4 157.7 %collective-permute-start.42 = (f32[2,256]{1,0:T(2,128)S(1)}, f32[2,256]{1,0:T(2,128)S(1)}, u32[]{:S(2)}, u32[]{:S(2)}) collective-permute-start(f32[2,256]{1,0:T(2,128)S(1)} %get-tuple-element.353), channel_id=1, source_target_pairs={{0,1},{1,2},{2,3},{4,5},{5,6},{6,7},{8,9},{9,10},{10,11},{12,13},{... | collective-permute-start | bytes 6152 | tf_op jit(solution)/shard_map/ppermute | solution.py:29
  25.9 154.5 %collective-permute-start.43 = (f32[2,256]{1,0:T(2,128)S(1)}, f32[2,256]{1,0:T(2,128)S(1)}, u32[]{:S(2)}, u32[]{:S(2)}) collective-permute-start(f32[2,256]{1,0:T(2,128)S(1)} %get-tuple-element.354), channel_id=1, source_target_pairs={{1,0},{2,1},{3,2},{5,4},{6,5},{7,6},{9,8},{10,9},{11,10},{13,12},{... | collective-permute-start | bytes 6152 | tf_op jit(solution)/shard_map/ppermute | solution.py:31
  27.2 171.3 %collective-permute-start.30 = (f32[2,256]{1,0:T(2,128)S(1)}, f32[2,256]{1,0:T(2,128)S(1)}, u32[]{:S(2)}, u32[]{:S(2)}) collective-permute-start(f32[2,256]{1,0:T(2,128)S(1)} %get-tuple-element.341), channel_id=1, source_target_pairs={{0,1},{1,2},{2,3},{4,5},{5,6},{6,7},{8,9},{9,10},{10,11},{12,13},{... | collective-permute-start | bytes 6152 | tf_op jit(solution)/shard_map/ppermute | solution.py:29
  31.8 900.0 %reduce-scatter.20.cloned.1.call-start = ((), (), s32[]{:S(2)}) async-start(), calls=%async_computation.12 | async-start | bytes 1327104 | tf_op jit(solution)/shard_map/reduce_scatter | solution.py:325
  101.8 223.1 %copy-start.190 = (f32[512]{0:T(512)}, f32[512]{0:T(512)S(1)}, u32[]{:S(2)}) copy-start(f32[512]{0:T(512)S(1)} %get-tuple-element.205) | copy-start | bytes 6148
  159.3 40.5 %collective-permute-start.31 = (f32[2,256]{1,0:T(2,128)S(1)}, f32[2,256]{1,0:T(2,128)S(1)}, u32[]{:S(2)}, u32[]{:S(2)}) collective-permute-start(f32[2,256]{1,0:T(2,128)S(1)} %get-tuple-element.342), channel_id=1, source_target_pairs={{1,0},{2,1},{3,2},{5,4},{6,5},{7,6},{9,8},{10,9},{11,10},{13,12},{... | collective-permute-start | bytes 6152 | tf_op jit(solution)/shard_map/ppermute | solution.py:31
  160.7 57.4 %collective-permute-start.24 = (f32[2,256]{1,0:T(2,128)S(1)}, f32[2,256]{1,0:T(2,128)S(1)}, u32[]{:S(2)}, u32[]{:S(2)}) collective-permute-start(f32[2,256]{1,0:T(2,128)S(1)} %get-tuple-element.335), channel_id=1, source_target_pairs={{0,1},{1,2},{2,3},{4,5},{5,6},{6,7},{8,9},{9,10},{10,11},{12,13},{... | collective-permute-start | bytes 6152 | tf_op jit(solution)/shard_map/ppermute | solution.py:29
  179.0 40.5 %collective-permute-start.25 = (f32[2,256]{1,0:T(2,128)S(1)}, f32[2,256]{1,0:T(2,128)S(1)}, u32[]{:S(2)}, u32[]{:S(2)}) collective-permute-start(f32[2,256]{1,0:T(2,128)S(1)} %get-tuple-element.336), channel_id=1, source_target_pairs={{1,0},{2,1},{3,2},{5,4},{6,5},{7,6},{9,8},{10,9},{11,10},{13,12},{... | collective-permute-start | bytes 6152 | tf_op jit(solution)/shard_map/ppermute | solution.py:31
  180.4 57.0 %collective-permute-start.12 = (bf16[3,512]{1,0:T(4,128)(2,1)S(1)}, bf16[3,512]{1,0:T(4,128)(2,1)S(1)}, u32[]{:S(2)}, u32[]{:S(2)}) collective-permute-start(bf16[3,512]{1,0:T(4,128)(2,1)S(1)} %get-tuple-element.365), channel_id=1, source_target_pairs={{0,1},{1,2},{2,3},{4,5},{5,6},{6,7},{8,9},{9,10},{10,11},{12,13},{... | collective-permute-start | bytes 9224 | tf_op jit(solution)/shard_map/ppermute | solution.py:29
  198.5 40.2 %collective-permute-start.13 = (bf16[3,512]{1,0:T(4,128)(2,1)S(1)}, bf16[3,512]{1,0:T(4,128)(2,1)S(1)}, u32[]{:S(2)}, u32[]{:S(2)}) collective-permute-start(bf16[3,512]{1,0:T(4,128)(2,1)S(1)} %get-tuple-element.366), channel_id=1, source_target_pairs={{1,0},{2,1},{3,2},{5,4},{6,5},{7,6},{9,8},{10,9},{11,10},{13,12},{... | collective-permute-start | bytes 9224 | tf_op jit(solution)/shard_map/ppermute | solution.py:31
  199.9 44.9 %collective-permute-start.18 = (bf16[3,512]{1,0:T(4,128)(2,1)S(1)}, bf16[3,512]{1,0:T(4,128)(2,1)S(1)}, u32[]{:S(2)}, u32[]{:S(2)}) collective-permute-start(bf16[3,512]{1,0:T(4,128)(2,1)S(1)} %get-tuple-element.369), channel_id=1, source_target_pairs={{0,1},{1,2},{2,3},{4,5},{5,6},{6,7},{8,9},{9,10},{10,11},{12,13},{... | collective-permute-start | bytes 9224 | tf_op jit(solution)/shard_map/ppermute | solution.py:29
  218.1 28.0 %collective-permute-start.19 = (bf16[3,512]{1,0:T(4,128)(2,1)S(1)}, bf16[3,512]{1,0:T(4,128)(2,1)S(1)}, u32[]{:S(2)}, u32[]{:S(2)}) collective-permute-start(bf16[3,512]{1,0:T(4,128)(2,1)S(1)} %get-tuple-element.370), channel_id=1, source_target_pairs={{1,0},{2,1},{3,2},{5,4},{6,5},{7,6},{9,8},{10,9},{11,10},{13,12},{... | collective-permute-start | bytes 9224 | tf_op jit(solution)/shard_map/ppermute | solution.py:31
  219.5 28.1 %collective-permute-start.6 = (bf16[3,512]{1,0:T(4,128)(2,1)S(1)}, bf16[3,512]{1,0:T(4,128)(2,1)S(1)}, u32[]{:S(2)}, u32[]{:S(2)}) collective-permute-start(bf16[3,512]{1,0:T(4,128)(2,1)S(1)} %get-tuple-element.361), channel_id=1, source_target_pairs={{0,1},{1,2},{2,3},{4,5},{5,6},{6,7},{8,9},{9,10},{10,11},{12,13},{... | collective-permute-start | bytes 9224 | tf_op jit(solution)/shard_map/ppermute | solution.py:29
  237.4 10.2 collective-permute-start.7
  238.7 10.5 collective-permute-start
  244.8 5.5 collective-permute-start.1
  276.4 15.5 %collective-permute-start.20 = (bf16[3,512]{1,0:T(4,128)(2,1)S(1)}, bf16[3,512]{1,0:T(4,128)(2,1)S(1)}, u32[]{:S(2)}, u32[]{:S(2)}) collective-permute-start(bf16[3,512]{1,0:T(4,128)(2,1)S(1)} %get-tuple-element.367), channel_id=1, source_target_pairs={{0,1},{1,2},{2,3},{4,5},{5,6},{6,7},{8,9},{9,10},{10,11},{12,13},{... | collective-permute-start | bytes 9224 | tf_op jit(solution)/shard_map/ppermute | solution.py:29
  280.0 13.2 %collective-permute-start.21 = (bf16[3,512]{1,0:T(4,128)(2,1)S(1)}, bf16[3,512]{1,0:T(4,128)(2,1)S(1)}, u32[]{:S(2)}, u32[]{:S(2)}) collective-permute-start(bf16[3,512]{1,0:T(4,128)(2,1)S(1)} %get-tuple-element.368), channel_id=1, source_target_pairs={{1,0},{2,1},{3,2},{5,4},{6,5},{7,6},{9,8},{10,9},{11,10},{13,12},{... | collective-permute-start | bytes 9224 | tf_op jit(solution)/shard_map/ppermute | solution.py:31
  281.3 18.0 %collective-permute-start.14 = (bf16[3,512]{1,0:T(4,128)(2,1)S(1)}, bf16[3,512]{1,0:T(4,128)(2,1)S(1)}, u32[]{:S(2)}, u32[]{:S(2)}) collective-permute-start(bf16[3,512]{1,0:T(4,128)(2,1)S(1)} %get-tuple-element.363), channel_id=1, source_target_pairs={{0,1},{1,2},{2,3},{4,5},{5,6},{6,7},{8,9},{9,10},{10,11},{12,13},{... | collective-permute-start | bytes 9224 | tf_op jit(solution)/shard_map/ppermute | solution.py:29
  285.8 14.8 %collective-permute-start.15 = (bf16[3,512]{1,0:T(4,128)(2,1)S(1)}, bf16[3,512]{1,0:T(4,128)(2,1)S(1)}, u32[]{:S(2)}, u32[]{:S(2)}) collective-permute-start(bf16[3,512]{1,0:T(4,128)(2,1)S(1)} %get-tuple-element.364), channel_id=1, source_target_pairs={{1,0},{2,1},{3,2},{5,4},{6,5},{7,6},{9,8},{10,9},{11,10},{13,12},{... | collective-permute-start | bytes 9224 | tf_op jit(solution)/shard_map/ppermute | solution.py:31
  287.1 15.0 %collective-permute-start.8 = (bf16[3,512]{1,0:T(4,128)(2,1)S(1)}, bf16[3,512]{1,0:T(4,128)(2,1)S(1)}, u32[]{:S(2)}, u32[]{:S(2)}) collective-permute-start(bf16[3,512]{1,0:T(4,128)(2,1)S(1)} %get-tuple-element.359), channel_id=1, source_target_pairs={{0,1},{1,2},{2,3},{4,5},{5,6},{6,7},{8,9},{9,10},{10,11},{12,13},{... | collective-permute-start | bytes 9224 | tf_op jit(solution)/shard_map/ppermute | solution.py:29
  291.9 10.2 collective-permute-start.9
  293.2 10.4 collective-permute-start.2
  299.3 5.5 collective-permute-start.3
  399.4 373.0 %collective-permute-start.4 = (bf16[2,256]{1,0:T(2,128)(2,1)}, bf16[2,256]{1,0:T(2,128)(2,1)}, u32[]{:S(2)}, u32[]{:S(2)}) collective-permute-start(bf16[2,256]{1,0:T(2,128)(2,1)} %get-tuple-element.371), channel_id=1, source_target_pairs={{0,1},{1,2},{2,3},{4,5},{5,6},{6,7},{8,9},{9,10},{10,11},{12,13},{... | collective-permute-start | bytes 3080 | tf_op jit(solution)/shard_map/ppermute | solution.py:29
  403.5 370.4 %collective-permute-start.5 = (bf16[2,256]{1,0:T(2,128)(2,1)}, bf16[2,256]{1,0:T(2,128)(2,1)}, u32[]{:S(2)}, u32[]{:S(2)}) collective-permute-start(bf16[2,256]{1,0:T(2,128)(2,1)} %get-tuple-element.372), channel_id=1, source_target_pairs={{1,0},{2,1},{3,2},{5,4},{6,5},{7,6},{9,8},{10,9},{11,10},{13,12},{... | collective-permute-start | bytes 3080 | tf_op jit(solution)/shard_map/ppermute | solution.py:31
  488.9 293.2 %collective-permute-start.10 = (bf16[2,256]{1,0:T(2,128)(2,1)}, bf16[2,256]{1,0:T(2,128)(2,1)}, u32[]{:S(2)}, u32[]{:S(2)}) collective-permute-start(bf16[2,256]{1,0:T(2,128)(2,1)} %get-tuple-element.373), channel_id=1, source_target_pairs={{0,1},{1,2},{2,3},{4,5},{5,6},{6,7},{8,9},{9,10},{10,11},{12,13},{... | collective-permute-start | bytes 3080 | tf_op jit(solution)/shard_map/ppermute | solution.py:29
  494.1 289.3 %collective-permute-start.11 = (bf16[2,256]{1,0:T(2,128)(2,1)}, bf16[2,256]{1,0:T(2,128)(2,1)}, u32[]{:S(2)}, u32[]{:S(2)}) collective-permute-start(bf16[2,256]{1,0:T(2,128)(2,1)} %get-tuple-element.374), channel_id=1, source_target_pairs={{1,0},{2,1},{3,2},{5,4},{6,5},{7,6},{9,8},{10,9},{11,10},{13,12},{... | collective-permute-start | bytes 3080 | tf_op jit(solution)/shard_map/ppermute | solution.py:31
  562.5 228.2 %collective-permute-start.16 = (bf16[2,256]{1,0:T(2,128)(2,1)}, bf16[2,256]{1,0:T(2,128)(2,1)}, u32[]{:S(2)}, u32[]{:S(2)}) collective-permute-start(bf16[2,256]{1,0:T(2,128)(2,1)} %get-tuple-element.375), channel_id=1, source_target_pairs={{0,1},{1,2},{2,3},{4,5},{5,6},{6,7},{8,9},{9,10},{10,11},{12,13},{... | collective-permute-start | bytes 3080 | tf_op jit(solution)/shard_map/ppermute | solution.py:29
  652.9 278.9 %reduce-scatter.16.cloned.1.call-start = ((), (), s32[]{:S(2)}) async-start(), calls=%async_computation.10 | async-start | bytes 3538944 | tf_op jit(solution)/shard_map/reduce_scatter | solution.py:310
  772.5 20.6 %collective-permute-start.17 = (bf16[2,256]{1,0:T(2,128)(2,1)S(1)}, bf16[2,256]{1,0:T(2,128)(2,1)S(1)}, u32[]{:S(2)}, u32[]{:S(2)}) collective-permute-start(bf16[2,256]{1,0:T(2,128)(2,1)S(1)} %copy-done.261), channel_id=1, source_target_pairs={{1,0},{2,1},{3,2},{5,4},{6,5},{7,6},{9,8},{10,9},{11,10},{13,12},{... | collective-permute-start | bytes 3080 | tf_op jit(solution)/shard_map/ppermute | solution.py:31
  773.9 79.5 %collective-permute-start.22 = (bf16[2,256]{1,0:T(2,128)(2,1)}, bf16[2,256]{1,0:T(2,128)(2,1)}, u32[]{:S(2)}, u32[]{:S(2)}) collective-permute-start(bf16[2,256]{1,0:T(2,128)(2,1)} %get-tuple-element.377), channel_id=1, source_target_pairs={{0,1},{1,2},{2,3},{4,5},{5,6},{6,7},{8,9},{9,10},{10,11},{12,13},{... | collective-permute-start | bytes 3080 | tf_op jit(solution)/shard_map/ppermute | solution.py:29
  782.1 71.3 %collective-permute-start.23 = (bf16[2,256]{1,0:T(2,128)(2,1)}, bf16[2,256]{1,0:T(2,128)(2,1)}, u32[]{:S(2)}, u32[]{:S(2)}) collective-permute-start(bf16[2,256]{1,0:T(2,128)(2,1)} %get-tuple-element.378), channel_id=1, source_target_pairs={{1,0},{2,1},{3,2},{5,4},{6,5},{7,6},{9,8},{10,9},{11,10},{13,12},{... | collective-permute-start | bytes 3080 | tf_op jit(solution)/shard_map/ppermute | solution.py:31
  783.4 32.8 %collective-permute-start.26 = (bf16[3,512]{1,0:T(4,128)(2,1)S(1)}, bf16[3,512]{1,0:T(4,128)(2,1)S(1)}, u32[]{:S(2)}, u32[]{:S(2)}) collective-permute-start(bf16[3,512]{1,0:T(4,128)(2,1)S(1)} %get-tuple-element.333), channel_id=1, source_target_pairs={{0,1},{1,2},{2,3},{4,5},{5,6},{6,7},{8,9},{9,10},{10,11},{12,13},{... | collective-permute-start | bytes 9224 | tf_op jit(solution)/shard_map/ppermute | solution.py:29
  790.7 5.8 collective-permute-start.32
  793.1 8.0 collective-permute-start.33
  796.5 7.7 collective-permute-start.38
  801.1 7.8 collective-permute-start.39
  804.2 7.7 collective-permute-start.44
  808.9 5.5 collective-permute-start.45
  812.0 6.2 collective-permute-start.27
  853.3 97.3 %reduce-scatter.18.cloned.1.call-start = ((), (), s32[]{:S(2)}) async-start(), calls=%async_computation.11 | async-start | bytes 3538944 | tf_op jit(solution)/shard_map/reduce_scatter | solution.py:316
  882.6 104.6 %reduce-scatter.24.cloned.1.call-start = ((), (), s32[]{:S(2)}) async-start(), calls=%async_computation.14 | async-start | bytes 147456
  899.5 124.7 %reduce-scatter.28.cloned.1.call-start = ((), (), s32[]{:S(2)}) async-start(), calls=%async_computation.16 | async-start | bytes 442368
  900.6 51.0 %collective-permute-start.28 = (bf16[3,512]{1,0:T(4,128)(2,1)S(1)}, bf16[3,512]{1,0:T(4,128)(2,1)S(1)}, u32[]{:S(2)}, u32[]{:S(2)}) collective-permute-start(bf16[3,512]{1,0:T(4,128)(2,1)S(1)} %get-tuple-element.331), channel_id=1, source_target_pairs={{0,1},{1,2},{2,3},{4,5},{5,6},{6,7},{8,9},{9,10},{10,11},{12,13},{... | collective-permute-start | bytes 9224 | tf_op jit(solution)/shard_map/ppermute | solution.py:29
  904.6 46.9 %collective-permute-start.29 = (bf16[3,512]{1,0:T(4,128)(2,1)S(1)}, bf16[3,512]{1,0:T(4,128)(2,1)S(1)}, u32[]{:S(2)}, u32[]{:S(2)}) collective-permute-start(bf16[3,512]{1,0:T(4,128)(2,1)S(1)} %get-tuple-element.332), channel_id=1, source_target_pairs={{1,0},{2,1},{3,2},{5,4},{6,5},{7,6},{9,8},{10,9},{11,10},{13,12},{... | collective-permute-start | bytes 9224 | tf_op jit(solution)/shard_map/ppermute | solution.py:31
  905.9 24.5 %collective-permute-start.46 = (bf16[3,512]{1,0:T(4,128)(2,1)S(1)}, bf16[3,512]{1,0:T(4,128)(2,1)S(1)}, u32[]{:S(2)}, u32[]{:S(2)}) collective-permute-start(bf16[3,512]{1,0:T(4,128)(2,1)S(1)} %get-tuple-element.349), channel_id=1, source_target_pairs={{0,1},{1,2},{2,3},{4,5},{5,6},{6,7},{8,9},{9,10},{10,11},{12,13},{... | collective-permute-start | bytes 9224 | tf_op jit(solution)/shard_map/ppermute | solution.py:29
  910.5 7.7 collective-permute-start.34
  914.3 8.5 collective-permute-start.35
  915.6 144.9 %reduce-scatter.26.cloned.1.call-start = ((), (), s32[]{:S(2)}) async-start(), calls=%async_computation.15 | async-start | bytes 147456
  916.8 180.8 %reduce-scatter.22.cloned.1.call-start = ((), (), s32[]{:S(2)}) async-start(), calls=%async_computation.13 | async-start | bytes 147456
  918.2 231.4 %all-reduce.30.cloned.1.call-start = ((), (), s32[]{:S(2)}) async-start(), calls=%async_computation.17 | async-start | bytes 1867776 | tf_op jit(solution)/shard_map/psum | solution.py:330
  918.2 7.1 collective-permute-start.40
  922.8 5.5 collective-permute-start.41
  925.3 6.3 collective-permute-start.47
  (301 other events, 3902.7 us)
Sparse Core Ops, SparseCore 0:
  9.9 36.0 all-gather.4
  47.9 32.3 all-gather.6
  82.2 29.1 all-gather.8
  653.1 34.3 reduce-scatter.19
  853.4 47.6 reduce-scatter.15
  904.3 46.2 reduce-scatter.17
  953.9 33.3 reduce-scatter.23
  990.3 33.8 reduce-scatter.27
  1027.2 33.2 reduce-scatter.25
  1064.2 33.3 reduce-scatter.21
  1100.2 49.2 all-reduce.29
where the time goes:
time: 1170 us; the launch traced here: 1160 us
  matrix products  474 us (41%)
  waiting for transfers between devices  203 us (17%)
  starting transfers between devices  139 us (12%)
  blocking collectives  114 us (10%)
  other arithmetic  111 us (9%)
  local copies, waits for them, and re-layouts  102 us (9%)
  between operations  20.5 us (2%)
    unnamed x15, waiting for transfers between devices  140 us
    ppermute x24, starting transfers between devices, padded_2(): lax.ppermute(tail, axis, [(i, (i + 1) % count) for i in range(ends)])  107 us
    dot_general x4, matrix products, head_forward(): jnp.dot(imag_part, sin_table, precision=exact_mode, preferred_element_typ...  72.6 us
    dot_general x4, matrix products, head_forward(): jnp.dot(real_part, cos_table, precision=exact_mode, preferred_element_typ...  71.1 us
    dot_general x4, matrix products, head_backward(): lax.dot_general(framed_grad, sin_table, contract_cols, precision=exact_mo...  67 us
    dot_general x4, matrix products, head_backward(): lax.dot_general(framed_grad, cos_table, contract_cols, precision=exact_mo...  53.8 us
    unnamed x639, local copies, waits for them, and re-layouts  48.2 us
    psum x1, blocking collectives, per_device(): bias_grad = lax.psum(bias_total, ('dp', 'seq'))  39 us
  transfers between devices with their start and end apart: 59, of which 12 were waited for; matrix products, arithmetic and copies ran while one was open for 49% of the time, Pallas kernels for 0%

commit v1 on v0

v1 whole, which is shorter than its diff:
```python
import functools
import math

import jax
import jax.numpy as jnp
import numpy as np
from jax import lax
from jax.experimental import pallas as pl
from jax.experimental.pallas import tpu as pltpu
from jax.sharding import PartitionSpec as P

NFFT = 1024
HOP = 256
BINS = 513
HALF = 512
EXTRA = 128
KERNEL = 7
BLOCKS = 2
HALO = 16
norm_eps = 1e-06
f32 = jnp.float32
low = jnp.bfloat16
rows_dims = (((0,), (0,)), ((), ()))
cols_dims = (((1,), (1,)), ((), ()))
MiB = 2**20
GELU = (0.7978202661111929, 0.03654664812915587, -0.00019444764679970054, -1.3688682486738934e-05)
SIN = (6.283184921107194, -41.34159015596926, 81.59997289449204, -76.61480381354174, 41.34439732745281, -12.473668162531846)
COS = (0.9999992215705861, -19.738982516102407, 64.92872660899411, -85.27239689575316, 58.79403819232432, -21.076781286284348)


def window_values():
    return 0.5 - 0.5 * np.cos(np.arange(NFFT) * (2.0 * math.pi / NFFT))


def head_tables():
    row = np.arange(NFFT)
    frequency = np.where(row < HALF, row, np.where(row == HALF, HALF, row - HALF))
    angles = (frequency[:, None] * np.arange(NFFT)[None, :] % NFFT) * (2.0 * math.pi / NFFT)
    weight = np.where((row == 0) | (row == HALF), 1.0, 2.0)[:, None] / NFFT
    values = np.where((row <= HALF)[:, None], np.cos(angles), -np.sin(angles)) * weight
    return (values * window_values()[None, :]).astype(jnp.bfloat16)


def swap(x, axis, d):
    return lax.ppermute(x, axis, [(i, i ^ d) for i in range(lax.axis_size(axis))])


def by_owner(pieces, axis):
    me = lax.axis_index(axis)
    stacked = jnp.stack(pieces) if isinstance(pieces, list) else pieces
    count = stacked.shape[0]
    bit = 1
    while bit < count:
        split = stacked.reshape((count // (2 * bit), 2, bit) + stacked.shape[1:])
        split = jnp.where((me & bit) != 0, split[:, ::-1], split)
        stacked = split.reshape(stacked.shape)
        bit *= 2
    return stacked


def gathered(x):
    even = jnp.stack([x] + [swap(x, "dp", d) for d in range(2, lax.axis_size("dp"), 2)])
    return even, swap(even, "dp", 1)


def poly(z, coefficients):
    p = coefficients[-1]
    for c in coefficients[-2::-1]:
        p = p * z + c
    return p


def gelu_parts(x):
    u = jnp.clip(x, -5.2, 5.2)
    z = u * u
    p = poly(z, [jnp.asarray(c, x.dtype) for c in GELU])
    half = jnp.asarray(0.5, x.dtype)
    cumulative = half * jnp.tanh(u * p) + half
    density = jnp.exp2(z * jnp.asarray(-0.5 * math.log2(math.e), x.dtype))
    return x * cumulative, cumulative + (x * jnp.asarray(1.0 / math.sqrt(2.0 * math.pi), x.dtype)) * density


def norm_parts(values):
    centred = values - jnp.mean(values, axis=1, keepdims=True)
    inv_std = lax.rsqrt(jnp.mean(centred * centred, axis=1, keepdims=True) + norm_eps)
    return centred * inv_std, inv_std


def norm_back(normed_grad, unit, inv_std, gain):
    unit_grad = normed_grad * gain
    inner = jnp.mean(unit_grad * unit, axis=1, keepdims=True)
    return inv_std * (unit_grad - jnp.mean(unit_grad, axis=1, keepdims=True) - unit * inner)


def frames_of(scal, ext):
    t = lax.broadcasted_iota(jnp.int32, (ext, 1), 0) + scal[0]
    return t, (t >= 0) & (t < scal[1])


def total_rows(x):
    return jnp.sum(x, axis=0, keepdims=True)


def assemble(scal, even_ref, odd_ref, whole_ref, sems):
    size = even_ref.shape[1]
    copies = []
    for h in range(even_ref.shape[0]):
        for c, ref in enumerate((even_ref, odd_ref)):
            at = pl.multiple_of((scal[2] ^ (2 * h + c)) * size, size)
            copies.append(pltpu.make_async_copy(ref.at[h], whole_ref.at[pl.ds(at, size)], sems.at[2 * h + c]))
    for copy in copies:
        copy.start()
    return copies


def split_out(scal, total_ref, keep_ref, send_ref):
    size = keep_ref.shape[1]
    for h in range(keep_ref.shape[0]):
        at = pl.multiple_of((scal[2] ^ (2 * h)) * size, size)
        keep_ref[h] = total_ref[pl.ds(at, size), :]
        at = pl.multiple_of((scal[2] ^ (2 * h + 1)) * size, size)
        send_ref[h] = total_ref[pl.ds(at, size), :].astype(low)


def call(kernel, grid, scal, ins, outs, scratch, flops, name):
    def spec(shape, kind):
        if kind == "any":
            return pl.BlockSpec(memory_space=pl.ANY)
        if kind == "rows":
            return pl.BlockSpec((1,) + tuple(shape[1:]), lambda i, s: (i,) + (0,) * (len(shape) - 1))
        return pl.BlockSpec(tuple(shape), lambda i, s: (0,) * len(shape))

    moved = sum(a.size * a.dtype.itemsize for a, _ in ins)
    moved += sum(math.prod(s) * jnp.dtype(d).itemsize for s, d, _ in outs)
    return pl.pallas_call(
        kernel,
        out_shape=[jax.ShapeDtypeStruct(tuple(s), d) for s, d, _ in outs],
        grid_spec=pltpu.PrefetchScalarGridSpec(
            num_scalar_prefetch=1,
            grid=(grid,),
            in_specs=[spec(a.shape, kind) for a, kind in ins],
            out_specs=[spec(s, kind) for s, _, kind in outs],
            scratch_shapes=scratch,
        ),
        compiler_params=pltpu.CompilerParams(vmem_limit_bytes=56 * MiB, dimension_semantics=("arbitrary",)),
        cost_estimate=pl.CostEstimate(flops=int(flops), bytes_accessed=int(moved), transcendentals=0),
        name=name,
    )(scal, *[a for a, _ in ins])


def dft_kernel(ext, scal, grad_ref, recip_ref, table_ref, out_ref):
    t, inside = frames_of(scal, ext)
    mask = inside & (t < scal[3 + pl.program_id(0)])
    own = jnp.where(mask, grad_ref[0] * recip_ref[...], 0.0)
    parts = [own if q == 2 else pltpu.roll(own, (2 - q) % ext, 0) for q in range(4)]
    framed = jnp.where(inside, jnp.concatenate(parts, axis=1), 0.0).astype(low)
    out_ref[0] = lax.dot_general(framed, table_ref[...], cols_dims, preferred_element_type=f32).astype(low)


def conv_forward(block_in, taps_ref, bias):
    ext = block_in.shape[0]
    conv = bias + taps_ref[3:4] * block_in
    for k in range(KERNEL):
        if k != 3:
            conv = conv + taps_ref[k : k + 1] * pltpu.roll(block_in, (3 - k) % ext, 0)
    return conv


def conv_kernel(ext, scal, features_ref, taps_ref, vec_ref, normed_ref, unit_ref, inv_ref):
    t, inside = frames_of(scal, ext)
    h = jnp.where(inside & (t < scal[3 + pl.program_id(0)]), features_ref[0].astype(f32), 0.0)
    unit, inv_std = norm_parts(conv_forward(h, taps_ref, vec_ref[2:3]))
    unit_ref[0] = unit.astype(low)
    inv_ref[0] = inv_std
    normed_ref[0] = (unit * vec_ref[0:1] + vec_ref[3:4]).astype(low)


def up_kernel(chunk, scal, normed_ref, bias_ref, even_ref, odd_ref, act_ref, slope_ref, weight_ref, sems):
    @pl.when(pl.program_id(0) == 0)
    def _():
        for copy in assemble(scal, even_ref, odd_ref, weight_ref, sems):
            copy.wait()

    normed = normed_ref[0]
    for c in range(0, weight_ref.shape[1], chunk):
        pre = jnp.dot(normed, weight_ref[:, c : c + chunk], preferred_element_type=f32) + bias_ref[:, c : c + chunk]
        act, slope = gelu_parts(pre.astype(low))
        act_ref[0, :, c : c + chunk] = act
        slope_ref[0, :, c : c + chunk] = slope


def down_kernel(ext, first, final, scal, act_ref, h_ref, vec_ref, taps_ref, next_ref, even_ref, odd_ref, *refs):
    if final:
        hidden_ref, branch_ref, weight_ref, sems = refs
    else:
        hidden_ref, branch_ref, normed_ref, unit_ref, inv_ref, weight_ref, sems = refs

    @pl.when(pl.program_id(0) == 0)
    def _():
        for copy in assemble(scal, even_ref, odd_ref, weight_ref, sems):
            copy.wait()

    t, inside = frames_of(scal, ext)
    h = h_ref[0].astype(f32)
    if first:
        h = jnp.where(inside & (t < scal[3 + pl.program_id(0)]), h, 0.0)
    branch = jnp.dot(act_ref[0], weight_ref[...], preferred_element_type=f32) + vec_ref[4:5]
    branch_ref[0] = branch.astype(low)
    hidden = h + vec_ref[1:2] * branch
    hidden_ref[0] = hidden
    if not final:
        block_in = jnp.where(inside, hidden, 0.0).astype(low).astype(f32)
        unit, inv_std = norm_parts(conv_forward(block_in, taps_ref, next_ref[2:3]))
        unit_ref[0] = unit.astype(low)
        inv_ref[0] = inv_std
        normed_ref[0] = (unit * next_ref[0:1] + next_ref[3:4]).astype(low)


def head_kernel(
    ext, rows, scal, h_ref, tgrad_ref, recip_ref, table_ref, vec_ref, bias_ref, even_ref, odd_ref,
    audio_ref, hgrad_ref, keep_ref, send_ref, small_ref, sbias_ref, weight_ref, total_ref, sems,
):
    step = pl.program_id(0)

    @pl.when(step == 0)
    def _():
        copies = assemble(scal, even_ref, odd_ref, weight_ref, sems)
        total_ref[...] = jnp.zeros_like(total_ref)
        small_ref[...] = jnp.zeros_like(small_ref)
        sbias_ref[...] = jnp.zeros_like(sbias_ref)
        for copy in copies:
            copy.wait()

    t, inside = frames_of(scal, ext)
    own = slice(HALO, HALO + rows)
    unit, inv_std = norm_parts(h_ref[0])
    normed = (unit * vec_ref[0:1] + vec_ref[1:2]).astype(low)
    logits = jnp.dot(normed, weight_ref[...], preferred_element_type=f32) + bias_ref[...]

    def turns(x):
        r = x * (1.0 / (2.0 * math.pi))
        r = r - jnp.floor(r + 0.5)
        z = r * r
        return poly(z, COS), r * poly(z, SIN)

    magnitude = jnp.exp(logits[:, :HALF])
    cos, sin = turns(logits[:, HALF : 2 * HALF])
    re = magnitude * cos
    im = magnitude * sin
    last = logits[:, 2 * HALF :]
    lane = lax.broadcasted_iota(jnp.int32, (ext, EXTRA), 1)
    cos, sin = turns(pltpu.roll(last, EXTRA - 1, 1))
    top = jnp.exp(jnp.where(lane == 0, last, 0.0))
    top_re = top * cos
    top_im = top * sin
    im_first = jnp.where(lane == 0, top_re, im[:, :EXTRA])
    spectrum = jnp.concatenate([re, im_first, im[:, EXTRA:]], axis=1).astype(low)
    framed = jnp.dot(spectrum, table_ref[...], preferred_element_type=f32)
    framed = jnp.where(inside, framed, 0.0)
    audio = framed[:, 2 * HOP : 3 * HOP]
    for q in (0, 1, 3):
        audio = audio + pltpu.roll(framed[:, q * HOP : (q + 1) * HOP], (q - 2) % ext, 0)
    audio = jnp.where(t < scal[3 + step], audio * recip_ref[...], 0.0)
    audio_ref[0] = audio[own]

    tgrad = tgrad_ref[0].astype(f32)
    re_grad = tgrad[:, :HALF]
    top_grad = tgrad[:, HALF : HALF + EXTRA]
    im_grad = jnp.concatenate([jnp.where(lane == 0, 0.0, top_grad), tgrad[:, HALF + EXTRA :]], axis=1)
    log_last = jnp.where(lane == 0, top_grad * top_re, 0.0)
    phase_last = jnp.where(lane == 1, pltpu.roll(top_grad * top_im, 1, 1), 0.0)
    logit_grad = jnp.concatenate(
        [re_grad * re + im_grad * im, im_grad * re - re_grad * im, log_last - phase_last], axis=1
    )
    sbias_ref[...] += total_rows(logit_grad[own])
    logit_low = logit_grad.astype(low)
    total_ref[...] += lax.dot_general(normed[own], logit_low[own], rows_dims, preferred_element_type=f32)
    normed_grad = lax.dot_general(logit_low, weight_ref[...], cols_dims, preferred_element_type=f32)
    hgrad_ref[0] = norm_back(normed_grad, unit, inv_std, vec_ref[0:1])
    small_ref[0:1] += total_rows((normed_grad * unit)[own])
    small_ref[1:2] += total_rows(normed_grad[own])

    @pl.when(step == pl.num_programs(0) - 1)
    def _():
        split_out(scal, total_ref, keep_ref, send_ref)


def back_down_kernel(
    rows, chunk, scal, hgrad_ref, branch_ref, act_ref, slope_ref, vec_ref, even_ref, odd_ref,
    pgrad_ref, keep_ref, send_ref, small_ref, sbias_ref, weight_ref, total_ref, sems,
):
    step = pl.program_id(0)

    @pl.when(step == 0)
    def _():
        copies = assemble(scal, even_ref, odd_ref, weight_ref, sems)
        total_ref[...] = jnp.zeros_like(total_ref)
        small_ref[...] = jnp.zeros_like(small_ref)
        sbias_ref[...] = jnp.zeros_like(sbias_ref)
        for copy in copies:
            copy.wait()

    own = slice(HALO, HALO + rows)
    hgrad = hgrad_ref[0]
    small_ref[0:1] += total_rows(hgrad[own] * branch_ref[0, own].astype(f32))
    branch_grad = (vec_ref[1:2] * hgrad).astype(low)
    small_ref[1:2] += total_rows(branch_grad[own].astype(f32))
    for c in range(0, weight_ref.shape[0], chunk):
        part = slice(c, c + chunk)
        total_ref[part] += lax.dot_general(act_ref[0, own, part], branch_grad[own], rows_dims, preferred_element_type=f32)
        act_grad = lax.dot_general(branch_grad, weight_ref[part], cols_dims, preferred_element_type=f32)
        pre_grad = (act_grad * slope_ref[0, :, part].astype(f32)).astype(low)
        pgrad_ref[0, :, part] = pre_grad
        sbias_ref[:, part] += total_rows(pre_grad[own].astype(f32))

    @pl.when(step == pl.num_programs(0) - 1)
    def _():
        split_out(scal, total_ref, keep_ref, send_ref)


def up_grad_kernel(rows, scal, normed_ref, pgrad_ref, keep_ref, send_ref, total_ref):
    step = pl.program_id(0)

    @pl.when(step == 0)
    def _():
        total_ref[...] = jnp.zeros_like(total_ref)

    own = slice(HALO, HALO + rows)
    total_ref[...] += lax.dot_general(normed_ref[0, own], pgrad_ref[0, own], rows_dims, preferred_element_type=f32)

    @pl.when(step == pl.num_programs(0) - 1)
    def _():
        split_out(scal, total_ref, keep_ref, send_ref)


def back_up_kernel(
    ext, rows, first, scal, pgrad_ref, unit_ref, inv_ref, block_in_ref, hgrad_ref, vec_ref, taps_ref, even_ref, odd_ref,
    out_ref, small_ref, weight_ref, sems,
):
    step = pl.program_id(0)

    @pl.when(step == 0)
    def _():
        copies = assemble(scal, even_ref, odd_ref, weight_ref, sems)
        small_ref[...] = jnp.zeros_like(small_ref)
        for copy in copies:
            copy.wait()

    t, inside = frames_of(scal, ext)
    mask = inside & (t < scal[3 + step])
    own = slice(HALO, HALO + rows)
    block_in = block_in_ref[0]
    block_in = jnp.where(mask if first else inside, block_in.astype(f32), 0.0)[own]
    if not first:
        block_in = block_in.astype(low).astype(f32)
    unit = unit_ref[0].astype(f32)
    normed_grad = lax.dot_general(pgrad_ref[0], weight_ref[...], cols_dims, preferred_element_type=f32)
    small_ref[8:9] += total_rows((normed_grad * unit)[own])
    small_ref[9:10] += total_rows(normed_grad[own])
    conv_grad = norm_back(normed_grad, unit, inv_ref[0], vec_ref[0:1])
    conv_grad = jnp.where(inside, conv_grad, 0.0).astype(low).astype(f32)
    small_ref[7:8] += total_rows(conv_grad[own])
    hgrad = hgrad_ref[0]
    for k in range(KERNEL):
        moved = conv_grad if k == 3 else pltpu.roll(conv_grad, (k - 3) % ext, 0)
        hgrad = hgrad + taps_ref[k : k + 1] * moved
        small_ref[k : k + 1] += total_rows(block_in * moved[own])
    if first:
        out_ref[0] = jnp.where(mask, hgrad, 0.0)[own]
    else:
        out_ref[0] = hgrad


def add_pair(keep, received):
    total = keep + received.astype(f32)
    sent = total[1:].astype(low)
    return total[0], [sent[h] for h in range(sent.shape[0])]


def scattered(keep, send):
    own, sent = add_pair(keep, swap(send, "dp", 1))
    for h, piece in enumerate(sent):
        own = own + swap(piece, "dp", 2 * (h + 1)).astype(f32)
    return own


def over_seq(part):
    count = lax.axis_size("seq")
    cut = part.astype(low).reshape((count, part.shape[0] // count) + part.shape[1:])
    cut = by_owner(cut, "seq")
    total = cut[0].astype(f32)
    for d in range(1, count):
        total = total + swap(cut[d], "seq", d).astype(f32)
    total = total.astype(low)
    whole = by_owner([total] + [swap(total, "seq", d) for d in range(1, count)], "seq")
    return whole.reshape(part.shape).astype(f32)


def summed_everywhere(x):
    for axis in ("dp", "seq"):
        bit = 1
        while bit < lax.axis_size(axis):
            x = x + swap(x, axis, bit)
            bit *= 2
    return x


def per_device(
    features,
    lengths,
    dw_weight,
    block_gains,
    block_biases,
    up_weight,
    up_bias,
    down_weight,
    head_gain,
    head_shift,
    head_weight,
    head_bias,
    audio_grad,
):
    count = lax.axis_size("dp")
    pairs = count // 2
    micro = features.shape[0]
    rows = features.shape[2]
    width = features.shape[3]
    units = up_weight.shape[2]
    ext = rows + 2 * HALO
    seq_count = lax.axis_size("seq")
    seq_rows = rows * seq_count
    features = features[:, 0]
    audio_grad = audio_grad[:, 0]
    up_pairs = [(i, i + 1) for i in range(seq_count - 1)]
    down_pairs = [(i + 1, i) for i in range(seq_count - 1)]
    grad_low = audio_grad.astype(low)
    last = jnp.concatenate([features[:, rows - HALO :], grad_low[:, rows - HALO :]], axis=2)
    first = jnp.concatenate([features[:, :HALO], grad_low[:, :HALO]], axis=2)
    before = lax.ppermute(last, "seq", up_pairs)
    after = lax.ppermute(first, "seq", down_pairs)

    own = width // count
    gain_high = head_gain.astype(low)
    shift_high = head_shift.astype(low)
    small = jnp.concatenate(
        [
            dw_weight.reshape(-1, own),
            block_gains.reshape(-1, own),
            block_biases.reshape(-1, own),
            gain_high[None],
            (head_gain - gain_high.astype(f32)).astype(low)[None],
            shift_high[None],
            (head_shift - shift_high.astype(f32)).astype(low)[None],
            up_bias.reshape(-1, own),
        ]
    )
    even, odd = gathered(small)
    small = by_owner(jnp.stack([even, odd], axis=1).reshape((count,) + small.shape), "dp")
    split = small.shape[1] - BLOCKS * (units // width)
    wide = jnp.swapaxes(small[:, :split], 0, 1).reshape(split, width).astype(f32)
    up_bias_all = jnp.swapaxes(small[:, split:].reshape(count, BLOCKS, units // count), 0, 1)
    up_bias_all = up_bias_all.reshape(BLOCKS, 1, units).astype(f32)
    zero_row = jnp.zeros((1, width), f32)
    taps = [jnp.concatenate([wide[KERNEL * b : KERNEL * (b + 1)], zero_row]) for b in range(BLOCKS)]
    vecs = [
        jnp.concatenate([wide[14 + 2 * b : 16 + 2 * b], wide[18 + 3 * b : 21 + 3 * b], zero_row, zero_row, zero_row])
        for b in range(BLOCKS)
    ]
    head_vec = jnp.concatenate([wide[24:25] + wide[25:26], wide[26:27] + wide[27:28]] + [zero_row] * 6)

    def reordered(x, kind):
        return jnp.concatenate(
            [
                x[..., : BINS - 1],
                x[..., BINS : 2 * BINS - 1],
                x[..., BINS - 1 : BINS],
                x[..., 2 * BINS - 1 :],
                jnp.zeros(x.shape[:-1] + (EXTRA - 2,), kind),
            ],
            axis=-1,
        )

    head_low = reordered(head_weight.astype(low), low)
    head_bias_all = reordered(head_bias, f32)[None]
    ups = [None] * BLOCKS
    downs = [None] * BLOCKS
    for b in range(BLOCKS):
        ups[b] = gathered(up_weight[b])
        downs[b] = gathered(down_weight[b])
    head_pieces = gathered(head_low)

    row_ids = lax.axis_index("seq") * rows - HALO + jnp.arange(ext, dtype=jnp.int32)
    squared = jnp.asarray((window_values() ** 2).reshape(4, HOP), f32)
    envelope = jnp.zeros((ext, HOP), f32)
    for q in range(4):
        source = row_ids + 2 - q
        envelope = envelope + ((source >= 0) & (source < seq_rows)).astype(f32)[:, None] * squared[q]
    recip = jnp.where(((row_ids >= 0) & (row_ids < seq_rows))[:, None], 1.0 / envelope, 0.0)
    tables = jnp.asarray(head_tables())
    scal = jnp.concatenate(
        [
            jnp.stack([lax.axis_index("seq") * rows - HALO, jnp.int32(seq_rows), lax.axis_index("dp")]).astype(jnp.int32),
            lengths[:, 0],
        ]
    )

    extended = jnp.concatenate([before[..., :width], features, after[..., :width]], axis=1)
    grad_rows = jnp.concatenate([before[..., width:].astype(f32), audio_grad, after[..., width:].astype(f32)], axis=1)

    def shape(columns):
        return (micro, ext, columns)

    def dma(size=count):
        return pltpu.SemaphoreType.DMA((size,))

    run = functools.partial(call, grid=micro, scal=scal)
    cells = micro * ext
    (table_grad,) = run(
        functools.partial(dft_kernel, ext),
        ins=[(grad_rows, "rows"), (recip, "all"), (tables, "all")],
        outs=[(shape(NFFT), low, "rows")],
        scratch=[],
        flops=2 * cells * NFFT * NFFT,
        name="dft",
    )
    normed, unit, inv_std = run(
        functools.partial(conv_kernel, ext),
        ins=[(extended, "rows"), (taps[0], "all"), (vecs[0], "all")],
        outs=[(shape(width), low, "rows"), (shape(width), low, "rows"), (shape(1), f32, "rows")],
        scratch=[],
        flops=20 * cells * width,
        name="conv",
    )
    mm = 2 * cells * width * units
    saved = []
    source = extended
    for b in range(BLOCKS):
        act, slope = run(
            functools.partial(up_kernel, 256),
            ins=[(normed, "rows"), (up_bias_all[b], "all"), (ups[b][0], "any"), (ups[b][1], "any")],
            outs=[(shape(units), low, "rows"), (shape(units), low, "rows")],
            scratch=[pltpu.VMEM((width, units), low), dma()],
            flops=mm,
            name=f"up{b}",
        )
        final = b == BLOCKS - 1
        after_conv = [] if final else [(shape(width), low, "rows"), (shape(width), low, "rows"), (shape(1), f32, "rows")]
        results = run(
            functools.partial(down_kernel, ext, b == 0, final),
            ins=[
                (act, "rows"),
                (source, "rows"),
                (vecs[b], "all"),
                (taps[min(b + 1, BLOCKS - 1)], "all"),
                (vecs[min(b + 1, BLOCKS - 1)], "all"),
                (downs[b][0], "any"),
                (downs[b][1], "any"),
            ],
            outs=[(shape(width), f32, "rows"), (shape(width), low, "rows")] + after_conv,
            scratch=[pltpu.VMEM((units, width), low), dma()],
            flops=mm,
            name=f"down{b}",
        )
        saved.append((source, normed, unit, inv_std, act, slope, results[1]))
        source = results[0]
        if not final:
            normed, unit, inv_std = results[2:]

    columns = 2 * HALF + EXTRA
    audio, incoming, head_keep, head_send, head_small, bias_grad = run(
        functools.partial(head_kernel, ext, rows),
        ins=[
            (source, "rows"),
            (table_grad, "rows"),
            (recip, "all"),
            (tables, "all"),
            (head_vec, "all"),
            (head_bias_all, "all"),
            (head_pieces[0], "any"),
            (head_pieces[1], "any"),
        ],
        outs=[
            ((micro, rows, HOP), f32, "rows"),
            (shape(width), f32, "rows"),
            ((pairs, own, columns), f32, "all"),
            ((pairs, own, columns), low, "all"),
            ((8, width), f32, "all"),
            ((1, columns), f32, "all"),
        ],
        scratch=[pltpu.VMEM((width, columns), low), pltpu.VMEM((width, columns), f32), dma()],
        flops=2 * cells * (3 * width * columns + NFFT * NFFT),
        name="head",
    )
    head_part = scattered(head_keep, head_send)
    smalls = [None] * BLOCKS
    up_parts = [None] * BLOCKS
    down_parts = [None] * BLOCKS
    for b in reversed(range(BLOCKS)):
        block_source, normed, unit, inv_std, act, slope, branch = saved[b]
        pre_grad, keep, send, small_down, small_bias = run(
            functools.partial(back_down_kernel, rows, 512),
            ins=[
                (incoming, "rows"),
                (branch, "rows"),
                (act, "rows"),
                (slope, "rows"),
                (vecs[b], "all"),
                (downs[b][0], "any"),
                (downs[b][1], "any"),
            ],
            outs=[
                (shape(units), low, "rows"),
                ((pairs, units // count, width), f32, "all"),
                ((pairs, units // count, width), low, "all"),
                ((8, width), f32, "all"),
                ((1, units), f32, "all"),
            ],
            scratch=[pltpu.VMEM((units, width), low), pltpu.VMEM((units, width), f32), dma()],
            flops=2 * mm,
            name=f"back_down{b}",
        )
        down_parts[b] = scattered(keep, send)
        keep, send = run(
            functools.partial(up_grad_kernel, rows),
            ins=[(normed, "rows"), (pre_grad, "rows")],
            outs=[((pairs, own, units), f32, "all"), ((pairs, own, units), low, "all")],
            scratch=[pltpu.VMEM((width, units), f32)],
            flops=mm,
            name=f"up_grad{b}",
        )
        up_parts[b] = scattered(keep, send)
        kind = (micro, rows, width) if b == 0 else shape(width)
        incoming, small_conv = run(
            functools.partial(back_up_kernel, ext, rows, b == 0),
            ins=[
                (pre_grad, "rows"),
                (unit, "rows"),
                (inv_std, "rows"),
                (block_source, "rows"),
                (incoming, "rows"),
                (vecs[b], "all"),
                (taps[b], "all"),
                (ups[b][0], "any"),
                (ups[b][1], "any"),
            ],
            outs=[(kind, f32, "rows"), ((16, width), f32, "all")],
            scratch=[pltpu.VMEM((width, units), low), dma()],
            flops=mm,
            name=f"back_up{b}",
        )
        smalls[b] = (small_down, small_bias, small_conv)

    tap_rows = [smalls[b][2][:KERNEL] for b in range(BLOCKS)]
    gain_rows = [r for b in range(BLOCKS) for r in (smalls[b][2][8:9], smalls[b][0][0:1])]
    bias_rows = [r for b in range(BLOCKS) for r in (smalls[b][2][7:8], smalls[b][2][9:10], smalls[b][0][1:2])]
    small_grads = jnp.concatenate(
        [
            jnp.concatenate(tap_rows + gain_rows + bias_rows + [head_small[0:2]])
            .reshape(-1, count, own)
            .swapaxes(0, 1)
            .reshape(count, -1),
            jnp.concatenate([smalls[b][1] for b in range(BLOCKS)])
            .reshape(BLOCKS, count, -1)
            .swapaxes(0, 1)
            .reshape(count, -1),
        ],
        axis=1,
    )
    small_all = summed_everywhere(small_grads)
    mine = lax.dynamic_index_in_dim(small_all, lax.axis_index("dp"), 0, keepdims=False)
    bias_grad = summed_everywhere(bias_grad)[0]
    entries = mine[: 26 * own].reshape(26, own)
    head_part = over_seq(head_part)

    def restored(x):
        return jnp.concatenate(
            [
                x[..., :HALF],
                x[..., 2 * HALF : 2 * HALF + 1],
                x[..., HALF : 2 * HALF],
                x[..., 2 * HALF + 1 : 2 * HALF + 2],
            ],
            axis=-1,
        )

    return (
        audio[:, None],
        incoming[:, None],
        entries[:14].reshape(BLOCKS, KERNEL, own),
        entries[14:18].reshape(BLOCKS, 2, own),
        entries[18:24].reshape(BLOCKS, 3, own),
        jnp.stack([over_seq(up_parts[b]) for b in range(BLOCKS)]),
        mine[26 * own :].reshape(BLOCKS, -1),
        jnp.stack([over_seq(down_parts[b]) for b in range(BLOCKS)]),
        entries[24],
        entries[25],
        restored(head_part),
        restored(bias_grad),
    )


def solution(mesh):
    return jax.shard_map(
        per_device,
        mesh=mesh,
        in_specs=(
            P(None, "dp", "seq", None),
            P(None, "dp"),
            P(None, None, "dp"),
            P(None, None, "dp"),
            P(None, None, "dp"),
            P(None, "dp", None),
            P(None, "dp"),
            P(None, "dp", None),
            P("dp"),
            P("dp"),
            P("dp", None),
            P(),
            P(None, "dp", "seq", None),
        ),
        out_specs=(
            P(None, "dp", "seq", None),
            P(None, "dp", "seq", None),
            P(None, None, "dp"),
            P(None, None, "dp"),
            P(None, None, "dp"),
            P(None, "dp", None),
            P(None, "dp"),
            P(None, "dp", None),
            P("dp"),
            P("dp"),
            P("dp", None),
            P(),
        ),
        check_vma=False,
    )
```

time: 1170 us -> 420 us (0.36)
  matrix products: 474 us -> 0 us
  Pallas kernels: 0 us -> 191 us
  waiting for transfers between devices: 203 us -> 56.8 us
  blocking collectives: 114 us -> 0 us
  other arithmetic: 111 us -> 29.3 us
  local copies, waits for them, and re-layouts: 102 us -> 39.9 us
  starting transfers between devices: 139 us -> 96.2 us
  between operations: 20.5 us -> 2.08 us
    dot_general x76 -> x0, matrix products: 474 us -> none  [the longest x4 72.6 us: head_forward(): jnp.dot(imag_part, sin_table, precision=exact_mode, preferred_element_typ...]
    pallas_call x0 -> x13, Pallas kernels: none -> 191 us  [call(): pl.pallas_call(kernel, out_shape=[jax.ShapeDtypeStruct(tuple(s), d) for s...]
    unnamed x15 -> x0, waiting for transfers between devices: 140 us -> none
    psum x2 -> x0, blocking collectives: 51.1 us -> none  [the longest x1 39 us: per_device(): bias_grad = lax.psum(bias_total, ('dp', 'seq'))]
    convert_element_type x48 -> x20, other arithmetic: 54.9 us -> 5.7 us  [the longest x5 2.84 us: over_seq(): part.astype(low).reshape((count, part.shape[0] // count) + part.shape[1:])]
    ppermute x48 -> x86, waiting for transfers between devices: 8.2 us -> 56.8 us  [the longest x84 56.8 us: swap(): lax.ppermute(x, axis, [(i, i ^ d) for i in range(lax.axis_size(axis))])]
    ppermute x48 -> x86, starting transfers between devices: 138 us -> 96.2 us  [the longest x84 90.3 us: swap(): lax.ppermute(x, axis, [(i, i ^ d) for i in range(lax.axis_size(axis))])]
    unnamed x639 -> x63, local copies, waits for them, and re-layouts: 48.2 us -> 6.39 us
  transfers between devices with their start and end apart: 59 -> 86, of which waited for: 12 -> 25; matrix products, arithmetic and copies ran while one was open for 49% -> 13% of each run, Pallas kernels for 0% -> 22%
where the time goes in v1:
time: 420 us; the launch traced here: 415 us
  Pallas kernels  191 us (45%)
  starting transfers between devices  96.2 us (23%)
  waiting for transfers between devices  56.8 us (14%)
  local copies, waits for them, and re-layouts  39.9 us (10%)
  other arithmetic  29.3 us (7%)
    pallas_call x13, Pallas kernels, call(): pl.pallas_call(kernel, out_shape=[jax.ShapeDtypeStruct(tuple(s), d) for s...  191 us
    ppermute x84, starting transfers between devices, swap(): lax.ppermute(x, axis, [(i, i ^ d) for i in range(lax.axis_size(axis))])  90.3 us
    ppermute x84, waiting for transfers between devices, swap(): lax.ppermute(x, axis, [(i, i ^ d) for i in range(lax.axis_size(axis))])  56.8 us
  transfers between devices with their start and end apart: 86, of which 25 were waited for; matrix products, arithmetic and copies ran while one was open for 13% of the time, Pallas kernels for 22%

profile of v1, /device:TPU:0, one launch (start us, length us, event | category | flops | bytes accessed | tf_op | source)
XLA Modules:
  0.0 415.5 jit_solution(11204817935430750456)
XLA Ops:
  4.7 3.0 collective-permute-start.2
  7.7 1.5 collective-permute-start.3
  9.2 1.8 fusion.73
  11.0 1.9 collective-permute-start.6
  12.9 1.5 collective-permute-start.7
  21.9 4.6 %collective-permute-start = (bf16[4,16,768]{2,1,0:T(8,128)(2,1)}, bf16[4,16,768]{2,1,0:T(8,128)(2,1)}, u32[]{:S(2)}, u32[]{:S(2)}) collective-permute-start(bf16[4,16,768]{2,1,0:T(8,128)(2,1)} %pad_maximum_fusion.12), channel_id=1, source_target_pairs={{0,1},{1,2},{2,3},{4,5},{5,6},{6,7},{8,9},{9,10},{10,11},{12,13},{... | collective-permute-start | bytes 294920 | tf_op jit(solution)/shard_map/ppermute | solution.py:439
  30.3 2.1 concatenate.69
  47.3 1.5 collective-permute-start.10
  49.6 1.6 collective-permute-start.11
  51.9 1.5 pad_maximum_fusion.1.grad_ref
  53.4 9.9 %dft.1.tgrad_ref = bf16[4,544,1024]{2,1,0:T(8,128)(2,1)} custom-call(s32[7]{0:T(128)} %pad_add_fusion.scal, f32[4,544,256]{2,1,0:T(8,128)} %pad_maximum_fusion.1.grad_ref, f32[544,256]{1,0:T(8,128)} %divide_select_fusion.recip_ref, bf16[1024,1024]{1,0:T(8,128)(2,1)} %constant.59.clone.table_ref), custom_call_target="tpu_custom_call" | custom-call | flops 4563402752 | bytes 9338880 | tf_op jit(solution)/shard_map/dft/pallas_call | solution.py:135
  67.1 1.5 collective-permute-start.15
  71.9 1.9 collective-permute-done.12
  75.4 9.6 %conv.1 = (bf16[4,544,512]{2,1,0:T(8,128)(2,1)}, bf16[4,544,512]{2,1,0:T(8,128)(2,1)}, f32[4,544,1]{2,1,0:T(8,128)}) custom-call(s32[7]{0:T(128)} %pad_add_fusion.scal, bf16[4,544,512]{2,1,0:T(8,128)(2,1)} %pad_maximum_fusion.features_ref.h_ref.block_in_ref, f32[8,512]{1,0:T(8,128)} %broadcast_select_fusion.1.taps_ref, f32[8,512]{1,0:T(8,128)} %get-tuple-element.229.vec_ref), custom_call_target="tpu_custom_call" | custom-call | flops 22282240 | bytes 6726144 | tf_op jit(solution)/shard_map/conv/pallas_call | solution.py:135
  85.6 1.5 collective-permute-start.24
  87.2 1.5 collective-permute-start.18
  88.8 5.8 %collective-permute-done.23 = bf16[64,1152]{1,0:T(8,128)(2,1)S(1)} collective-permute-done((bf16[64,1152]{1,0:T(8,128)(2,1)S(1)}, bf16[64,1152]{1,0:T(8,128)(2,1)S(1)}, u32[]{:S(2)}, u32[]{:S(2)}) %collective-permute-start.23) | collective-permute-done | bytes 147488 | tf_op jit(solution)/shard_map/ppermute | solution.py:45
  95.0 1.5 collective-permute-start.20
  97.0 8.4 %collective-permute-done.19 = bf16[192,512]{1,0:T(8,128)(2,1)S(1)} collective-permute-done((bf16[192,512]{1,0:T(8,128)(2,1)S(1)}, bf16[192,512]{1,0:T(8,128)(2,1)S(1)}, u32[]{:S(2)}, u32[]{:S(2)}) %collective-permute-start.19) | collective-permute-done | bytes 196640 | tf_op jit(solution)/shard_map/ppermute | solution.py:45
  106.9 12.2 %up0.1 = (bf16[4,544,1536]{2,1,0:T(8,128)(2,1)}, bf16[4,544,1536]{2,1,0:T(8,128)(2,1)}) custom-call(s32[7]{0:T(128)} %pad_add_fusion.scal, bf16[4,544,512]{2,1,0:T(8,128)(2,1)} %get-tuple-element.50.normed_ref, f32[1,1536]{1,0:T(1,128)} %squeeze.149.bias_ref, bf16[4,64,1536]{2,1,0:T(8,128)(2,1)} %copy-done.3, bf16[4,64,1536]{2,1,0:T(8,128)(2,1)} %copy-done.13), custom_call_target="tpu_custom_call" | custom-call | flops 3422552064 | bytes 17176576 | tf_op jit(solution)/shard_map/up0/pallas_call | solution.py:135
  120.1 16.2 %down0.1 = (f32[4,544,512]{2,1,0:T(8,128)}, bf16[4,544,512]{2,1,0:T(8,128)(2,1)}, bf16[4,544,512]{2,1,0:T(8,128)(2,1)}, bf16[4,544,512]{2,1,0:T(8,128)(2,1)}, f32[4,544,1]{2,1,0:T(8,128)}) custom-call(s32[7]{0:T(128)} %pad_add_fusion.scal, bf16[4,544,1536]{2,1,0:T(8,128)(2,1)} %get-tuple-element.51.act_ref, ...), custom_call_target="tpu_custom_call" | custom-call | flops 3422552064 | bytes 21684736 | tf_op jit(solution)/shard_map/down0/pallas_call | solution.py:135
  137.2 12.1 %up1.1 = (bf16[4,544,1536]{2,1,0:T(8,128)(2,1)}, bf16[4,544,1536]{2,1,0:T(8,128)(2,1)}) custom-call(s32[7]{0:T(128)} %pad_add_fusion.scal, bf16[4,544,512]{2,1,0:T(8,128)(2,1)} %get-tuple-element.52.normed_ref, f32[1,1536]{1,0:T(1,128)} %squeeze.152.bias_ref, bf16[4,64,1536]{2,1,0:T(8,128)(2,1)} %copy-done.1, bf16[4,64,1536]{2,1,0:T(8,128)(2,1)} %copy-done.10), custom_call_target="tpu_custom_call" | custom-call | flops 3422552064 | bytes 17176576 | tf_op jit(solution)/shard_map/up1/pallas_call | solution.py:135
  150.2 11.8 %down1.1 = (f32[4,544,512]{2,1,0:T(8,128)}, bf16[4,544,512]{2,1,0:T(8,128)(2,1)}) custom-call(s32[7]{0:T(128)} %pad_add_fusion.scal, bf16[4,544,1536]{2,1,0:T(8,128)(2,1)} %get-tuple-element.53.act_ref, f32[4,544,512]{2,1,0:T(8,128)} %get-tuple-element.54.h_ref.block_in_ref, f32[8,512]{1,0:T(8,128)} %get-tuple-element.228.next_ref.vec_ref, ...), custom_call_target="tpu_custom_call" | custom-call | flops 3422552064 | bytes 19447808 | tf_op jit(solution)/shard_map/down1/pallas_call | solution.py:135
  162.0 27.2 %head.1 = (f32[4,512,256]{2,1,0:T(8,128)}, f32[4,544,512]{2,1,0:T(8,128)}, f32[4,64,1152]{2,1,0:T(8,128)}, bf16[4,64,1152]{2,1,0:T(8,128)(2,1)}, f32[8,512]{1,0:T(8,128)}, /*index=5*/f32[1,1152]{1,0:T(1,128)}) custom-call(s32[7]{0:T(128)} %pad_add_fusion.scal, f32[4,544,512]{2,1,0:T(8,128)} %get-tuple-element.55.h_ref, bf16[4,544,1024]{2,1,0:T(8,128)(2,1)} %dft.1.tgrad_ref, ...), custom_call_target="tpu_custom_call" | custom-call | flops 12264144896 | bytes 21111808 | tf_op jit(solution)/shard_map/head/pallas_call | solution.py:135
  189.3 17.0 %back_down1.1 = (bf16[4,544,1536]{2,1,0:T(8,128)(2,1)}, f32[4,192,512]{2,1,0:T(8,128)}, bf16[4,192,512]{2,1,0:T(8,128)(2,1)}, f32[8,512]{1,0:T(8,128)}, f32[1,1536]{1,0:T(1,128)}) custom-call(s32[7]{0:T(128)} %pad_add_fusion.scal, f32[4,544,512]{2,1,0:T(8,128)} %get-tuple-element.57.hgrad_ref, bf16[4,544,512]{2,1,0:T(8,128)(2,1)} %get-tuple-element.58.branch_ref, ...), custom_call_target="tpu_custom_call" | custom-call | flops 6845104128 | bytes 30709760 | tf_op jit(solution)/shard_map/back_down1/pallas_call | solution.py:135
  206.3 19.8 %back_up1.1 = (f32[4,544,512]{2,1,0:T(8,128)}, f32[16,512]{1,0:T(8,128)}) custom-call(s32[7]{0:T(128)} %pad_add_fusion.scal, bf16[4,544,1536]{2,1,0:T(8,128)(2,1)} %get-tuple-element.60.pgrad_ref, bf16[4,544,512]{2,1,0:T(8,128)(2,1)} %get-tuple-element.61.unit_ref, f32[4,544,1]{2,1,0:T(8,128)} %get-tuple-element.62.inv_ref, ...), custom_call_target="tpu_custom_call" | custom-call | flops 3422552064 | bytes 23929344 | tf_op jit(solution)/shard_map/back_up1/pallas_call | solution.py:135
  226.1 17.2 %back_down0.1 = (bf16[4,544,1536]{2,1,0:T(8,128)(2,1)}, f32[4,192,512]{2,1,0:T(8,128)}, bf16[4,192,512]{2,1,0:T(8,128)(2,1)}, f32[8,512]{1,0:T(8,128)}, f32[1,1536]{1,0:T(1,128)}) custom-call(s32[7]{0:T(128)} %pad_add_fusion.scal, f32[4,544,512]{2,1,0:T(8,128)} %get-tuple-element.63.hgrad_ref, bf16[4,544,512]{2,1,0:T(8,128)(2,1)} %get-tuple-element.64.branch_ref, ...), custom_call_target="tpu_custom_call" | custom-call | flops 6845104128 | bytes 30709760 | tf_op jit(solution)/shard_map/back_down0/pallas_call | solution.py:135
  243.3 20.0 %back_up0.1 = (f32[4,512,512]{2,1,0:T(8,128)}, f32[16,512]{1,0:T(8,128)}) custom-call(s32[7]{0:T(128)} %pad_add_fusion.scal, bf16[4,544,1536]{2,1,0:T(8,128)(2,1)} %get-tuple-element.66.pgrad_ref, bf16[4,544,512]{2,1,0:T(8,128)(2,1)} %get-tuple-element.67.unit_ref, f32[4,544,1]{2,1,0:T(8,128)} %get-tuple-element.68.inv_ref, ...), custom_call_target="tpu_custom_call" | custom-call | flops 3422552064 | bytes 21438976 | tf_op jit(solution)/shard_map/back_up0/pallas_call | solution.py:135
  269.8 3.1 collective-permute-done.82
  273.2 3.3 collective-permute-done.83
  276.5 2.7 collective-permute-start.84
  279.8 8.9 %up_grad0.1 = (f32[4,64,1536]{2,1,0:T(8,128)}, bf16[4,64,1536]{2,1,0:T(8,128)(2,1)}) custom-call(s32[7]{0:T(128)} %pad_add_fusion.scal, bf16[4,544,512]{2,1,0:T(8,128)(2,1)} %get-tuple-element.50.normed_ref, bf16[4,544,1536]{2,1,0:T(8,128)(2,1)} %get-tuple-element.66.pgrad_ref), custom_call_target="tpu_custom_call" | custom-call | flops 3422552064 | bytes 11272192 | tf_op jit(solution)/shard_map/up_grad0/pallas_call | solution.py:135
  288.7 2.6 collective-permute-start.85
  291.7 9.3 %up_grad1.1 = (f32[4,64,1536]{2,1,0:T(8,128)}, bf16[4,64,1536]{2,1,0:T(8,128)(2,1)}) custom-call(s32[7]{0:T(128)} %pad_add_fusion.scal, bf16[4,544,512]{2,1,0:T(8,128)(2,1)} %get-tuple-element.52.normed_ref, bf16[4,544,1536]{2,1,0:T(8,128)(2,1)} %get-tuple-element.60.pgrad_ref), custom_call_target="tpu_custom_call" | custom-call | flops 3422552064 | bytes 11272192 | tf_op jit(solution)/shard_map/up_grad1/pallas_call | solution.py:135
  301.8 4.4 %collective-permute-done.29 = f32[8,2048]{1,0:T(8,128)S(1)} collective-permute-done((f32[8,2048]{1,0:T(8,128)S(1)}, f32[8,2048]{1,0:T(8,128)S(1)}, u32[]{:S(2)}, u32[]{:S(2)}) %collective-permute-start.29) | collective-permute-done | bytes 65568 | tf_op jit(solution)/shard_map/ppermute | solution.py:45
  307.2 2.0 concatenate.75
  309.2 2.9 collective-permute-done.30
  312.9 1.6 collective-permute-start.72
  314.5 1.6 collective-permute-start.73
  316.5 2.6 collective-permute-done.72
  319.1 3.7 collective-permute-done.73
  323.5 4.0 collective-permute-start.77
  330.7 3.1 collective-permute-start.79
  342.4 2.6 fusion.67
  352.6 2.3 collective-permute-done.54
  358.3 1.7 collective-permute-start.34
  361.5 1.8 collective-permute-done.64
  366.7 1.8 collective-permute-start.44
  368.8 2.9 collective-permute-done.34
  371.7 1.8 collective-permute-start.56
  375.9 2.1 collective-permute-done.44
  379.5 2.6 collective-permute-start.57
  384.6 2.5 collective-permute-start.67
  387.6 1.5 collective-permute-start.46
  389.1 2.5 collective-permute-start.47
  391.7 1.9 collective-permute-start.59
  393.6 2.5 collective-permute-start.60
  396.2 1.9 collective-permute-start.69
  398.1 2.5 collective-permute-start.70
  400.7 1.9 collective-permute-start.39
  402.7 2.5 collective-permute-start.40
  405.3 1.9 collective-permute-start.49
  407.3 2.5 collective-permute-start.50
  410.3 2.9 collective-permute-done.50
  (350 shorter events, 94.7 us)
Async XLA Ops:
  4.7 17.2 %collective-permute-start.2 = (bf16[34,64]{1,0:T(8,128)(2,1)S(1)}, bf16[34,64]{1,0:T(8,128)(2,1)}, u32[]{:S(2)}, u32[]{:S(2)}) collective-permute-start(bf16[34,64]{1,0:T(8,128)(2,1)S(1)} %concatenate.61), channel_id=1, source_target_pairs={{0,8},{4,12},{8,0},{12,4},{16,24},{20,28},{24,16},{28,20},{1,9},{5... | collective-permute-start | bytes 13064 | tf_op jit(solution)/shard_map/ppermute | solution.py:45
  7.7 14.3 %collective-permute-start.3 = (bf16[34,64]{1,0:T(8,128)(2,1)S(1)}, bf16[34,64]{1,0:T(8,128)(2,1)}, u32[]{:S(2)}, u32[]{:S(2)}) collective-permute-start(bf16[34,64]{1,0:T(8,128)(2,1)S(1)} %concatenate.61), channel_id=1, source_target_pairs={{0,16},{4,20},{8,24},{12,28},{16,0},{20,4},{24,8},{28,12},{1,17},{... | collective-permute-start | bytes 13064 | tf_op jit(solution)/shard_map/ppermute | solution.py:45
  9.2 17.3 %collective-permute-start.4 = (bf16[34,64]{1,0:T(8,128)(2,1)S(1)}, bf16[34,64]{1,0:T(8,128)(2,1)}, u32[]{:S(2)}, u32[]{:S(2)}) collective-permute-start(bf16[34,64]{1,0:T(8,128)(2,1)S(1)} %concatenate.61), channel_id=1, source_target_pairs={{0,24},{4,28},{8,16},{12,20},{16,8},{20,12},{24,0},{28,4},{1,25},{... | collective-permute-start | bytes 13064 | tf_op jit(solution)/shard_map/ppermute | solution.py:45
  11.0 54.1 %collective-permute-start.6 = (bf16[64,1536]{1,0:T(8,128)(2,1)}, bf16[64,1536]{1,0:T(8,128)(2,1)}, u32[]{:S(2)}, u32[]{:S(2)}) collective-permute-start(bf16[64,1536]{1,0:T(8,128)(2,1)} %get-tuple-element.174), channel_id=1, source_target_pairs={{0,8},{4,12},{8,0},{12,4},{16,24},{20,28},{24,16},{28,20},{1,9},{5... | collective-permute-start | bytes 589832 | tf_op jit(solution)/shard_map/ppermute | solution.py:45
  12.9 52.7 %collective-permute-start.7 = (bf16[64,1536]{1,0:T(8,128)(2,1)}, bf16[64,1536]{1,0:T(8,128)(2,1)}, u32[]{:S(2)}, u32[]{:S(2)}) collective-permute-start(bf16[64,1536]{1,0:T(8,128)(2,1)} %get-tuple-element.174), channel_id=1, source_target_pairs={{0,16},{4,20},{8,24},{12,28},{16,0},{20,4},{24,8},{28,12},{1,17},{... | collective-permute-start | bytes 589832 | tf_op jit(solution)/shard_map/ppermute | solution.py:45
  21.9 45.2 %collective-permute-start.8 = (bf16[64,1536]{1,0:T(8,128)(2,1)}, bf16[64,1536]{1,0:T(8,128)(2,1)}, u32[]{:S(2)}, u32[]{:S(2)}) collective-permute-start(bf16[64,1536]{1,0:T(8,128)(2,1)} %get-tuple-element.174), channel_id=1, source_target_pairs={{0,24},{4,28},{8,16},{12,20},{16,8},{20,12},{24,0},{28,4},{1,25},{... | collective-permute-start | bytes 589832 | tf_op jit(solution)/shard_map/ppermute | solution.py:45
  21.9 27.6 %collective-permute-start = (bf16[4,16,768]{2,1,0:T(8,128)(2,1)}, bf16[4,16,768]{2,1,0:T(8,128)(2,1)}, u32[]{:S(2)}, u32[]{:S(2)}) collective-permute-start(bf16[4,16,768]{2,1,0:T(8,128)(2,1)} %pad_maximum_fusion.12), channel_id=1, source_target_pairs={{0,1},{1,2},{2,3},{4,5},{5,6},{6,7},{8,9},{9,10},{10,11},{12,13},{... | collective-permute-start | bytes 294920 | tf_op jit(solution)/shard_map/ppermute | solution.py:439
  34.4 12.9 %collective-permute-start.1 = (bf16[4,16,768]{2,1,0:T(8,128)(2,1)}, bf16[4,16,768]{2,1,0:T(8,128)(2,1)}, u32[]{:S(2)}, u32[]{:S(2)}) collective-permute-start(bf16[4,16,768]{2,1,0:T(8,128)(2,1)} %pad_maximum_fusion.13), channel_id=1, source_target_pairs={{1,0},{2,1},{3,2},{5,4},{6,5},{7,6},{9,8},{10,9},{11,10},{13,12},{... | collective-permute-start | bytes 294920 | tf_op jit(solution)/shard_map/ppermute | solution.py:440
  47.3 22.6 %collective-permute-start.10 = (bf16[192,512]{1,0:T(8,128)(2,1)}, bf16[192,512]{1,0:T(8,128)(2,1)S(1)}, u32[]{:S(2)}, u32[]{:S(2)}) collective-permute-start(bf16[192,512]{1,0:T(8,128)(2,1)} %get-tuple-element.170), channel_id=1, source_target_pairs={{0,8},{4,12},{8,0},{12,4},{16,24},{20,28},{24,16},{28,20},{1,9},{5... | collective-permute-start | bytes 589832 | tf_op jit(solution)/shard_map/ppermute | solution.py:45
  49.6 20.8 %collective-permute-start.11 = (bf16[192,512]{1,0:T(8,128)(2,1)}, bf16[192,512]{1,0:T(8,128)(2,1)S(1)}, u32[]{:S(2)}, u32[]{:S(2)}) collective-permute-start(bf16[192,512]{1,0:T(8,128)(2,1)} %get-tuple-element.170), channel_id=1, source_target_pairs={{0,16},{4,20},{8,24},{12,28},{16,0},{20,4},{24,8},{28,12},{1,17},{... | collective-permute-start | bytes 589832 | tf_op jit(solution)/shard_map/ppermute | solution.py:45
  65.1 8.8 %collective-permute-start.12 = (bf16[192,512]{1,0:T(8,128)(2,1)S(1)}, bf16[192,512]{1,0:T(8,128)(2,1)S(1)}, u32[]{:S(2)}, u32[]{:S(2)}) collective-permute-start(bf16[192,512]{1,0:T(8,128)(2,1)S(1)} %copy-done.16), channel_id=1, source_target_pairs={{0,24},{4,28},{8,16},{12,20},{16,8},{20,12},{24,0},{28,4},{1,25},{... | collective-permute-start | bytes 589832 | tf_op jit(solution)/shard_map/ppermute | solution.py:45
  65.6 20.0 %collective-permute-start.14 = (bf16[64,1536]{1,0:T(8,128)(2,1)S(1)}, bf16[64,1536]{1,0:T(8,128)(2,1)S(1)}, u32[]{:S(2)}, u32[]{:S(2)}) collective-permute-start(bf16[64,1536]{1,0:T(8,128)(2,1)S(1)} %get-tuple-element.175), channel_id=1, source_target_pairs={{0,8},{4,12},{8,0},{12,4},{16,24},{20,28},{24,16},{28,20},{1,9},{5... | collective-permute-start | bytes 589832 | tf_op jit(solution)/shard_map/ppermute | solution.py:45
  67.1 20.0 %collective-permute-start.15 = (bf16[64,1536]{1,0:T(8,128)(2,1)S(1)}, bf16[64,1536]{1,0:T(8,128)(2,1)S(1)}, u32[]{:S(2)}, u32[]{:S(2)}) collective-permute-start(bf16[64,1536]{1,0:T(8,128)(2,1)S(1)} %get-tuple-element.175), channel_id=1, source_target_pairs={{0,16},{4,20},{8,24},{12,28},{16,0},{20,4},{24,8},{28,12},{1,17},{... | collective-permute-start | bytes 589832 | tf_op jit(solution)/shard_map/ppermute | solution.py:45
  69.9 18.8 %collective-permute-start.16 = (bf16[64,1536]{1,0:T(8,128)(2,1)S(1)}, bf16[64,1536]{1,0:T(8,128)(2,1)S(1)}, u32[]{:S(2)}, u32[]{:S(2)}) collective-permute-start(bf16[64,1536]{1,0:T(8,128)(2,1)S(1)} %get-tuple-element.175), channel_id=1, source_target_pairs={{0,24},{4,28},{8,16},{12,20},{16,8},{20,12},{24,0},{28,4},{1,25},{... | collective-permute-start | bytes 589832 | tf_op jit(solution)/shard_map/ppermute | solution.py:45
  70.4 14.6 %collective-permute-start.22 = (bf16[64,1152]{1,0:T(8,128)(2,1)S(1)}, bf16[64,1152]{1,0:T(8,128)(2,1)S(1)}, u32[]{:S(2)}, u32[]{:S(2)}) collective-permute-start(bf16[64,1152]{1,0:T(8,128)(2,1)S(1)} %concatenate.70), channel_id=1, source_target_pairs={{0,8},{4,12},{8,0},{12,4},{16,24},{20,28},{24,16},{28,20},{1,9},{5... | collective-permute-start | bytes 442376 | tf_op jit(solution)/shard_map/ppermute | solution.py:45
  73.9 32.2 %collective-permute-start.9 = (bf16[4,64,1536]{2,1,0:T(8,128)(2,1)S(1)}, bf16[4,64,1536]{2,1,0:T(8,128)(2,1)S(1)}, u32[]{:S(2)}, u32[]{:S(2)}) collective-permute-start(bf16[4,64,1536]{2,1,0:T(8,128)(2,1)S(1)} %pad_maximum_fusion.2.even_ref), channel_id=1, source_target_pairs={{0,4},{4,0},{8,12},{12,8},{16,20},{20,16},{24,28},{28,24},{1,5},{5... | collective-permute-start | bytes 2359304 | tf_op jit(solution)/shard_map/ppermute | solution.py:45
  85.1 9.5 %collective-permute-start.23 = (bf16[64,1152]{1,0:T(8,128)(2,1)S(1)}, bf16[64,1152]{1,0:T(8,128)(2,1)S(1)}, u32[]{:S(2)}, u32[]{:S(2)}) collective-permute-start(bf16[64,1152]{1,0:T(8,128)(2,1)S(1)} %concatenate.70), channel_id=1, source_target_pairs={{0,16},{4,20},{8,24},{12,28},{16,0},{20,4},{24,8},{28,12},{1,17},{... | collective-permute-start | bytes 442376 | tf_op jit(solution)/shard_map/ppermute | solution.py:45
  85.6 9.4 %collective-permute-start.24 = (bf16[64,1152]{1,0:T(8,128)(2,1)S(1)}, bf16[64,1152]{1,0:T(8,128)(2,1)S(1)}, u32[]{:S(2)}, u32[]{:S(2)}) collective-permute-start(bf16[64,1152]{1,0:T(8,128)(2,1)S(1)} %concatenate.70), channel_id=1, source_target_pairs={{0,24},{4,28},{8,16},{12,20},{16,8},{20,12},{24,0},{28,4},{1,25},{... | collective-permute-start | bytes 442376 | tf_op jit(solution)/shard_map/ppermute | solution.py:45
  87.2 9.7 %collective-permute-start.18 = (bf16[192,512]{1,0:T(8,128)(2,1)S(1)}, bf16[192,512]{1,0:T(8,128)(2,1)S(1)}, u32[]{:S(2)}, u32[]{:S(2)}) collective-permute-start(bf16[192,512]{1,0:T(8,128)(2,1)S(1)} %get-tuple-element.171), channel_id=1, source_target_pairs={{0,8},{4,12},{8,0},{12,4},{16,24},{20,28},{24,16},{28,20},{1,9},{5... | collective-permute-start | bytes 589832 | tf_op jit(solution)/shard_map/ppermute | solution.py:45
  88.6 30.5 %collective-permute-start.13 = (bf16[4,192,512]{2,1,0:T(8,128)(2,1)S(1)}, bf16[4,192,512]{2,1,0:T(8,128)(2,1)S(1)}, u32[]{:S(2)}, u32[]{:S(2)}) collective-permute-start(bf16[4,192,512]{2,1,0:T(8,128)(2,1)S(1)} %pad_maximum_fusion.3.even_ref), channel_id=1, source_target_pairs={{0,4},{4,0},{8,12},{12,8},{16,20},{20,16},{24,28},{28,24},{1,5},{5... | collective-permute-start | bytes 2359304 | tf_op jit(solution)/shard_map/ppermute | solution.py:45
  94.6 10.7 %collective-permute-start.19 = (bf16[192,512]{1,0:T(8,128)(2,1)S(1)}, bf16[192,512]{1,0:T(8,128)(2,1)S(1)}, u32[]{:S(2)}, u32[]{:S(2)}) collective-permute-start(bf16[192,512]{1,0:T(8,128)(2,1)S(1)} %get-tuple-element.171), channel_id=1, source_target_pairs={{0,16},{4,20},{8,24},{12,28},{16,0},{20,4},{24,8},{28,12},{1,17},{... | collective-permute-start | bytes 589832 | tf_op jit(solution)/shard_map/ppermute | solution.py:45
  95.0 10.3 %collective-permute-start.20 = (bf16[192,512]{1,0:T(8,128)(2,1)S(1)}, bf16[192,512]{1,0:T(8,128)(2,1)S(1)}, u32[]{:S(2)}, u32[]{:S(2)}) collective-permute-start(bf16[192,512]{1,0:T(8,128)(2,1)S(1)} %get-tuple-element.171), channel_id=1, source_target_pairs={{0,24},{4,28},{8,16},{12,20},{16,8},{20,12},{24,0},{28,4},{1,25},{... | collective-permute-start | bytes 589832 | tf_op jit(solution)/shard_map/ppermute | solution.py:45
  96.9 39.4 %collective-permute-start.17 = (bf16[4,64,1536]{2,1,0:T(8,128)(2,1)S(1)}, bf16[4,64,1536]{2,1,0:T(8,128)(2,1)S(1)}, u32[]{:S(2)}, u32[]{:S(2)}) collective-permute-start(bf16[4,64,1536]{2,1,0:T(8,128)(2,1)S(1)} %pad_maximum_fusion.4.even_ref), channel_id=1, source_target_pairs={{0,4},{4,0},{8,12},{12,8},{16,20},{20,16},{24,28},{28,24},{1,5},{5... | collective-permute-start | bytes 2359304 | tf_op jit(solution)/shard_map/ppermute | solution.py:45
  105.3 56.7 %collective-permute-start.25 = (bf16[4,64,1152]{2,1,0:T(8,128)(2,1)S(1)}, bf16[4,64,1152]{2,1,0:T(8,128)(2,1)}, u32[]{:S(2)}, u32[]{:S(2)}) collective-permute-start(bf16[4,64,1152]{2,1,0:T(8,128)(2,1)S(1)} %pad_maximum_fusion.6.even_ref), channel_id=1, source_target_pairs={{0,4},{4,0},{8,12},{12,8},{16,20},{20,16},{24,28},{28,24},{1,5},{5... | collective-permute-start | bytes 1769480 | tf_op jit(solution)/shard_map/ppermute | solution.py:45
  105.4 43.9 %collective-permute-start.21 = (bf16[4,192,512]{2,1,0:T(8,128)(2,1)S(1)}, bf16[4,192,512]{2,1,0:T(8,128)(2,1)S(1)}, u32[]{:S(2)}, u32[]{:S(2)}) collective-permute-start(bf16[4,192,512]{2,1,0:T(8,128)(2,1)S(1)} %pad_maximum_fusion.5.even_ref), channel_id=1, source_target_pairs={{0,4},{4,0},{8,12},{12,8},{16,20},{20,16},{24,28},{28,24},{1,5},{5... | collective-permute-start | bytes 2359304 | tf_op jit(solution)/shard_map/ppermute | solution.py:45
  267.8 11.3 %collective-permute-start.26 = (f32[8,2048]{1,0:T(8,128)S(1)}, f32[8,2048]{1,0:T(8,128)S(1)}, u32[]{:S(2)}, u32[]{:S(2)}) collective-permute-start(f32[8,2048]{1,0:T(8,128)S(1)} %constant_dynamic-update-slice_fusion), channel_id=1, source_target_pairs={{0,4},{4,0},{8,12},{12,8},{16,20},{20,16},{24,28},{28,24},{1,5},{5... | collective-permute-start | bytes 196616 | tf_op jit(solution)/shard_map/ppermute | solution.py:45
  276.5 12.2 %collective-permute-start.84 = (f32[1,1152]{1,0:T(1,128)S(1)}, f32[1,1152]{1,0:T(1,128)S(1)}, u32[]{:S(2)}, u32[]{:S(2)}) collective-permute-start(f32[1,1152]{1,0:T(1,128)S(1)} %add.272), channel_id=1, source_target_pairs={{0,1},{1,0},{2,3},{3,2},{4,5},{5,4},{6,7},{7,6},{8,9},{9,8},{10,11... | collective-permute-start | bytes 13832 | tf_op jit(solution)/shard_map/ppermute | solution.py:45
  279.2 12.2 %collective-permute-start.27 = (f32[8,2048]{1,0:T(8,128)S(1)}, f32[8,2048]{1,0:T(8,128)S(1)}, u32[]{:S(2)}, u32[]{:S(2)}) collective-permute-start(f32[8,2048]{1,0:T(8,128)S(1)} %add.229), channel_id=1, source_target_pairs={{0,8},{4,12},{8,0},{12,4},{16,24},{20,28},{24,16},{28,20},{1,9},{5... | collective-permute-start | bytes 196616 | tf_op jit(solution)/shard_map/ppermute | solution.py:45
  288.7 13.0 %collective-permute-start.85 = (f32[1,1152]{1,0:T(1,128)S(1)}, f32[1,1152]{1,0:T(1,128)S(1)}, u32[]{:S(2)}, u32[]{:S(2)}) collective-permute-start(f32[1,1152]{1,0:T(1,128)S(1)} %add.273), channel_id=1, source_target_pairs={{0,2},{1,3},{2,0},{3,1},{4,6},{5,7},{6,4},{7,5},{8,10},{9,11},{10,... | collective-permute-start | bytes 13832 | tf_op jit(solution)/shard_map/ppermute | solution.py:45
  291.4 10.3 %collective-permute-start.28 = (f32[8,2048]{1,0:T(8,128)S(1)}, f32[8,2048]{1,0:T(8,128)S(1)}, u32[]{:S(2)}, u32[]{:S(2)}) collective-permute-start(f32[8,2048]{1,0:T(8,128)S(1)} %add.230), channel_id=1, source_target_pairs={{0,16},{4,20},{8,24},{12,28},{16,0},{20,4},{24,8},{28,12},{1,17},{... | collective-permute-start | bytes 196616 | tf_op jit(solution)/shard_map/ppermute | solution.py:45
  301.0 11.7 %collective-permute-start.71 = (bf16[4,64,1152]{2,1,0:T(8,128)(2,1)}, bf16[4,64,1152]{2,1,0:T(8,128)(2,1)S(1)}, u32[]{:S(2)}, u32[]{:S(2)}) collective-permute-start(bf16[4,64,1152]{2,1,0:T(8,128)(2,1)} %get-tuple-element.86), channel_id=1, source_target_pairs={{0,4},{4,0},{8,12},{12,8},{16,20},{20,16},{24,28},{28,24},{1,5},{5... | collective-permute-start | bytes 1769480 | tf_op jit(solution)/shard_map/ppermute | solution.py:45
  301.1 29.7 %collective-permute-start.51 = (bf16[4,192,512]{2,1,0:T(8,128)(2,1)S(1)}, bf16[4,192,512]{2,1,0:T(8,128)(2,1)S(1)}, u32[]{:S(2)}, u32[]{:S(2)}) collective-permute-start(bf16[4,192,512]{2,1,0:T(8,128)(2,1)S(1)} %copy-done.27), channel_id=1, source_target_pairs={{0,4},{4,0},{8,12},{12,8},{16,20},{20,16},{24,28},{28,24},{1,5},{5... | collective-permute-start | bytes 2359304 | tf_op jit(solution)/shard_map/ppermute | solution.py:45
  301.6 39.5 %collective-permute-start.61 = (bf16[4,192,512]{2,1,0:T(8,128)(2,1)}, bf16[4,192,512]{2,1,0:T(8,128)(2,1)}, u32[]{:S(2)}, u32[]{:S(2)}) collective-permute-start(bf16[4,192,512]{2,1,0:T(8,128)(2,1)} %get-tuple-element.84), channel_id=1, source_target_pairs={{0,4},{4,0},{8,12},{12,8},{16,20},{20,16},{24,28},{28,24},{1,5},{5... | collective-permute-start | bytes 2359304 | tf_op jit(solution)/shard_map/ppermute | solution.py:45
  314.5 8.3 %collective-permute-start.73 = (bf16[64,1152]{1,0:T(8,128)(2,1)S(1)}, bf16[64,1152]{1,0:T(8,128)(2,1)S(1)}, u32[]{:S(2)}, u32[]{:S(2)}) collective-permute-start(bf16[64,1152]{1,0:T(8,128)(2,1)S(1)} %get-tuple-element.168), channel_id=1, source_target_pairs={{0,16},{4,20},{8,24},{12,28},{16,0},{20,4},{24,8},{28,12},{1,17},{... | collective-permute-start | bytes 442376 | tf_op jit(solution)/shard_map/ppermute | solution.py:45
  323.0 7.1 %collective-permute-start.75 = (bf16[16,1152]{1,0:T(8,128)(2,1)S(1)}, bf16[16,1152]{1,0:T(8,128)(2,1)S(1)}, u32[]{:S(2)}, u32[]{:S(2)}) collective-permute-start(bf16[16,1152]{1,0:T(8,128)(2,1)S(1)} %get-tuple-element.193), channel_id=1, source_target_pairs={{0,1},{1,0},{2,3},{3,2},{4,5},{5,4},{6,7},{7,6},{8,9},{9,8},{10,11... | collective-permute-start | bytes 110600 | tf_op jit(solution)/shard_map/ppermute | solution.py:45
  323.1 7.1 %collective-permute-start.76 = (bf16[16,1152]{1,0:T(8,128)(2,1)S(1)}, bf16[16,1152]{1,0:T(8,128)(2,1)S(1)}, u32[]{:S(2)}, u32[]{:S(2)}) collective-permute-start(bf16[16,1152]{1,0:T(8,128)(2,1)S(1)} %get-tuple-element.195), channel_id=1, source_target_pairs={{0,2},{1,3},{2,0},{3,1},{4,6},{5,7},{6,4},{7,5},{8,10},{9,11},{10,... | collective-permute-start | bytes 110600 | tf_op jit(solution)/shard_map/ppermute | solution.py:45
  323.5 7.1 %collective-permute-start.77 = (bf16[16,1152]{1,0:T(8,128)(2,1)S(1)}, bf16[16,1152]{1,0:T(8,128)(2,1)S(1)}, u32[]{:S(2)}, u32[]{:S(2)}) collective-permute-start(bf16[16,1152]{1,0:T(8,128)(2,1)S(1)} %get-tuple-element.194), channel_id=1, source_target_pairs={{0,3},{1,2},{2,1},{3,0},{4,7},{5,6},{6,5},{7,4},{8,11},{9,10},{10,... | collective-permute-start | bytes 110600 | tf_op jit(solution)/shard_map/ppermute | solution.py:45
  330.1 7.6 %collective-permute-start.41 = (bf16[4,64,1536]{2,1,0:T(8,128)(2,1)}, bf16[4,64,1536]{2,1,0:T(8,128)(2,1)S(1)}, u32[]{:S(2)}, u32[]{:S(2)}) collective-permute-start(bf16[4,64,1536]{2,1,0:T(8,128)(2,1)} %get-tuple-element.80), channel_id=1, source_target_pairs={{0,4},{4,0},{8,12},{12,8},{16,20},{20,16},{24,28},{28,24},{1,5},{5... | collective-permute-start | bytes 2359304 | tf_op jit(solution)/shard_map/ppermute | solution.py:45
  330.7 15.2 %collective-permute-start.78 = (bf16[16,1152]{1,0:T(8,128)(2,1)S(1)}, bf16[16,1152]{1,0:T(8,128)(2,1)S(1)}, u32[]{:S(2)}, u32[]{:S(2)}) collective-permute-start(bf16[16,1152]{1,0:T(8,128)(2,1)S(1)} %fusion.44), channel_id=1, source_target_pairs={{0,1},{1,0},{2,3},{3,2},{4,5},{5,4},{6,7},{7,6},{8,9},{9,8},{10,11... | collective-permute-start | bytes 110600 | tf_op jit(solution)/shard_map/ppermute | solution.py:45
  330.7 16.3 %collective-permute-start.79 = (bf16[16,1152]{1,0:T(8,128)(2,1)S(1)}, bf16[16,1152]{1,0:T(8,128)(2,1)S(1)}, u32[]{:S(2)}, u32[]{:S(2)}) collective-permute-start(bf16[16,1152]{1,0:T(8,128)(2,1)S(1)} %fusion.44), channel_id=1, source_target_pairs={{0,2},{1,3},{2,0},{3,1},{4,6},{5,7},{6,4},{7,5},{8,10},{9,11},{10,... | collective-permute-start | bytes 110600 | tf_op jit(solution)/shard_map/ppermute | solution.py:45
  336.2 11.8 %collective-permute-start.80 = (bf16[16,1152]{1,0:T(8,128)(2,1)S(1)}, bf16[16,1152]{1,0:T(8,128)(2,1)S(1)}, u32[]{:S(2)}, u32[]{:S(2)}) collective-permute-start(bf16[16,1152]{1,0:T(8,128)(2,1)S(1)} %fusion.44), channel_id=1, source_target_pairs={{0,3},{1,2},{2,1},{3,0},{4,7},{5,6},{6,5},{7,4},{8,11},{9,10},{10,... | collective-permute-start | bytes 110600 | tf_op jit(solution)/shard_map/ppermute | solution.py:45
  337.7 12.7 %collective-permute-start.52 = (bf16[192,512]{1,0:T(8,128)(2,1)}, bf16[192,512]{1,0:T(8,128)(2,1)}, u32[]{:S(2)}, u32[]{:S(2)}) collective-permute-start(bf16[192,512]{1,0:T(8,128)(2,1)} %get-tuple-element.154), channel_id=1, source_target_pairs={{0,8},{4,12},{8,0},{12,4},{16,24},{20,28},{24,16},{28,20},{1,9},{5... | collective-permute-start | bytes 589832 | tf_op jit(solution)/shard_map/ppermute | solution.py:45
  341.0 10.6 %collective-permute-start.53 = (bf16[192,512]{1,0:T(8,128)(2,1)}, bf16[192,512]{1,0:T(8,128)(2,1)}, u32[]{:S(2)}, u32[]{:S(2)}) collective-permute-start(bf16[192,512]{1,0:T(8,128)(2,1)} %get-tuple-element.156), channel_id=1, source_target_pairs={{0,16},{4,20},{8,24},{12,28},{16,0},{20,4},{24,8},{28,12},{1,17},{... | collective-permute-start | bytes 589832 | tf_op jit(solution)/shard_map/ppermute | solution.py:45
  345.8 9.1 %collective-permute-start.54 = (bf16[192,512]{1,0:T(8,128)(2,1)}, bf16[192,512]{1,0:T(8,128)(2,1)}, u32[]{:S(2)}, u32[]{:S(2)}) collective-permute-start(bf16[192,512]{1,0:T(8,128)(2,1)} %get-tuple-element.155), channel_id=1, source_target_pairs={{0,24},{4,28},{8,16},{12,20},{16,8},{20,12},{24,0},{28,4},{1,25},{... | collective-permute-start | bytes 589832 | tf_op jit(solution)/shard_map/ppermute | solution.py:45
  347.0 11.3 %collective-permute-start.62 = (bf16[192,512]{1,0:T(8,128)(2,1)}, bf16[192,512]{1,0:T(8,128)(2,1)}, u32[]{:S(2)}, u32[]{:S(2)}) collective-permute-start(bf16[192,512]{1,0:T(8,128)(2,1)} %get-tuple-element.157), channel_id=1, source_target_pairs={{0,8},{4,12},{8,0},{12,4},{16,24},{20,28},{24,16},{28,20},{1,9},{5... | collective-permute-start | bytes 589832 | tf_op jit(solution)/shard_map/ppermute | solution.py:45
  348.0 12.4 %collective-permute-start.63 = (bf16[192,512]{1,0:T(8,128)(2,1)}, bf16[192,512]{1,0:T(8,128)(2,1)}, u32[]{:S(2)}, u32[]{:S(2)}) collective-permute-start(bf16[192,512]{1,0:T(8,128)(2,1)} %get-tuple-element.159), channel_id=1, source_target_pairs={{0,16},{4,20},{8,24},{12,28},{16,0},{20,4},{24,8},{28,12},{1,17},{... | collective-permute-start | bytes 589832 | tf_op jit(solution)/shard_map/ppermute | solution.py:45
  350.4 12.8 %collective-permute-start.64 = (bf16[192,512]{1,0:T(8,128)(2,1)}, bf16[192,512]{1,0:T(8,128)(2,1)S(1)}, u32[]{:S(2)}, u32[]{:S(2)}) collective-permute-start(bf16[192,512]{1,0:T(8,128)(2,1)} %get-tuple-element.158), channel_id=1, source_target_pairs={{0,24},{4,28},{8,16},{12,20},{16,8},{20,12},{24,0},{28,4},{1,25},{... | collective-permute-start | bytes 589832 | tf_op jit(solution)/shard_map/ppermute | solution.py:45
  351.6 15.1 %collective-permute-start.32 = (bf16[64,1536]{1,0:T(8,128)(2,1)}, bf16[64,1536]{1,0:T(8,128)(2,1)S(1)}, u32[]{:S(2)}, u32[]{:S(2)}) collective-permute-start(bf16[64,1536]{1,0:T(8,128)(2,1)} %get-tuple-element.160), channel_id=1, source_target_pairs={{0,8},{4,12},{8,0},{12,4},{16,24},{20,28},{24,16},{28,20},{1,9},{5... | collective-permute-start | bytes 589832 | tf_op jit(solution)/shard_map/ppermute | solution.py:45
  354.9 13.8 %collective-permute-start.33 = (bf16[64,1536]{1,0:T(8,128)(2,1)}, bf16[64,1536]{1,0:T(8,128)(2,1)S(1)}, u32[]{:S(2)}, u32[]{:S(2)}) collective-permute-start(bf16[64,1536]{1,0:T(8,128)(2,1)} %get-tuple-element.162), channel_id=1, source_target_pairs={{0,16},{4,20},{8,24},{12,28},{16,0},{20,4},{24,8},{28,12},{1,17},{... | collective-permute-start | bytes 589832 | tf_op jit(solution)/shard_map/ppermute | solution.py:45
  358.3 13.3 %collective-permute-start.34 = (bf16[64,1536]{1,0:T(8,128)(2,1)}, bf16[64,1536]{1,0:T(8,128)(2,1)S(1)}, u32[]{:S(2)}, u32[]{:S(2)}) collective-permute-start(bf16[64,1536]{1,0:T(8,128)(2,1)} %get-tuple-element.161), channel_id=1, source_target_pairs={{0,24},{4,28},{8,16},{12,20},{16,8},{20,12},{24,0},{28,4},{1,25},{... | collective-permute-start | bytes 589832 | tf_op jit(solution)/shard_map/ppermute | solution.py:45
  360.4 14.5 %collective-permute-start.42 = (bf16[64,1536]{1,0:T(8,128)(2,1)}, bf16[64,1536]{1,0:T(8,128)(2,1)S(1)}, u32[]{:S(2)}, u32[]{:S(2)}) collective-permute-start(bf16[64,1536]{1,0:T(8,128)(2,1)} %get-tuple-element.163), channel_id=1, source_target_pairs={{0,8},{4,12},{8,0},{12,4},{16,24},{20,28},{24,16},{28,20},{1,9},{5... | collective-permute-start | bytes 589832 | tf_op jit(solution)/shard_map/ppermute | solution.py:45
  363.2 12.6 %collective-permute-start.43 = (bf16[64,1536]{1,0:T(8,128)(2,1)}, bf16[64,1536]{1,0:T(8,128)(2,1)S(1)}, u32[]{:S(2)}, u32[]{:S(2)}) collective-permute-start(bf16[64,1536]{1,0:T(8,128)(2,1)} %get-tuple-element.165), channel_id=1, source_target_pairs={{0,16},{4,20},{8,24},{12,28},{16,0},{20,4},{24,8},{28,12},{1,17},{... | collective-permute-start | bytes 589832 | tf_op jit(solution)/shard_map/ppermute | solution.py:45
  366.7 11.4 %collective-permute-start.44 = (bf16[64,1536]{1,0:T(8,128)(2,1)S(1)}, bf16[64,1536]{1,0:T(8,128)(2,1)S(1)}, u32[]{:S(2)}, u32[]{:S(2)}) collective-permute-start(bf16[64,1536]{1,0:T(8,128)(2,1)S(1)} %copy-done.17), channel_id=1, source_target_pairs={{0,24},{4,28},{8,16},{12,20},{16,8},{20,12},{24,0},{28,4},{1,25},{... | collective-permute-start | bytes 589832 | tf_op jit(solution)/shard_map/ppermute | solution.py:45
  368.7 15.9 %collective-permute-start.55 = (bf16[48,512]{1,0:T(8,128)(2,1)S(1)}, bf16[48,512]{1,0:T(8,128)(2,1)S(1)}, u32[]{:S(2)}, u32[]{:S(2)}) collective-permute-start(bf16[48,512]{1,0:T(8,128)(2,1)S(1)} %get-tuple-element.181), channel_id=1, source_target_pairs={{0,1},{1,0},{2,3},{3,2},{4,5},{5,4},{6,7},{7,6},{8,9},{9,8},{10,11... | collective-permute-start | bytes 147464 | tf_op jit(solution)/shard_map/ppermute | solution.py:45
  371.7 15.5 %collective-permute-start.56 = (bf16[48,512]{1,0:T(8,128)(2,1)S(1)}, bf16[48,512]{1,0:T(8,128)(2,1)S(1)}, u32[]{:S(2)}, u32[]{:S(2)}) collective-permute-start(bf16[48,512]{1,0:T(8,128)(2,1)S(1)} %get-tuple-element.183), channel_id=1, source_target_pairs={{0,2},{1,3},{2,0},{3,1},{4,6},{5,7},{6,4},{7,5},{8,10},{9,11},{10,... | collective-permute-start | bytes 147464 | tf_op jit(solution)/shard_map/ppermute | solution.py:45
  379.5 8.1 %collective-permute-start.57 = (bf16[48,512]{1,0:T(8,128)(2,1)S(1)}, bf16[48,512]{1,0:T(8,128)(2,1)S(1)}, u32[]{:S(2)}, u32[]{:S(2)}) collective-permute-start(bf16[48,512]{1,0:T(8,128)(2,1)S(1)} %get-tuple-element.182), channel_id=1, source_target_pairs={{0,3},{1,2},{2,1},{3,0},{4,7},{5,6},{6,5},{7,4},{8,11},{9,10},{10,... | collective-permute-start | bytes 147464 | tf_op jit(solution)/shard_map/ppermute | solution.py:45
  384.0 7.7 %collective-permute-start.66 = (bf16[48,512]{1,0:T(8,128)(2,1)S(1)}, bf16[48,512]{1,0:T(8,128)(2,1)S(1)}, u32[]{:S(2)}, u32[]{:S(2)}) collective-permute-start(bf16[48,512]{1,0:T(8,128)(2,1)S(1)} %get-tuple-element.186), channel_id=1, source_target_pairs={{0,2},{1,3},{2,0},{3,1},{4,6},{5,7},{6,4},{7,5},{8,10},{9,11},{10,... | collective-permute-start | bytes 147464 | tf_op jit(solution)/shard_map/ppermute | solution.py:45
  384.6 7.0 %collective-permute-start.67 = (bf16[48,512]{1,0:T(8,128)(2,1)S(1)}, bf16[48,512]{1,0:T(8,128)(2,1)S(1)}, u32[]{:S(2)}, u32[]{:S(2)}) collective-permute-start(bf16[48,512]{1,0:T(8,128)(2,1)S(1)} %get-tuple-element.185), channel_id=1, source_target_pairs={{0,3},{1,2},{2,1},{3,0},{4,7},{5,6},{6,5},{7,4},{8,11},{9,10},{10,... | collective-permute-start | bytes 147464 | tf_op jit(solution)/shard_map/ppermute | solution.py:45
  387.6 8.6 %collective-permute-start.46 = (bf16[16,1536]{1,0:T(8,128)(2,1)S(1)}, bf16[16,1536]{1,0:T(8,128)(2,1)S(1)}, u32[]{:S(2)}, u32[]{:S(2)}) collective-permute-start(bf16[16,1536]{1,0:T(8,128)(2,1)S(1)} %get-tuple-element.192), channel_id=1, source_target_pairs={{0,2},{1,3},{2,0},{3,1},{4,6},{5,7},{6,4},{7,5},{8,10},{9,11},{10,... | collective-permute-start | bytes 147464 | tf_op jit(solution)/shard_map/ppermute | solution.py:45
  391.7 9.0 %collective-permute-start.59 = (bf16[48,512]{1,0:T(8,128)(2,1)S(1)}, bf16[48,512]{1,0:T(8,128)(2,1)S(1)}, u32[]{:S(2)}, u32[]{:S(2)}) collective-permute-start(bf16[48,512]{1,0:T(8,128)(2,1)S(1)} %fusion.35), channel_id=1, source_target_pairs={{0,2},{1,3},{2,0},{3,1},{4,6},{5,7},{6,4},{7,5},{8,10},{9,11},{10,... | collective-permute-start | bytes 147464 | tf_op jit(solution)/shard_map/ppermute | solution.py:45
  396.2 9.1 %collective-permute-start.69 = (bf16[48,512]{1,0:T(8,128)(2,1)S(1)}, bf16[48,512]{1,0:T(8,128)(2,1)S(1)}, u32[]{:S(2)}, u32[]{:S(2)}) collective-permute-start(bf16[48,512]{1,0:T(8,128)(2,1)S(1)} %fusion.32), channel_id=1, source_target_pairs={{0,2},{1,3},{2,0},{3,1},{4,6},{5,7},{6,4},{7,5},{8,10},{9,11},{10,... | collective-permute-start | bytes 147464 | tf_op jit(solution)/shard_map/ppermute | solution.py:45
  398.1 7.1 %collective-permute-start.70 = (bf16[48,512]{1,0:T(8,128)(2,1)S(1)}, bf16[48,512]{1,0:T(8,128)(2,1)S(1)}, u32[]{:S(2)}, u32[]{:S(2)}) collective-permute-start(bf16[48,512]{1,0:T(8,128)(2,1)S(1)} %fusion.32), channel_id=1, source_target_pairs={{0,3},{1,2},{2,1},{3,0},{4,7},{5,6},{6,5},{7,4},{8,11},{9,10},{10,... | collective-permute-start | bytes 147464 | tf_op jit(solution)/shard_map/ppermute | solution.py:45
  400.7 9.1 %collective-permute-start.39 = (bf16[16,1536]{1,0:T(8,128)(2,1)S(1)}, bf16[16,1536]{1,0:T(8,128)(2,1)S(1)}, u32[]{:S(2)}, u32[]{:S(2)}) collective-permute-start(bf16[16,1536]{1,0:T(8,128)(2,1)S(1)} %fusion.41), channel_id=1, source_target_pairs={{0,2},{1,3},{2,0},{3,1},{4,6},{5,7},{6,4},{7,5},{8,10},{9,11},{10,... | collective-permute-start | bytes 147464 | tf_op jit(solution)/shard_map/ppermute | solution.py:45
  402.7 7.1 %collective-permute-start.40 = (bf16[16,1536]{1,0:T(8,128)(2,1)S(1)}, bf16[16,1536]{1,0:T(8,128)(2,1)S(1)}, u32[]{:S(2)}, u32[]{:S(2)}) collective-permute-start(bf16[16,1536]{1,0:T(8,128)(2,1)S(1)} %fusion.41), channel_id=1, source_target_pairs={{0,3},{1,2},{2,1},{3,0},{4,7},{5,6},{6,5},{7,4},{8,11},{9,10},{10,... | collective-permute-start | bytes 147464 | tf_op jit(solution)/shard_map/ppermute | solution.py:45
  (51 other events, 449.8 us)

commit v2 on v0

v2 whole, which is shorter than its diff:
```python
import functools
import math

import jax
import jax.numpy as jnp
import numpy as np
from jax import lax
from jax.experimental import pallas as pl
from jax.experimental.pallas import tpu as pltpu
from jax.sharding import PartitionSpec as P

NFFT = 1024
HOP = 256
BINS = 513
HALF = 512
EXTRA = 128
KERNEL = 7
BLOCKS = 2
HALO = 16
SMALL = 32
norm_eps = 1e-06
f32 = jnp.float32
low = jnp.bfloat16
rows_dims = (((0,), (0,)), ((), ()))
cols_dims = (((1,), (1,)), ((), ()))
MiB = 2**20
GELU = (0.7978202661111929, 0.03654664812915587, -0.00019444764679970054, -1.3688682486738934e-05)
SIN = (6.283184921107194, -41.34159015596926, 81.59997289449204, -76.61480381354174, 41.34439732745281, -12.473668162531846)
COS = (0.9999992215705861, -19.738982516102407, 64.92872660899411, -85.27239689575316, 58.79403819232432, -21.076781286284348)


def window_values():
    return 0.5 - 0.5 * np.cos(np.arange(NFFT) * (2.0 * math.pi / NFFT))


def head_tables():
    row = np.arange(NFFT)
    frequency = np.where(row < HALF, row, np.where(row == HALF, HALF, row - HALF))
    angles = (frequency[:, None] * np.arange(NFFT)[None, :] % NFFT) * (2.0 * math.pi / NFFT)
    weight = np.where((row == 0) | (row == HALF), 1.0, 2.0)[:, None] / NFFT
    values = np.where((row <= HALF)[:, None], np.cos(angles), -np.sin(angles)) * weight
    return (values * window_values()[None, :]).astype(jnp.bfloat16)


def swap(x, axis, d):
    return lax.ppermute(x, axis, [(i, i ^ d) for i in range(lax.axis_size(axis))])


def poly(z, coefficients):
    p = coefficients[-1]
    for c in coefficients[-2::-1]:
        p = p * z + c
    return p


def gelu_parts(x):
    u = jnp.clip(x, -5.2, 5.2)
    z = u * u
    p = poly(z, [jnp.asarray(c, x.dtype) for c in GELU])
    half = jnp.asarray(0.5, x.dtype)
    cumulative = half * jnp.tanh(u * p) + half
    density = jnp.exp2(z * jnp.asarray(-0.5 * math.log2(math.e), x.dtype))
    return x * cumulative, cumulative + (x * jnp.asarray(1.0 / math.sqrt(2.0 * math.pi), x.dtype)) * density


def norm_parts(values):
    centred = values - jnp.mean(values, axis=1, keepdims=True)
    inv_std = lax.rsqrt(jnp.mean(centred * centred, axis=1, keepdims=True) + norm_eps)
    return centred * inv_std, inv_std


def norm_back(normed_grad, unit, inv_std, gain):
    unit_grad = normed_grad * gain
    inner = jnp.mean(unit_grad * unit, axis=1, keepdims=True)
    return inv_std * (unit_grad - jnp.mean(unit_grad, axis=1, keepdims=True) - unit * inner)


def total_rows(x):
    return jnp.sum(x, axis=0, keepdims=True)


def row(ref, i):
    return ref[i : i + 1]


def turns(x):
    r = x * (1.0 / (2.0 * math.pi))
    r = r - jnp.floor(r + 0.5)
    z = r * r
    return poly(z, COS), r * poly(z, SIN)


class Frames:
    def __init__(self, rows, lengths_ref):
        self.rows = rows
        self.ext = rows + 2 * HALO
        self.own = slice(HALO, HALO + rows)
        self.start = lax.axis_index("seq") * rows - HALO
        self.total = rows * lax.axis_size("seq")
        self.length = lengths_ref[pl.program_id(0), 0]
        self.tiles = [(0, HALO)] + [(r, 32) for r in range(HALO, HALO + rows, 32)] + [(HALO + rows, HALO)]
        self.half = self.ext // 2

    def at(self, r=0, n=None):
        return lax.broadcasted_iota(jnp.int32, (n or self.ext, 1), 0) + (self.start + r)

    def inside(self, r=0, n=None):
        t = self.at(r, n)
        return (t >= 0) & (t < self.total)

    def mask(self, r=0, n=None):
        t = self.at(r, n)
        return (t >= 0) & (t < self.total) & (t < self.length)

    def owns(self, r):
        return HALO <= r < HALO + self.rows

    def parts(self):
        return [(r0, range(r0, r0 + self.half, 16)) for r0 in (0, self.half)]


def feature_tile(frames, before_ref, features_ref, after_ref, r, n):
    width = features_ref.shape[2]
    if r < HALO:
        tile = before_ref[0, r : r + n, :width]
    elif r < HALO + frames.rows:
        tile = features_ref[0, r - HALO : r - HALO + n]
    else:
        tile = after_ref[0, r - HALO - frames.rows : r - HALO - frames.rows + n, :width]
    return jnp.where(frames.mask(r, n), tile.astype(f32), 0.0)


def fold(x):
    total = x[0:8]
    for r in range(8, x.shape[0], 8):
        total = total + x[r : r + 8]
    return total


def add_to(ref, i, x):
    ref[8 * i : 8 * i + 8] += fold(x)


def assemble(even_ref, odd_ref, size, whole_ref, sems):
    me = lax.axis_index("dp")
    copies = []
    for h in range(even_ref.shape[0]):
        for c, ref in enumerate((even_ref, odd_ref)):
            at = pl.multiple_of((me ^ (2 * h + c)) * size, size)
            copies.append(
                pltpu.make_async_copy(ref.at[h, pl.ds(0, size)], whole_ref.at[pl.ds(at, size)], sems.at[2 * h + c])
            )
    return copies


def run_copies(copies):
    for copy in copies:
        copy.start()
    for copy in copies:
        copy.wait()


def skipping(kernel, start, count):
    def inner(*refs):
        return kernel(*refs[:start], *refs[start + count :])

    return inner if count else kernel


def in_hbm(x):
    return pltpu.with_memory_space_constraint(x, pltpu.HBM)


def cost(us):
    return pl.CostEstimate(flops=1000 + int(us * 1e9), bytes_accessed=1000, transcendentals=0)


def call(kernel, grid, lengths, ins, outs, scratch, name, after=(), limit=48, us=0):
    def spec(shape, kind):
        if isinstance(kind, pl.BlockSpec):
            return kind
        if kind == "any":
            return pl.BlockSpec(memory_space=pl.ANY)
        if kind == "rows":
            return pl.BlockSpec((1,) + tuple(shape[1:]), lambda i, s: (i,) + (0,) * (len(shape) - 1))
        return pl.BlockSpec(tuple(shape), lambda i, s: (0,) * len(shape))

    kernel = skipping(kernel, 1 + len(ins), len(after))
    ins = ins + [(a, "any") for a in after]
    return pl.pallas_call(
        kernel,
        out_shape=[(pltpu.HBM if kind == "rows" else jax.ShapeDtypeStruct)(tuple(s), d) for s, d, kind in outs],
        grid_spec=pltpu.PrefetchScalarGridSpec(
            num_scalar_prefetch=1,
            grid=(grid,),
            in_specs=[spec(a.shape, kind) for a, kind in ins],
            out_specs=[spec(s, kind) for s, _, kind in outs],
            scratch_shapes=scratch,
        ),
        compiler_params=pltpu.CompilerParams(vmem_limit_bytes=limit * MiB, dimension_semantics=("arbitrary",)),
        cost_estimate=cost(us),
        name=name,
    )(lengths, *[in_hbm(a) if kind == "rows" and a.shape[1] != HALO else a for a, kind in ins])


def simple_call(kernel, ins, outs, name, scratch=(), after=(), limit=16, us=0):
    whole = pl.BlockSpec(memory_space=pltpu.VMEM)
    return pl.pallas_call(
        skipping(kernel, len(ins), len(after)),
        out_shape=[jax.ShapeDtypeStruct(tuple(s), d) for s, d in outs],
        in_specs=[whole] * len(ins) + [pl.BlockSpec(memory_space=pl.ANY)] * len(after),
        out_specs=[whole] * len(outs),
        scratch_shapes=list(scratch),
        compiler_params=pltpu.CompilerParams(vmem_limit_bytes=limit * MiB),
        cost_estimate=cost(us),
        name=name,
    )(*ins, *after)


def head_columns(x):
    lane = lax.broadcasted_iota(jnp.int32, (x.shape[0], EXTRA), 1)
    tail = jnp.where(lane == 0, x[:, BINS - 1 : BINS], jnp.where(lane == 1, x[:, 2 * BINS - 1 :], 0.0))
    return x[:, : BINS - 1], x[:, BINS : 2 * BINS - 1], tail


def pack_kernel(
    first_ref, last_ref, gfirst_ref, glast_ref, dw_ref, gains_ref, biases_ref, upb_ref, hgain_ref, hshift_ref,
    head_ref, up_ref, down_ref, first_out, last_out, up0_out, rest_out,
):
    width = first_ref.shape[2]
    first_out[:, :, :width] = first_ref[...]
    first_out[:, :, width:] = gfirst_ref[...].astype(low)
    last_out[:, :, :width] = last_ref[...]
    last_out[:, :, width:] = glast_ref[...].astype(low)
    own = up_ref.shape[1]
    up0_out[0:own] = up_ref[0]
    up0_out[own:] = jnp.zeros((16, up_ref.shape[2]), low)

    def stack(parts):
        parts = [p.astype(f32) for p in parts]
        filled = sum(p.shape[0] for p in parts)
        return jnp.concatenate(parts + [jnp.zeros((16 - filled, parts[0].shape[1]), f32)], axis=0).astype(low)

    def halves(x):
        high = x.astype(low).astype(f32)
        return [high, x - high]

    up0_out[own:, 0:own] = stack([dw_ref[:, 0, :], dw_ref[:, 1, :]])
    up0_out[own:, 128 : 128 + own] = stack(
        [gains_ref[0], gains_ref[1], biases_ref[:, 0, :], biases_ref[:, 1, :]] + halves(hgain_ref[...]) + halves(hshift_ref[...])
    )
    up0_out[own:, 256 : 256 + upb_ref.shape[1]] = stack([upb_ref[...]])
    size = down_ref.shape[1]
    base = up_ref.shape[2] // HALF * own
    for g in range(0, up_ref.shape[2], HALF):
        rest_out[g // HALF * own : (g // HALF + 1) * own] = up_ref[1, :, g : g + HALF]
    rest_out[base : base + size] = down_ref[1]
    size = base + size

    magnitude, phase, tail = head_columns(head_ref[...])
    rest_out[size : size + own] = magnitude.astype(low)
    rest_out[size + own : size + 2 * own] = phase.astype(low)
    rest_out[size + 2 * own :] = jnp.zeros((own, HALF), low)
    rest_out[size + 2 * own :, :EXTRA] = tail.astype(low)


def dft_kernel(rows, lengths, before_ref, grad_ref, after_ref, squared_ref, table_ref, out_ref, recip_ref):
    frames = Frames(rows, lengths)
    width = before_ref.shape[2] - HOP

    @pl.when(pl.program_id(0) == 0)
    def _():
        envelope = jnp.zeros((frames.ext, HOP), f32)
        for q in range(4):
            source = frames.at() + (2 - q)
            valid = (source >= 0) & (source < frames.total)
            envelope = envelope + jnp.where(valid, row(squared_ref, q), 0.0)
        recip_ref[...] = jnp.where(frames.inside(), 1.0 / envelope, 0.0)

    whole = jnp.concatenate(
        [before_ref[0, :, width:].astype(f32), grad_ref[0], after_ref[0, :, width:].astype(f32)], axis=0
    )
    own = jnp.where(frames.mask(), whole * recip_ref[...], 0.0)
    parts = [own if q == 2 else pltpu.roll(own, (2 - q) % frames.ext, 0) for q in range(4)]
    framed = jnp.where(frames.inside(), jnp.concatenate(parts, axis=1), 0.0).astype(low)
    out_ref[0] = lax.dot_general(framed, table_ref[...], cols_dims, preferred_element_type=f32).astype(low)


def put_padded(pad_ref, frames, tile_of):
    zeros = jnp.zeros((8, pad_ref.shape[1]), f32)
    pad_ref[0:8] = zeros
    pad_ref[frames.ext + 8 :] = zeros
    for r, n in frames.tiles:
        pad_ref[8 + r : 8 + r + n] = tile_of(r, n)


def conv_tile(pad_ref, r, n, taps_ref, base, bias):
    window = pad_ref[r : r + n + 16]
    conv = bias + row(taps_ref, base + 3) * window[8 : 8 + n]
    for k in range(KERNEL):
        if k != 3:
            conv = conv + row(taps_ref, base + k) * pltpu.roll(window, (3 - k) % (n + 16), 0)[8 : 8 + n]
    return conv


def conv_norm(frames, pad_ref, taps_ref, base, vec_ref, b, unit_at, inv_at, normed_at):
    for r, n in frames.tiles:
        unit, inv_std = norm_parts(conv_tile(pad_ref, r, n, taps_ref, base, bias_row(vec_ref, b, 0)))
        unit_at[r : r + n] = unit.astype(unit_at.dtype)
        inv_at[r : r + n] = inv_std
        normed_at[r : r + n] = (unit * gain_row(vec_ref, b, 0) + bias_row(vec_ref, b, 1)).astype(low)


def gain_row(ref, b, i):
    return row(ref, 2 * b + i)


def bias_row(ref, b, i):
    return row(ref, 4 + 3 * b + i)


def conv_kernel(
    rows, own, units, lengths, before_ref, features_ref, after_ref, hbias_ref, even_ref, odd_ref,
    normed_ref, unit_ref, inv_ref, taps_ref, vec_ref, upb_ref, bias_ref, small_ref, pad_ref, sems,
):
    @pl.when(pl.program_id(0) == 0)
    def _():
        me = lax.axis_index("dp")
        count = 2 * even_ref.shape[0]
        copies = []
        for d in range(count):
            ref = odd_ref if d % 2 else even_ref
            copies.append(
                pltpu.make_async_copy(ref.at[d // 2, pl.ds(own, 16), pl.ds(0, small_ref.shape[2])], small_ref.at[d], sems.at[d])
            )
        run_copies(copies)

        def spread(lanes, size, out_ref):
            total = jnp.zeros(out_ref.shape, f32)
            at = lax.broadcasted_iota(jnp.int32, (size, out_ref.shape[1]), 0)
            to = lax.broadcasted_iota(jnp.int32, (size, out_ref.shape[1]), 1)
            for d in range(count):
                place = jnp.where(to == at + (me ^ d) * size, 1.0, 0.0).astype(low)
                total = total + jnp.dot(small_ref[d, :, lanes : lanes + size], place, preferred_element_type=f32)
            out_ref[...] = total

        spread(0, own, taps_ref)
        spread(128, own, vec_ref)
        spread(256, units // count, upb_ref)
        magnitude, phase, tail = head_columns(hbias_ref[...])
        bias_ref[:, :HALF] = magnitude
        bias_ref[:, HALF : 2 * HALF] = phase
        bias_ref[:, 2 * HALF :] = tail

    frames = Frames(rows, lengths)
    put_padded(pad_ref, frames, functools.partial(feature_tile, frames, before_ref, features_ref, after_ref))
    conv_norm(frames, pad_ref, taps_ref, 0, vec_ref, 0, unit_ref.at[0], inv_ref.at[0], normed_ref.at[0])


def up_gelu(frames, normed_at, weight_ref, bias, act_at, slope_at, chunk=256):
    for r0, _ in frames.parts():
        normed = normed_at[r0 : r0 + frames.half]
        for c in range(0, weight_ref.shape[1], chunk):
            pre = jnp.dot(normed, weight_ref[:, c : c + chunk], preferred_element_type=f32) + bias[:, c : c + chunk]
            act, slope = gelu_parts(pre.astype(low))
            act_at[r0 : r0 + frames.half, c : c + chunk] = act
            slope_at[r0 : r0 + frames.half, c : c + chunk] = slope


def forward_kernel(
    rows, own, size, lengths, before_ref, features_ref, after_ref, normed_ref, vec_ref, upb_ref,
    ueven_ref, uodd_ref, deven_ref, dodd_ref, hidden_ref, act_ref, slope_ref, branch_ref, up_ref, down_ref, sems, sems2,
):
    @pl.when(pl.program_id(0) == 0)
    def _():
        run_copies(assemble(ueven_ref, uodd_ref, own, up_ref, sems) + assemble(deven_ref, dodd_ref, size, down_ref, sems2))

    frames = Frames(rows, lengths)
    act_at = act_ref.at[0]
    up_gelu(frames, normed_ref.at[0], up_ref, row(upb_ref, 0), act_at, slope_ref.at[0])
    for r0, tiles in frames.parts():
        product = jnp.dot(act_at[r0 : r0 + frames.half], down_ref[...], preferred_element_type=f32)
        for r in tiles:
            branch = product[r - r0 : r - r0 + 16] + bias_row(vec_ref, 0, 2)
            branch_ref[0, r : r + 16] = branch.astype(low)
            h = feature_tile(frames, before_ref, features_ref, after_ref, r, 16)
            hidden_ref[0, r : r + 16] = h + gain_row(vec_ref, 0, 1) * branch


def split_rows(total_at, size, keep_at, send_at, pieces):
    me = lax.axis_index("dp")
    for h in range(pieces):
        at = pl.multiple_of((me ^ (2 * h)) * size, size)
        keep_at(h, total_at(pl.ds(at, size)).astype(low))
        at = pl.multiple_of((me ^ (2 * h + 1)) * size, size)
        send_at(h, total_at(pl.ds(at, size)).astype(low))


def give(ref, base):
    def put(h, value):
        ref[h, base : base + value.shape[0], : value.shape[1]] = value

    return put


def split_columns(total_ref, base, size, keep_ref, send_ref):
    for g in range(0, total_ref.shape[1], HALF):
        stop = min(g + HALF, total_ref.shape[1])
        at = base + g // HALF * size
        split_rows(lambda r: total_ref[r, g:stop], size, give(keep_ref, at), give(send_ref, at), keep_ref.shape[0])


def branch_tile(frames, r, hgrad, branch, gain, bgrad_at, sums_ref, at):
    bgrad = (gain * hgrad).astype(low)
    bgrad_at[r : r + 16] = bgrad
    if frames.owns(r):
        add_to(sums_ref, at, hgrad * branch.astype(f32))
        add_to(sums_ref, at + 1, bgrad.astype(f32))


def back_down(frames, bgrad_at, act_at, slope_at, weight_ref, total_ref, pgrad_at, bsums_ref, chunk=512):
    own = frames.own
    for c in range(0, weight_ref.shape[0], chunk):
        part = slice(c, c + chunk)
        for r0, tiles in frames.parts():
            act_grad = lax.dot_general(bgrad_at[r0 : r0 + frames.half], weight_ref[part], cols_dims, preferred_element_type=f32)
            for r in tiles:
                grad = (act_grad[r - r0 : r - r0 + 16] * slope_at[r : r + 16, part].astype(f32)).astype(low)
                pgrad_at[r : r + 16, part] = grad
                if frames.owns(r):
                    bsums_ref[:, part] += fold(grad.astype(f32))
        total_ref[part] += lax.dot_general(act_at[own, part], bgrad_at[own], rows_dims, preferred_element_type=f32)


def back_up_norm(frames, pgrad_at, unit_at, inv_at, gain, weight_ref, pad_ref, sums_ref):
    zeros = jnp.zeros((8, pad_ref.shape[1]), f32)
    pad_ref[0:8] = zeros
    pad_ref[frames.ext + 8 :] = zeros
    for r0, tiles in frames.parts():
        product = lax.dot_general(pgrad_at[r0 : r0 + frames.half], weight_ref[...], cols_dims, preferred_element_type=f32)
        for r in tiles:
            normed_grad = product[r - r0 : r - r0 + 16]
            unit = unit_at[r : r + 16].astype(f32)
            conv_grad = norm_back(normed_grad, unit, inv_at[r : r + 16], gain)
            if frames.owns(r):
                conv_grad = conv_grad.astype(low).astype(f32)
                add_to(sums_ref, 7, conv_grad)
                add_to(sums_ref, 8, normed_grad * unit)
                add_to(sums_ref, 9, normed_grad)
            else:
                conv_grad = jnp.where(frames.inside(r, 16), conv_grad, 0.0).astype(low).astype(f32)
            pad_ref[8 + r : 8 + r + 16] = conv_grad


def conv_back_tile(frames, r, n, pad_ref, block_in_of, hgrad, taps_ref, base, sums_ref):
    window = pad_ref[r : r + n + 16]
    owns = frames.owns(r)
    block_in = block_in_of(r, n) if owns else None
    for k in range(KERNEL):
        moved = (window if k == 3 else pltpu.roll(window, (k - 3) % (n + 16), 0))[8 : 8 + n]
        hgrad = hgrad + row(taps_ref, base + k) * moved
        if owns:
            add_to(sums_ref, k, block_in * moved)
    return hgrad


def close_sums(sums_ref, small_ref):
    for i in range(sums_ref.shape[0] // 8):
        small_ref[i : i + 1] = total_rows(sums_ref[8 * i : 8 * i + 8])


def middle_kernel(
    rows, own, size, lengths, h_ref, tgrad_ref, recip_ref, taps_ref, vec_ref, upb_ref, bias_ref,
    table_hbm, rest_ref,
    audio_ref, hgrad_ref, keep_ref, send_ref, small_ref, sbias_ref,
    table_ref, up_ref, down_ref, head_ref, head_total, up_total, down_total, act_ref, slope_ref,
    pad_ref, cpad_ref, frame_ref, unit1_ref, unit2_ref, inv1_ref, inv2_ref, normed1_ref, normed2_ref, turned_ref,
    branch_ref, bgrad_ref, spectrum_ref, lgrad_ref, sums_ref, bsums_ref, hsums_ref, sems,
):
    step = pl.program_id(0)

    @pl.when(step == 0)
    def _():
        copies = []
        groups = up_ref.shape[1] // HALF
        places = [(g * own, own, up_ref, g * HALF, HALF) for g in range(groups)]
        places.append((groups * own, size, down_ref, 0, HALF))
        base = groups * own + size
        places += [(base + g * own, own, head_ref, g * HALF, lanes) for g, lanes in enumerate((HALF, HALF, EXTRA))]
        for j in range(rest_ref.shape[0]):
            for i, (at, many, ref, lane, lanes) in enumerate(places):
                copies.append(
                    pltpu.make_async_copy(
                        rest_ref.at[j, pl.ds(at, many), pl.ds(0, lanes)],
                        ref.at[pl.ds(j * many, many), pl.ds(lane, lanes)],
                        sems.at[j, i],
                    )
                )
        copies.append(pltpu.make_async_copy(table_hbm, table_ref, sems.at[0, len(places)]))
        for copy in copies:
            copy.start()
        for ref in (head_total, up_total, down_total, sums_ref, bsums_ref, hsums_ref):
            ref[...] = jnp.zeros_like(ref)
        for copy in copies:
            copy.wait()

    frames = Frames(rows, lengths)
    mine, half, ext = frames.own, frames.half, frames.ext

    def block_in_tile(r, n):
        return jnp.where(frames.inside(r, n), h_ref[0, r : r + n], 0.0).astype(low).astype(f32)

    put_padded(pad_ref, frames, block_in_tile)
    conv_norm(frames, pad_ref, taps_ref, KERNEL, vec_ref, 1, unit1_ref, inv1_ref, normed1_ref)
    up_gelu(frames, normed1_ref, up_ref, row(upb_ref, 1), act_ref, slope_ref)

    head_gain = row(vec_ref, 10) + row(vec_ref, 11)
    head_shift = row(vec_ref, 12) + row(vec_ref, 13)
    for r0, tiles in frames.parts():
        product = jnp.dot(act_ref[r0 : r0 + half], down_ref[...], preferred_element_type=f32)
        for r in tiles:
            branch = product[r - r0 : r - r0 + 16] + bias_row(vec_ref, 1, 2)
            branch_ref[r : r + 16] = branch.astype(low)
            unit, inv_std = norm_parts(h_ref[0, r : r + 16] + gain_row(vec_ref, 1, 1) * branch)
            unit2_ref[r : r + 16] = unit
            inv2_ref[r : r + 16] = inv_std
            normed2_ref[r : r + 16] = (unit * head_gain + head_shift).astype(low)

    lane = lax.broadcasted_iota(jnp.int32, (16, EXTRA), 1)
    for r0, tiles in frames.parts():
        product = jnp.dot(normed2_ref[r0 : r0 + half], head_ref[...], preferred_element_type=f32)
        for r in tiles:
            logits = product[r - r0 : r - r0 + 16] + bias_ref[...]
            magnitude = jnp.exp(logits[:, :HALF])
            cos, sin = turns(logits[:, HALF : 2 * HALF])
            re = magnitude * cos
            im = magnitude * sin
            last = logits[:, 2 * HALF :]
            cos, sin = turns(pltpu.roll(last, EXTRA - 1, 1))
            top = jnp.exp(jnp.where(lane == 0, last, 0.0))
            top_re = top * cos
            top_im = top * sin
            spectrum_ref[r : r + 16, :HALF] = re.astype(low)
            spectrum_ref[r : r + 16, HALF : HALF + EXTRA] = jnp.where(lane == 0, top_re, im[:, :EXTRA]).astype(low)
            spectrum_ref[r : r + 16, HALF + EXTRA :] = im[:, EXTRA:].astype(low)
            tgrad = tgrad_ref[0, r : r + 16].astype(f32)
            re_grad = tgrad[:, :HALF]
            top_grad = tgrad[:, HALF : HALF + EXTRA]
            im_grad = jnp.concatenate([jnp.where(lane == 0, 0.0, top_grad), tgrad[:, HALF + EXTRA :]], axis=1)
            log_last = jnp.where(lane == 0, top_grad * top_re, 0.0)
            phase_last = jnp.where(lane == 1, pltpu.roll(top_grad * top_im, 1, 1), 0.0)
            grads = (re_grad * re + im_grad * im, im_grad * re - re_grad * im, log_last - phase_last)
            for g, grad in enumerate(grads):
                part = slice(g * HALF, g * HALF + grad.shape[1])
                lgrad_ref[r : r + 16, part] = grad.astype(low)
                if frames.owns(r):
                    hsums_ref[:, part] += fold(grad)

    for r0, tiles in frames.parts():
        product = jnp.dot(spectrum_ref[r0 : r0 + half], table_ref[...], preferred_element_type=f32)
        for r in tiles:
            framed = product[r - r0 : r - r0 + 16]
            if not frames.owns(r):
                framed = jnp.where(frames.inside(r, 16), framed, 0.0)
            frame_ref[8 + r : 8 + r + 16] = framed

    hgrad_at = hgrad_ref.at[0]
    for r0, tiles in frames.parts():
        product = lax.dot_general(lgrad_ref[r0 : r0 + half], head_ref[...], cols_dims, preferred_element_type=f32)
        for r in tiles:
            normed_grad = product[r - r0 : r - r0 + 16]
            unit = unit2_ref[r : r + 16]
            hgrad = norm_back(normed_grad, unit, inv2_ref[r : r + 16], head_gain)
            hgrad_at[r : r + 16] = hgrad
            if frames.owns(r):
                add_to(sums_ref, 12, normed_grad * unit)
                add_to(sums_ref, 13, normed_grad)
            branch_tile(frames, r, hgrad, branch_ref[r : r + 16], gain_row(vec_ref, 1, 1), bgrad_ref, sums_ref, 10)

    def audio_tile(r, n):
        audio = frame_ref[8 + r : 8 + r + n, 2 * HOP : 3 * HOP]
        for q in (0, 1, 3):
            window = frame_ref[r : r + n + 16, q * HOP : (q + 1) * HOP]
            audio = audio + pltpu.roll(window, (q - 2) % (n + 16), 0)[8 : 8 + n]
        audio_ref[0, r - HALO : r - HALO + n] = jnp.where(frames.mask(r, n), audio * recip_ref[r : r + n], 0.0)

    def beside(chunks, tiles, dot_of, put, work):
        each = -(-len(tiles) // len(chunks))
        for i, part in enumerate(chunks):
            product = dot_of(part)
            for r, n in tiles[i * each : (i + 1) * each]:
                work(r, n)
            put(part, product)

    own_tiles = [tile for tile in frames.tiles if frames.owns(tile[0])]
    turned_ref[...] = normed2_ref[mine].T

    def put_head(part, product):
        head_total[:, part] += product

    beside(
        [slice(c, c + 384) for c in range(0, head_total.shape[1], 384)],
        own_tiles,
        lambda part: jnp.dot(turned_ref[...], lgrad_ref[mine, part], preferred_element_type=f32),
        put_head,
        audio_tile,
    )

    back_down(frames, bgrad_ref, act_ref, slope_ref, down_ref, down_total, slope_ref, bsums_ref)
    back_up_norm(frames, slope_ref, unit1_ref, inv1_ref, gain_row(vec_ref, 1, 0), up_ref, cpad_ref, sums_ref)
    turned_ref[...] = normed1_ref[mine].T

    def put_up(part, product):
        up_total[:, part] += product

    def conv_back(r, n):
        hgrad_at[r : r + n] = conv_back_tile(
            frames, r, n, cpad_ref, lambda r, n: pad_ref[8 + r : 8 + r + n], hgrad_at[r : r + n], taps_ref, KERNEL, sums_ref
        )

    beside(
        [slice(c, c + 256) for c in range(0, up_total.shape[1], 256)],
        frames.tiles,
        lambda part: jnp.dot(turned_ref[...], slope_ref[mine, part], preferred_element_type=f32),
        put_up,
        conv_back,
    )

    @pl.when(step == pl.num_programs(0) - 1)
    def _():
        close_sums(sums_ref, small_ref)
        sbias_ref[...] = total_rows(bsums_ref[...])
        groups = up_ref.shape[1] // HALF * own
        split_columns(up_total, 0, own, keep_ref, send_ref)
        split_columns(down_total, groups, size, keep_ref, send_ref)
        base = groups + size
        bias = total_rows(hsums_ref[...])
        block = jnp.concatenate([bias[:, g : g + 384] for g in (0, 384, 768)] + [jnp.zeros((13, 384), f32)], axis=0)
        for h in range(keep_ref.shape[0]):
            for ref in (keep_ref, send_ref):
                ref[h, base + 2 * own :] = jnp.zeros((own, HALF), low)
                ref[h, base + 2 * own : base + 2 * own + 16, EXTRA:] = block.astype(low)
        split_columns(head_total, base, own, keep_ref, send_ref)


def back_down_kernel(
    rows, own, size, lengths, hgrad_ref, branch_ref, act_ref, slope_ref, normed_ref, vec_ref, even_ref, odd_ref,
    pgrad_ref, keep_ref, send_ref, small_ref, sbias_ref, weight_ref, down_total, up_total, bgrad_ref, sums_ref, bsums_ref, sems,
):
    step = pl.program_id(0)

    @pl.when(step == 0)
    def _():
        copies = assemble(even_ref, odd_ref, size, weight_ref, sems)
        for copy in copies:
            copy.start()
        for ref in (down_total, up_total, sums_ref, bsums_ref):
            ref[...] = jnp.zeros_like(ref)
        for copy in copies:
            copy.wait()

    frames = Frames(rows, lengths)
    mine = frames.own
    for r in range(0, frames.ext, 16):
        branch_tile(frames, r, hgrad_ref[0, r : r + 16], branch_ref[0, r : r + 16], gain_row(vec_ref, 0, 1), bgrad_ref, sums_ref, 0)
    back_down(frames, bgrad_ref, act_ref.at[0], slope_ref.at[0], weight_ref, down_total, pgrad_ref.at[0], bsums_ref)
    up_total[...] += lax.dot_general(normed_ref[0, mine], pgrad_ref[0, mine], rows_dims, preferred_element_type=f32)

    @pl.when(step == pl.num_programs(0) - 1)
    def _():
        close_sums(sums_ref, small_ref)
        sbias_ref[...] = total_rows(bsums_ref[...])
        split_columns(up_total, 0, own, keep_ref, send_ref)
        split_columns(down_total, up_total.shape[1] // HALF * own, size, keep_ref, send_ref)


def back_up_kernel(
    rows, own, lengths, pgrad_ref, unit_ref, inv_ref, features_ref, hgrad_ref, taps_ref, vec_ref, even_ref, odd_ref,
    out_ref, small_ref, weight_ref, pad_ref, sums_ref, sems,
):
    step = pl.program_id(0)

    @pl.when(step == 0)
    def _():
        sums_ref[...] = jnp.zeros_like(sums_ref)
        run_copies(assemble(even_ref, odd_ref, own, weight_ref, sems))

    frames = Frames(rows, lengths)
    back_up_norm(
        frames, pgrad_ref.at[0], unit_ref.at[0], inv_ref.at[0], gain_row(vec_ref, 0, 0), weight_ref, pad_ref, sums_ref
    )

    def block_in_tile(r, n):
        return jnp.where(frames.mask(r, n), features_ref[0, r - HALO : r - HALO + n].astype(f32), 0.0)

    for r, n in frames.tiles:
        if frames.owns(r):
            hgrad = conv_back_tile(frames, r, n, pad_ref, block_in_tile, hgrad_ref[0, r : r + n], taps_ref, 0, sums_ref)
            out_ref[0, r - HALO : r - HALO + n] = jnp.where(frames.mask(r, n), hgrad, 0.0)

    @pl.when(step == pl.num_programs(0) - 1)
    def _():
        close_sums(sums_ref, small_ref)


def small_kernel(conv0_ref, down0_ref, bias0_ref, mid_ref, bias1_ref, out_ref):
    width = out_ref.shape[1]
    groups = [r[:, g : g + width] for r in (bias0_ref, bias1_ref) for g in range(0, r.shape[1], width)]
    rows = [
        conv0_ref[0:7], mid_ref[0:7],
        conv0_ref[8:9], down0_ref[0:1], mid_ref[8:9], mid_ref[10:11],
        conv0_ref[7:8], conv0_ref[9:10], down0_ref[1:2], mid_ref[7:8], mid_ref[9:10], mid_ref[11:12],
        mid_ref[12:14],
    ] + groups
    filled = 26 + len(groups)
    rows = rows + [jnp.zeros((out_ref.shape[0] - filled, width), f32)] * (filled < out_ref.shape[0])
    out_ref[...] = jnp.concatenate(rows, axis=0).astype(low)


def gather_kernel(pieces, at, *refs):
    for h in range(pieces):
        refs[-1 if len(refs) == pieces + 1 else pieces + 1][h] = refs[h][...]
    if len(refs) > pieces + 1:
        refs[-1][...] = refs[pieces][at]


def final_kernel(
    own, size, parts, late_ref, *refs,
):
    part_refs = refs[:parts]
    up_ref, down_ref, head_ref, hbias_ref, dw_ref, gains_ref, biases_ref, upb_ref, hgain_ref, hshift_ref, rows_ref = refs[parts:]
    total = 0.0
    for d, ref in enumerate(part_refs):
        cut = ref.shape[0] - SMALL
        total = total + ref[cut:].astype(f32)
        at = 0 if parts == 1 else pl.multiple_of((lax.axis_index("seq") ^ d) * cut, cut)
        rows_ref[pl.ds(at, cut), :] = ref[0:cut].astype(f32)
    groups = up_ref.shape[2] // HALF
    base = groups * own + size
    late = late_ref[...].astype(f32)
    for g in range(groups):
        up_ref[0, :, g * HALF : (g + 1) * HALF] = rows_ref[g * own : (g + 1) * own]
        up_ref[1, :, g * HALF : (g + 1) * HALF] = late[g * own : (g + 1) * own]
    down_ref[0] = rows_ref[groups * own : base]
    down_ref[1] = late[groups * own : base]

    def joined(magnitude, phase, tail):
        return jnp.concatenate([magnitude, tail[:, 0:1], phase, tail[:, 1:2]], axis=1)

    tail = late[base + 2 * own :]
    head_ref[...] = joined(late[base : base + own], late[base + own : base + 2 * own], tail)
    bias = jnp.concatenate([tail[g : g + 1, EXTRA:] for g in range(3)], axis=1)
    hbias_ref[...] = joined(bias[:, :HALF], bias[:, HALF : 2 * HALF], bias[:, 2 * HALF :])

    width = total.shape[1]
    me = lax.axis_index("dp")

    def pick(values, count, base):
        at = lax.broadcasted_iota(jnp.int32, (width, count), 0)
        to = lax.broadcasted_iota(jnp.int32, (width, count), 1)
        place = jnp.where(at + base == to + me * count, 1.0, 0.0).astype(low)
        high = values.astype(low)
        rest = (values - high.astype(f32)).astype(low)
        return jnp.dot(high, place, preferred_element_type=f32) + jnp.dot(rest, place, preferred_element_type=f32)

    rows = pick(total[0:32], own, 0)
    for b in range(BLOCKS):
        dw_ref[:, b, :] = rows[KERNEL * b : KERNEL * (b + 1)]
        gains_ref[b] = rows[14 + 2 * b : 16 + 2 * b]
        biases_ref[:, b, :] = rows[18 + 3 * b : 21 + 3 * b]
    hgain_ref[...] = rows[24:25]
    hshift_ref[...] = rows[25:26]
    biases = jnp.zeros((2, size), f32)
    for g in range(groups):
        picked = [pick(total[26 + b * groups + g : 27 + b * groups + g], size, g * width) for b in range(BLOCKS)]
        biases = biases + jnp.concatenate(picked, axis=0)
    upb_ref[...] = biases


def pair_kernel(keep_ref, recv_ref, kept_ref, *sent_refs):
    kept_ref[...] = keep_ref[0].astype(f32) + recv_ref[0].astype(f32)
    for h, ref in enumerate(sent_refs):
        ref[...] = (keep_ref[h + 1].astype(f32) + recv_ref[h + 1].astype(f32)).astype(low)


def cross_kernel(count, kept_ref, *refs):
    recvs, outs, total_ref = refs[: len(refs) - count - 1], refs[len(refs) - count - 1 : -1], refs[-1]
    total = kept_ref[...]
    for ref in recvs:
        total = total + ref[...].astype(f32)
    total_ref[...] = total
    cut = kept_ref.shape[0] // count
    for d, ref in enumerate(outs):
        at = pl.multiple_of((lax.axis_index("seq") ^ d) * cut, cut)
        ref[...] = total_ref[pl.ds(at, cut), :].astype(ref.dtype)


def over_seq_kernel(*refs):
    small_ref, out_ref = refs[-2:]
    total = refs[0][...].astype(f32)
    for ref in refs[1:-2]:
        total = total + ref[...].astype(f32)
    cut = total.shape[0]
    out_ref[0:cut] = total.astype(low)
    small = small_ref[0].astype(f32)
    for i in range(1, small_ref.shape[0]):
        small = small + small_ref[i].astype(f32)
    out_ref[cut:] = small.astype(low)


def sum_kernel(*refs):
    total = refs[0][...].astype(f32)
    for ref in refs[1:-1]:
        total = total + ref[...].astype(f32)
    refs[-1][...] = total.astype(refs[-1].dtype)


def add_all(arrays, kind, name, after=(), us=0):
    return simple_call(sum_kernel, arrays, [(arrays[0].shape, kind)], name, after=after, us=us)[0]


def pair_stage(keep, recv, name, after=()):
    piece = keep.shape[1:]
    kept, *sent = simple_call(
        pair_kernel, [keep, recv], [(piece, f32)] + [(piece, low)] * (keep.shape[0] - 1), name, after=after
    )
    return kept, [swap(x, "dp", 2 * (h + 1)) for h, x in enumerate(sent)]


def summed_over(x, axis):
    bit = 1
    while bit < lax.axis_size(axis):
        x = x + swap(x, axis, bit)
        bit *= 2
    return x


def per_device(
    features,
    lengths,
    dw_weight,
    block_gains,
    block_biases,
    up_weight,
    up_bias,
    down_weight,
    head_gain,
    head_shift,
    head_weight,
    head_bias,
    audio_grad,
):
    count = lax.axis_size("dp")
    pairs = count // 2
    micro = features.shape[0]
    rows = features.shape[2]
    width = features.shape[3]
    units = up_weight.shape[2]
    ext = rows + 2 * HALO
    own = width // count
    size = units // count
    seq_count = lax.axis_size("seq")
    features = features[:, 0]
    audio_grad = audio_grad[:, 0]
    columns = 2 * HALF + EXTRA
    run = functools.partial(call, grid=micro, lengths=lengths)

    def edge(columns, at):
        return pl.BlockSpec((micro, HALO, columns), lambda i: (0, at, 0))

    last_at = rows // HALO - 1
    packed_ins = [
        dw_weight.swapaxes(0, 1),
        block_gains,
        block_biases.swapaxes(0, 1),
        up_bias,
        head_gain[None],
        head_shift[None],
        head_weight,
        up_weight,
        down_weight,
    ]
    packed_outs = [
        (micro, HALO, width + HOP),
        (micro, HALO, width + HOP),
        (own + 16, units),
        (units // HALF * own + size + 3 * own, HALF),
    ]

    def whole_block(dims):
        return pl.BlockSpec(tuple(dims), lambda i: (0,) * len(dims))

    first, last, up0_piece, rest_piece = pl.pallas_call(
        pack_kernel,
        grid=(1,),
        in_specs=[edge(width, 0), edge(width, last_at), edge(HOP, 0), edge(HOP, last_at)]
        + [whole_block(a.shape) for a in packed_ins],
        out_specs=[whole_block(dims) for dims in packed_outs],
        out_shape=[jax.ShapeDtypeStruct(dims, low) for dims in packed_outs],
        compiler_params=pltpu.CompilerParams(vmem_limit_bytes=60 * MiB),
        cost_estimate=cost(0),
        name="pack",
    )(features, features, audio_grad, audio_grad, *packed_ins)
    before = lax.ppermute(last, "seq", [(i, i + 1) for i in range(seq_count - 1)])
    after = lax.ppermute(first, "seq", [(i + 1, i) for i in range(seq_count - 1)])
    rest = lax.all_gather(rest_piece, "dp", axis=0)
    squared = jnp.asarray((window_values() ** 2).reshape(4, HOP), f32)
    tables = jnp.asarray(head_tables())

    def shape(columns):
        return (micro, ext, columns)

    def dma(*size):
        return pltpu.SemaphoreType.DMA(size or (count,))

    def across(x):
        return [x] + [swap(x, "dp", d) for d in range(2, count, 2)]

    def stacked(pieces, name, after, following=None):
        piece = pieces[0].shape
        ins = pieces + ([] if following is None else [following[0]])
        outs = [((pairs,) + piece, low)] + ([] if following is None else [(following[0].shape[1:], low)])
        if following is None:
            (even,) = simple_call(functools.partial(gather_kernel, pairs, 0), ins, outs, name, after=after)
            return (even, swap(even, "dp", 1)), None
        even, piece = simple_call(functools.partial(gather_kernel, pairs, following[1]), ins, outs, name, after=after)
        return (even, swap(even, "dp", 1)), piece

    up0_pieces = across(up0_piece)
    table_grad, recip = run(
        functools.partial(dft_kernel, rows),
        ins=[(before, "rows"), (audio_grad, "rows"), (after, "rows"), (squared, "all"), (tables, "all")],
        outs=[(shape(NFFT), low, "rows"), ((ext, HOP), f32, "all")],
        scratch=[],
        us=20,
        name="dft",
    )
    up0, down0_piece = stacked(up0_pieces, "stack_up0", [recip], (down_weight, 0))
    down0_pieces = across(down0_piece)
    normed, unit, inv_std, taps, vec, upb, bias_row_all = run(
        functools.partial(conv_kernel, rows, own, units),
        ins=[(before, "rows"), (features, "rows"), (after, "rows"), (head_bias[None], "all"), (up0[0], "any"), (up0[1], "any")],
        outs=[
            (shape(width), low, "rows"),
            (shape(width), low, "rows"),
            (shape(1), f32, "rows"),
            ((16, width), f32, "all"),
            ((16, width), f32, "all"),
            ((16, units), f32, "all"),
            ((1, columns), f32, "all"),
        ],
        scratch=[pltpu.VMEM((count, 16, 512), low), pltpu.VMEM((ext + 16, width), f32), dma()],
        name="conv",
    )
    down0, _ = stacked(down0_pieces, "stack_down0", [taps])
    hidden, act, slope, branch = run(
        functools.partial(forward_kernel, rows, own, size),
        ins=[
            (before, "rows"),
            (features, "rows"),
            (after, "rows"),
            (normed, "rows"),
            (vec, "all"),
            (upb, "all"),
            (up0[0], "any"),
            (up0[1], "any"),
            (down0[0], "any"),
            (down0[1], "any"),
        ],
        outs=[(shape(width), f32, "rows"), (shape(units), low, "rows"), (shape(units), low, "rows"), (shape(width), low, "rows")],
        scratch=[pltpu.VMEM((width, units), low), pltpu.VMEM((units, width), low), dma(), dma()],
        name="forward",
    )
    grouped = units // HALF * own
    packed = 3 * own + size + grouped
    audio, incoming, keep1, send1, small_mid, sbias1 = run(
        functools.partial(middle_kernel, rows, own, size),
        ins=[
            (hidden, "rows"),
            (table_grad, "rows"),
            (recip, "all"),
            (taps, "all"),
            (vec, "all"),
            (upb, "all"),
            (bias_row_all, "all"),
            (tables, "any"),
            (rest, "any"),
        ],
        outs=[
            ((micro, rows, HOP), f32, "rows"),
            (shape(width), f32, "rows"),
            ((pairs, packed, HALF), low, "all"),
            ((pairs, packed, HALF), low, "all"),
            ((16, width), f32, "all"),
            ((1, units), f32, "all"),
        ],
        scratch=[
            pltpu.VMEM((NFFT, NFFT), low),
            pltpu.VMEM((width, units), low),
            pltpu.VMEM((units, width), low),
            pltpu.VMEM((width, columns), low),
            pltpu.VMEM((width, columns), f32),
            pltpu.VMEM((width, units), f32),
            pltpu.VMEM((units, width), f32),
            pltpu.VMEM((ext, units), low),
            pltpu.VMEM((ext, units), low),
            pltpu.VMEM((ext + 16, width), f32),
            pltpu.VMEM((ext + 16, width), f32),
            pltpu.VMEM((ext + 16, NFFT), f32),
            pltpu.VMEM((ext, width), f32),
            pltpu.VMEM((ext, width), f32),
            pltpu.VMEM((ext, 1), f32),
            pltpu.VMEM((ext, 1), f32),
            pltpu.VMEM((ext, width), low),
            pltpu.VMEM((ext, width), low),
            pltpu.VMEM((width, rows), low),
            pltpu.VMEM((ext, width), low),
            pltpu.VMEM((ext, width), low),
            pltpu.VMEM((ext, NFFT), low),
            pltpu.VMEM((ext, columns), low),
            pltpu.VMEM((128, width), f32),
            pltpu.VMEM((8, units), f32),
            pltpu.VMEM((8, columns), f32),
            dma(count, 5 + units // HALF),
        ],
        name="middle",
        limit=56,
    )
    kept1, recvs1 = pair_stage(keep1, swap(send1, "dp", 1), "late_pair")
    pre_grad, keep, send, small_down, sbias0 = run(
        functools.partial(back_down_kernel, rows, own, size),
        ins=[
            (incoming, "rows"),
            (branch, "rows"),
            (act, "rows"),
            (slope, "rows"),
            (normed, "rows"),
            (vec, "all"),
            (down0[0], "any"),
            (down0[1], "any"),
        ],
        outs=[
            (shape(units), low, "rows"),
            ((pairs, grouped + size, width), low, "all"),
            ((pairs, grouped + size, width), low, "all"),
            ((8, width), f32, "all"),
            ((1, units), f32, "all"),
        ],
        scratch=[
            pltpu.VMEM((units, width), low),
            pltpu.VMEM((units, width), f32),
            pltpu.VMEM((width, units), f32),
            pltpu.VMEM((ext, width), low),
            pltpu.VMEM((64, width), f32),
            pltpu.VMEM((8, units), f32),
            dma(),
        ],
        after=[kept1],
        us=20,
        name="back_down",
    )
    shard1 = add_all([kept1] + recvs1, low, "late_cross", after=[sbias0], us=200)
    late = lax.psum(shard1, "seq")
    kept, recvs = pair_stage(keep, swap(send, "dp", 1), "pair", after=[shard1])
    feature_grad, small_conv = run(
        functools.partial(back_up_kernel, rows, own),
        ins=[
            (pre_grad, "rows"),
            (unit, "rows"),
            (inv_std, "rows"),
            (features, "rows"),
            (incoming, "rows"),
            (taps, "all"),
            (vec, "all"),
            (up0[0], "any"),
            (up0[1], "any"),
        ],
        outs=[((micro, rows, width), f32, "rows"), ((16, width), f32, "all")],
        scratch=[pltpu.VMEM((width, units), low), pltpu.VMEM((ext + 16, width), f32), pltpu.VMEM((128, width), f32), dma()],
        after=[kept],
        name="back_up",
    )
    (smalls,) = simple_call(
        small_kernel, [small_conv, small_down, sbias0, small_mid, sbias1], [((SMALL, width), low)], "small"
    )
    cut = kept.shape[0] // seq_count
    small_all = lax.all_gather(smalls, "dp", axis=0)
    if cut % 16:
        own_sum = add_all([kept] + recvs, f32, "cross", after=[smalls])
        sent = own_sum.astype(low)
        whole = add_all([own_sum] + [swap(sent, "seq", d) for d in range(1, seq_count)], low, "over_seq")
        small = jnp.sum(small_all.astype(f32), axis=0).astype(low)
        small = add_all([small] + [swap(small, "seq", d) for d in range(1, seq_count)], low, "small_seq")
        parts = [jnp.concatenate([whole, small], axis=0)]
    else:
        pieces = simple_call(
            functools.partial(cross_kernel, seq_count),
            [kept] + recvs,
            [((cut, width), f32)] + [((cut, width), low)] * (seq_count - 1),
            "cross",
            scratch=[pltpu.VMEM(kept.shape, f32)],
            after=[smalls],
        )
        part = simple_call(
            over_seq_kernel,
            [pieces[0]] + [swap(pieces[d], "seq", d) for d in range(1, seq_count)] + [small_all],
            [((cut + SMALL, width), low)],
            "over_seq",
        )[0]
        parts = [part] + [swap(part, "seq", d) for d in range(1, seq_count)]
    outs = simple_call(
        functools.partial(final_kernel, own, size, len(parts)),
        [late] + parts,
        [
            ((BLOCKS, own, units), f32),
            ((BLOCKS, size, width), f32),
            ((own, 2 * BINS), f32),
            ((1, 2 * BINS), f32),
            ((KERNEL, BLOCKS, own), f32),
            ((BLOCKS, 2, own), f32),
            ((3, BLOCKS, own), f32),
            ((BLOCKS, size), f32),
            ((1, own), f32),
            ((1, own), f32),
        ],
        "final",
        scratch=[pltpu.VMEM(kept.shape, f32)],
    )
    up_grad, down_grad, head_grad, bias_grad, dw_grad, gains_grad, biases_grad, up_bias_grad, hgain_grad, hshift_grad = outs
    return (
        audio[:, None],
        feature_grad[:, None],
        dw_grad.swapaxes(0, 1),
        gains_grad,
        biases_grad.swapaxes(0, 1),
        up_grad,
        up_bias_grad,
        down_grad,
        hgain_grad[0],
        hshift_grad[0],
        head_grad,
        bias_grad[0],
    )


def solution(mesh):
    return jax.shard_map(
        per_device,
        mesh=mesh,
        in_specs=(
            P(None, "dp", "seq", None),
            P(None, "dp"),
            P(None, None, "dp"),
            P(None, None, "dp"),
            P(None, None, "dp"),
            P(None, "dp", None),
            P(None, "dp"),
            P(None, "dp", None),
            P("dp"),
            P("dp"),
            P("dp", None),
            P(),
            P(None, "dp", "seq", None),
        ),
        out_specs=(
            P(None, "dp", "seq", None),
            P(None, "dp", "seq", None),
            P(None, None, "dp"),
            P(None, None, "dp"),
            P(None, None, "dp"),
            P(None, "dp", None),
            P(None, "dp"),
            P(None, "dp", None),
            P("dp"),
            P("dp"),
            P("dp", None),
            P(),
        ),
        check_vma=False,
    )
```

time: 1170 us -> 257 us (0.22)
  matrix products: 474 us -> 0 us
  waiting for transfers between devices: 203 us -> 27.3 us
  Pallas kernels: 0 us -> 154 us
  other arithmetic: 111 us -> 0.62 us
  blocking collectives: 114 us -> 9.15 us
  starting transfers between devices: 139 us -> 39.7 us
  local copies, waits for them, and re-layouts: 102 us -> 10.7 us
    dot_general x76 -> x0, matrix products: 474 us -> none  [the longest x4 72.6 us: head_forward(): jnp.dot(imag_part, sin_table, precision=exact_mode, preferred_element_typ...]
    pallas_call x0 -> x16, Pallas kernels: none -> 154 us  [the longest x6 143 us: call(): pl.pallas_call(kernel, out_shape=[(pltpu.HBM if kind == 'rows' else jax.S...]
    unnamed x15 -> x2, waiting for transfers between devices: 140 us -> 0.03 us
    ppermute x48 -> x24, starting transfers between devices: 138 us -> 39.6 us  [the longest x22 33.4 us: swap(): lax.ppermute(x, axis, [(i, i ^ d) for i in range(lax.axis_size(axis))])]
    convert_element_type x48 -> x0, other arithmetic: 54.9 us -> none  [the longest x1 24.3 us: block_forward(): conv_taps[k].astype(jnp.float32) * padded_wide[k:k + rows_here]]
    psum x2 -> x0, blocking collectives: 51.1 us -> none  [the longest x1 39 us: per_device(): bias_grad = lax.psum(bias_total, ('dp', 'seq'))]
    slice x36 -> x0, local copies, waits for them, and re-layouts: 51 us -> none  [the longest x2 29.8 us: convnext_block_reverse(): conv_taps[k] * grad_padded[start:start + rows_here]]
    unnamed x639 -> x67, local copies, waits for them, and re-layouts: 48.2 us -> 10.7 us
  transfers between devices with their start and end apart: 59 -> 26, of which waited for: 12 -> 10; matrix products, arithmetic and copies ran while one was open for 49% -> 0% of each run, Pallas kernels for 0% -> 31%
where the time goes in v2:
time: 257 us; the launch traced here: 256 us
  Pallas kernels  154 us (60%)
  starting transfers between devices  39.7 us (15%)
  waiting for transfers between devices  27.3 us (11%)
  between operations  14.4 us (6%)
  local copies, waits for them, and re-layouts  10.7 us (4%)
  blocking collectives  9.15 us (4%)
    pallas_call x6, Pallas kernels, call(): pl.pallas_call(kernel, out_shape=[(pltpu.HBM if kind == 'rows' else jax.S...  143 us
    ppermute x22, starting transfers between devices, swap(): lax.ppermute(x, axis, [(i, i ^ d) for i in range(lax.axis_size(axis))])  33.4 us
    ppermute x22, waiting for transfers between devices, swap(): lax.ppermute(x, axis, [(i, i ^ d) for i in range(lax.axis_size(axis))])  25.5 us
    unnamed x67, local copies, waits for them, and re-layouts  10.7 us
    all_gather x1, blocking collectives, per_device(): small_all = lax.all_gather(smalls, 'dp', axis=0)  9.15 us
    pallas_call x9, Pallas kernels, simple_call(): pl.pallas_call(skipping(kernel, len(ins), len(after)), out_shape=[jax.Sha...  8.42 us
  transfers between devices with their start and end apart: 26, of which 10 were waited for; matrix products, arithmetic and copies ran while one was open for 0% of the time, Pallas kernels for 31%

profile of v2, /device:TPU:0, one launch (start us, length us, event | category | flops | bytes accessed | tf_op | source)
XLA Modules:
  0.0 256.1 jit_solution(18186127922387264448)
XLA Ops:
  7.2 0.0 all-gather.4.cloned.1.call-start
  7.3 2.5 pack.1
  9.8 0.0 all-gather.4.cloned.1.call-update
  9.8 4.9 %collective-permute-start = (bf16[4,16,768]{2,1,0:T(8,128)(2,1)}, bf16[4,16,768]{2,1,0:T(8,128)(2,1)S(1)}, u32[]{:S(2)}, u32[]{:S(2)}) collective-permute-start(bf16[4,16,768]{2,1,0:T(8,128)(2,1)} %get-tuple-element.66), channel_id=1, source_target_pairs={{0,1},{1,2},{2,3},{4,5},{5,6},{6,7},{8,9},{9,10},{10,11},{12,13},{... | collective-permute-start | bytes 294920 | tf_op jit(solution)/shard_map/ppermute | solution.py:904
  14.8 1.3 collective-permute-start.1
  16.1 2.5 collective-permute-start.4
  18.6 0.5 collective-permute-start.3
  19.1 0.5 collective-permute-start.2
  19.6 0.1 copy.30.lengths.refs_0_
  19.7 1.8 collective-permute-done.1.after_ref
  21.5 8.6 %dft.1 = (bf16[4,544,1024]{2,1,0:T(8,128)(2,1)}, f32[544,256]{1,0:T(8,128)S(1)}) custom-call(s32[4,1]{1,0:T(4,128)S(1)} %copy.30.lengths.refs_0_, bf16[4,16,768]{2,1,0:T(8,128)(2,1)S(1)} %collective-permute-done.before_ref, f32[4,512,256]{2,1,0:T(8,128)} %bitcast.26, bf16[4,16,768]{2,1,0:T(8,128)(2,1)S(1)} %collective-permute-done.1.after_ref, ...), custom_call_target="tpu_custom_call" | custom-call | flops 20000000000 | bytes 1000 | tf_op jit(solution)/shard_map/dft/pallas_call | solution.py:190
  30.1 4.9 %collective-permute-done.3.refs_2_ = bf16[80,1536]{1,0:T(8,128)(2,1)} collective-permute-done((bf16[80,1536]{1,0:T(8,128)(2,1)}, bf16[80,1536]{1,0:T(8,128)(2,1)}, u32[]{:S(2)}, u32[]{:S(2)}) %collective-permute-start.3) | collective-permute-done | bytes 245792 | tf_op jit(solution)/shard_map/ppermute | solution.py:46
  35.1 1.4 collective-permute-done.2.refs_1_
  36.4 1.1 stack_up0.1
  37.6 0.1 collective-permute-start.5
  37.7 1.5 collective-permute-start.8
  39.2 1.5 collective-permute-start.7
  40.7 0.5 collective-permute-start.6
  41.3 10.7 %conv.1 = (bf16[4,544,512]{2,1,0:T(8,128)(2,1)}, bf16[4,544,512]{2,1,0:T(8,128)(2,1)}, f32[4,544,1]{2,1,0:T(8,128)}, f32[16,512]{1,0:T(8,128)S(1)}, f32[16,512]{...) custom-call(s32[4,1]{1,0:T(4,128)S(1)} %copy.30.lengths.refs_0_, ...), custom_call_target="tpu_custom_call" | custom-call | flops 1000 | bytes 1000 | tf_op jit(solution)/shard_map/conv/pallas_call | solution.py:190
  52.0 0.6 copy-done.27
  52.6 1.7 collective-permute-done.7.refs_2_
  54.3 0.1 stack_down0.1.deven_ref.refs_7_
  54.4 0.1 collective-permute-start.9
  54.4 2.3 collective-permute-done.9.dodd_ref.refs_8_
  56.7 0.9 copy-done.13
  57.6 18.6 %forward.1 = (f32[4,544,512]{2,1,0:T(8,128)}, bf16[4,544,1536]{2,1,0:T(8,128)(2,1)}, bf16[4,544,1536]{2,1,0:T(8,128)(2,1)}, bf16[4,544,512]{2,1,0:T(8,128)(2,1)}) custom-call(s32[4,1]{1,0:T(4,128)S(1)} %copy.30.lengths.refs_0_, bf16[4,16,768]{2,1,0:T(8,128)(2,1)S(1)} %collective-permute-done.before_ref, bf16[4,512,512]{2,1,0:T(8,128)(2,1)} %bitcast.22, ...), custom_call_target="tpu_custom_call" | custom-call | flops 1000 | bytes 1000 | tf_op jit(solution)/shard_map/forward/pallas_call | solution.py:190
  76.3 0.0 all-gather.4.cloned.1.call-done
  76.3 66.9 %middle.1 = (f32[4,512,256]{2,1,0:T(8,128)}, f32[4,544,512]{2,1,0:T(8,128)}, bf16[4,576,512]{2,1,0:T(8,128)(2,1)}, bf16[4,576,512]{2,1,0:T(8,128)(2,1)}, f32[16,512]{1,0:T(8,128)}, /*index=5*/f32[1,1536]{1,0:T(1,128)}) custom-call(s32[4,1]{1,0:T(4,128)} %copy-done.20, f32[4,544,512]{2,1,0:T(8,128)} %get-tuple-element.76.h_ref, ...), custom_call_target="tpu_custom_call" | custom-call | flops 1000 | bytes 1000 | tf_op jit(solution)/shard_map/middle/pallas_call | solution.py:190
  143.2 0.2 collective-permute-start.10
  143.4 4.6 %collective-permute-done.10.recv_ref = bf16[4,576,512]{2,1,0:T(8,128)(2,1)S(1)} collective-permute-done((bf16[4,576,512]{2,1,0:T(8,128)(2,1)}, bf16[4,576,512]{2,1,0:T(8,128)(2,1)S(1)}, u32[]{:S(2)}, u32[]{:S(2)}) %collective-permute-start.10) | collective-permute-done | bytes 2359328 | tf_op jit(solution)/shard_map/ppermute | solution.py:46
  148.0 1.7 copy-done.4
  149.7 0.5 late_pair.1
  150.2 1.9 collective-permute-start.12
  152.1 1.3 collective-permute-start.13
  153.4 0.4 collective-permute-start.14
  153.8 19.9 %back_down.1 = (bf16[4,544,1536]{2,1,0:T(8,128)(2,1)}, bf16[4,384,512]{2,1,0:T(8,128)(2,1)S(1)}, bf16[4,384,512]{2,1,0:T(8,128)(2,1)}, f32[8,512]{1,0:T(8,128)S(1)}, f32[1,1536]{1,0:T(1,128)S(1)}) custom-call(s32[4,1]{1,0:T(4,128)S(1)} %copy-done.21, f32[4,544,512]{2,1,0:T(8,128)} %get-tuple-element.81.refs_1_.refs_5_, ...), custom_call_target="tpu_custom_call" | custom-call | flops 20000000000 | bytes 1000 | tf_op jit(solution)/shard_map/back_down/pallas_call | solution.py:190
  173.7 1.2 copy-done.8
  174.8 0.6 copy-done.24
  175.4 4.4 %collective-permute-done.13.refs_2_ = bf16[576,512]{1,0:T(8,128)(2,1)S(1)} collective-permute-done((bf16[576,512]{1,0:T(8,128)(2,1)S(1)}, bf16[576,512]{1,0:T(8,128)(2,1)S(1)}, u32[]{:S(2)}, u32[]{:S(2)}) %collective-permute-start.13) | collective-permute-done | bytes 589856 | tf_op jit(solution)/shard_map/ppermute | solution.py:46
  179.8 1.1 late_cross.1.refs_2_
  181.0 1.5 copy-done.9
  182.5 2.3 pair.1
  184.9 0.8 copy-done.28
  185.6 0.7 copy-done.29
  186.4 1.0 collective-permute-start.15
  187.4 0.7 collective-permute-start.16
  188.1 1.8 collective-permute-start.17
  189.9 0.7 copy-done.16
  190.7 0.8 copy-done.18
  191.4 18.5 %back_up.1 = (f32[4,512,512]{2,1,0:T(8,128)}, f32[16,512]{1,0:T(8,128)S(1)}) custom-call(s32[4,1]{1,0:T(4,128)S(1)} %copy-done.22, bf16[4,544,1536]{2,1,0:T(8,128)(2,1)} %get-tuple-element.88.refs_1_, bf16[4,544,512]{2,1,0:T(8,128)(2,1)} %get-tuple-element.89.refs_2_, f32[4,544,1]{2,1,0:T(8,128)} %get-tuple-element.90.refs_3_, ...), custom_call_target="tpu_custom_call" | custom-call | flops 1000 | bytes 1000 | tf_op jit(solution)/shard_map/back_up/pallas_call | solution.py:190
  210.1 1.3 cross.1
  211.4 3.1 %collective-permute-start.18 = (bf16[96,512]{1,0:T(8,128)(2,1)S(1)}, bf16[96,512]{1,0:T(8,128)(2,1)S(1)}, u32[]{:S(2)}, u32[]{:S(2)}) collective-permute-start(bf16[96,512]{1,0:T(8,128)(2,1)S(1)} %get-tuple-element.107), channel_id=1, source_target_pairs={{0,1},{1,0},{2,3},{3,2},{4,5},{5,4},{6,7},{7,6},{8,9},{9,8},{10,11... | collective-permute-start | bytes 294920 | tf_op jit(solution)/shard_map/ppermute | solution.py:46
  214.5 2.9 %collective-permute-start.19 = (bf16[96,512]{1,0:T(8,128)(2,1)S(1)}, bf16[96,512]{1,0:T(8,128)(2,1)S(1)}, u32[]{:S(2)}, u32[]{:S(2)}) collective-permute-start(bf16[96,512]{1,0:T(8,128)(2,1)S(1)} %get-tuple-element.108), channel_id=1, source_target_pairs={{0,2},{1,3},{2,0},{3,1},{4,6},{5,7},{6,4},{7,5},{8,10},{9,11},{10,... | collective-permute-start | bytes 294920 | tf_op jit(solution)/shard_map/ppermute | solution.py:46
  217.4 9.2 %all-gather.1 = bf16[256,512]{1,0:T(8,128)(2,1)S(1)} all-gather(bf16[32,512]{1,0:T(8,128)(2,1)S(1)} %small.1.refs_4_), channel_id=3, replica_groups=mesh['dp'=8,'seq'=4] {'dp'}, dimensions={0}, use_global_device_ids=true | all-gather | bytes 294912 | tf_op jit(solution)/shard_map/all_gather | solution.py:1087
  226.6 0.9 collective-permute-done.19.refs_2_
  227.5 0.1 over_seq.1.refs_0_
  227.6 3.0 %collective-permute-start.23 = (bf16[128,512]{1,0:T(8,128)(2,1)S(1)}, bf16[128,512]{1,0:T(8,128)(2,1)S(1)}, u32[]{:S(2)}, u32[]{:S(2)}) collective-permute-start(bf16[128,512]{1,0:T(8,128)(2,1)S(1)} %over_seq.1.refs_0_), channel_id=1, source_target_pairs={{0,3},{1,2},{2,1},{3,0},{4,7},{5,6},{6,5},{7,4},{8,11},{9,10},{10,... | collective-permute-start | bytes 393224 | tf_op jit(solution)/shard_map/ppermute | solution.py:46
  230.6 9.4 %collective-permute-start.22 = (bf16[128,512]{1,0:T(8,128)(2,1)S(1)}, bf16[128,512]{1,0:T(8,128)(2,1)S(1)}, u32[]{:S(2)}, u32[]{:S(2)}) collective-permute-start(bf16[128,512]{1,0:T(8,128)(2,1)S(1)} %over_seq.1.refs_0_), channel_id=1, source_target_pairs={{0,2},{1,3},{2,0},{3,1},{4,6},{5,7},{6,4},{7,5},{8,10},{9,11},{10,... | collective-permute-start | bytes 393224 | tf_op jit(solution)/shard_map/ppermute | solution.py:46
  240.0 0.5 collective-permute-start.21
  240.5 3.9 %collective-permute-done.22.refs_2_ = bf16[128,512]{1,0:T(8,128)(2,1)S(1)} collective-permute-done((bf16[128,512]{1,0:T(8,128)(2,1)S(1)}, bf16[128,512]{1,0:T(8,128)(2,1)S(1)}, u32[]{:S(2)}, u32[]{:S(2)}) %collective-permute-start.22) | collective-permute-done | bytes 131104 | tf_op jit(solution)/shard_map/ppermute | solution.py:46
  244.4 1.3 collective-permute-done.21.refs_1_
  245.7 1.1 copy-done.10
  246.8 1.9 final.1
  248.6 0.6 reduce
  (76 shorter events, 0.2 us)
Async XLA Ops:
  7.2 69.1 %all-gather.4.cloned.1.call-start = ((), (), s32[]{:S(2)}) async-start(), calls=%async_computation.1 | async-start | bytes 5308416 | tf_op jit(solution)/shard_map/all_gather | solution.py:906
  7.2 12.4 %copy-start.32 = (s32[4,1]{0,1:T(1,128)S(1)}, s32[4,1]{0,1:T(1,128)}, u32[]{:S(2)}) copy-start(s32[4,1]{0,1:T(1,128)} %param.16) | copy-start | bytes 52
  7.2 14.2 %copy-start.6 = (bf16[1024,1024]{1,0:T(8,128)(2,1)S(1)}, bf16[1024,1024]{1,0:T(8,128)(2,1)}, u32[]{:S(2)}) copy-start(bf16[1024,1024]{1,0:T(8,128)(2,1)} %constant.5.clone.table_ref.table_hbm) | copy-start | bytes 6291460
  7.2 14.2 %copy-start.30 = (f32[4,256]{1,0:T(4,128)S(1)}, f32[4,256]{1,0:T(4,128)}, u32[]{:S(2)}) copy-start(f32[4,256]{1,0:T(4,128)} %constant.4.clone.squared_ref) | copy-start | bytes 12292
  9.8 9.9 %collective-permute-start = (bf16[4,16,768]{2,1,0:T(8,128)(2,1)}, bf16[4,16,768]{2,1,0:T(8,128)(2,1)S(1)}, u32[]{:S(2)}, u32[]{:S(2)}) collective-permute-start(bf16[4,16,768]{2,1,0:T(8,128)(2,1)} %get-tuple-element.66), channel_id=1, source_target_pairs={{0,1},{1,2},{2,3},{4,5},{5,6},{6,7},{8,9},{9,10},{10,11},{12,13},{... | collective-permute-start | bytes 294920 | tf_op jit(solution)/shard_map/ppermute | solution.py:904
  14.8 6.7 %collective-permute-start.1 = (bf16[4,16,768]{2,1,0:T(8,128)(2,1)}, bf16[4,16,768]{2,1,0:T(8,128)(2,1)S(1)}, u32[]{:S(2)}, u32[]{:S(2)}) collective-permute-start(bf16[4,16,768]{2,1,0:T(8,128)(2,1)} %get-tuple-element.67), channel_id=1, source_target_pairs={{1,0},{2,1},{3,2},{5,4},{6,5},{7,6},{9,8},{10,9},{11,10},{13,12},{... | collective-permute-start | bytes 294920 | tf_op jit(solution)/shard_map/ppermute | solution.py:905
  16.1 14.1 %collective-permute-start.4 = (bf16[80,1536]{1,0:T(8,128)(2,1)}, bf16[80,1536]{1,0:T(8,128)(2,1)S(1)}, u32[]{:S(2)}, u32[]{:S(2)}) collective-permute-start(bf16[80,1536]{1,0:T(8,128)(2,1)} %get-tuple-element.68.refs_0_), channel_id=1, source_target_pairs={{0,24},{4,28},{8,16},{12,20},{16,8},{20,12},{24,0},{28,4},{1,25},{... | collective-permute-start | bytes 737288 | tf_op jit(solution)/shard_map/ppermute | solution.py:46
  18.6 16.5 %collective-permute-start.3 = (bf16[80,1536]{1,0:T(8,128)(2,1)}, bf16[80,1536]{1,0:T(8,128)(2,1)}, u32[]{:S(2)}, u32[]{:S(2)}) collective-permute-start(bf16[80,1536]{1,0:T(8,128)(2,1)} %get-tuple-element.68.refs_0_), channel_id=1, source_target_pairs={{0,16},{4,20},{8,24},{12,28},{16,0},{20,4},{24,8},{28,12},{1,17},{... | collective-permute-start | bytes 737288 | tf_op jit(solution)/shard_map/ppermute | solution.py:46
  19.1 17.4 %collective-permute-start.2 = (bf16[80,1536]{1,0:T(8,128)(2,1)}, bf16[80,1536]{1,0:T(8,128)(2,1)}, u32[]{:S(2)}, u32[]{:S(2)}) collective-permute-start(bf16[80,1536]{1,0:T(8,128)(2,1)} %get-tuple-element.68.refs_0_), channel_id=1, source_target_pairs={{0,8},{4,12},{8,0},{12,4},{16,24},{20,28},{24,16},{28,20},{1,9},{5... | collective-permute-start | bytes 737288 | tf_op jit(solution)/shard_map/ppermute | solution.py:46
  19.7 37.0 %copy-start.20 = (s32[4,1]{1,0:T(4,128)}, s32[4,1]{1,0:T(4,128)S(1)}, u32[]{:S(2)}) copy-start(s32[4,1]{1,0:T(4,128)S(1)} %copy.30.lengths.refs_0_) | copy-start | bytes 52
  19.7 16.7 %copy-start.7 = (bf16[2,192,512]{2,1,0:T(8,128)(2,1)S(1)}, bf16[2,192,512]{2,1,0:T(8,128)(2,1)}, u32[]{:S(2)}) copy-start(bf16[2,192,512]{2,1,0:T(8,128)(2,1)} %refs_4_.1) | copy-start | bytes 1179652
  19.7 16.7 %copy-start.19 = (bf16[80,1536]{1,0:T(8,128)(2,1)S(1)}, bf16[80,1536]{1,0:T(8,128)(2,1)}, u32[]{:S(2)}) copy-start(bf16[80,1536]{1,0:T(8,128)(2,1)} %get-tuple-element.68.refs_0_) | copy-start | bytes 737284
  19.7 21.5 %copy-start.31 = (f32[1026]{0:T(1024)S(1)}, f32[1026]{0:T(1024)}, u32[]{:S(2)}) copy-start(f32[1026]{0:T(1024)} %param.26) | copy-start | bytes 12316
  21.5 19.8 %copy-start.12 = (bf16[4,16,768]{2,1,0:T(8,128)(2,1)}, bf16[4,16,768]{2,1,0:T(8,128)(2,1)S(1)}, u32[]{:S(2)}) copy-start(bf16[4,16,768]{2,1,0:T(8,128)(2,1)S(1)} %collective-permute-done.1.after_ref) | copy-start | bytes 294916
  30.1 21.8 %copy-start.5 = (f32[544,256]{1,0:T(8,128)}, f32[544,256]{1,0:T(8,128)S(1)}, u32[]{:S(2)}) copy-start(f32[544,256]{1,0:T(8,128)S(1)} %get-tuple-element.69.refs_5_.recip_ref) | copy-start | bytes 1671172
  37.6 19.1 %copy-start = (bf16[4,80,1536]{2,1,0:T(8,128)(2,1)}, bf16[4,80,1536]{2,1,0:T(8,128)(2,1)S(1)}, u32[]{:S(2)}) copy-start(bf16[4,80,1536]{2,1,0:T(8,128)(2,1)S(1)} %get-tuple-element.70.even_ref.ueven_ref.refs_8_) | copy-start | bytes 2949124
  37.6 3.6 %collective-permute-start.5 = (bf16[4,80,1536]{2,1,0:T(8,128)(2,1)S(1)}, bf16[4,80,1536]{2,1,0:T(8,128)(2,1)S(1)}, u32[]{:S(2)}, u32[]{:S(2)}) collective-permute-start(bf16[4,80,1536]{2,1,0:T(8,128)(2,1)S(1)} %get-tuple-element.70.even_ref.ueven_ref.refs_8_), channel_id=1, source_target_pairs={{0,4},{4,0},{8,12},{12,8},{16,20},{20,16},{24,28},{28,24},{1,5},{5... | collective-permute-start | bytes 2949128 | tf_op jit(solution)/shard_map/ppermute | solution.py:46
  37.7 14.9 %collective-permute-start.8 = (bf16[192,512]{1,0:T(8,128)(2,1)S(1)}, bf16[192,512]{1,0:T(8,128)(2,1)S(1)}, u32[]{:S(2)}, u32[]{:S(2)}) collective-permute-start(bf16[192,512]{1,0:T(8,128)(2,1)S(1)} %get-tuple-element.74.refs_0_), channel_id=1, source_target_pairs={{0,24},{4,28},{8,16},{12,20},{16,8},{20,12},{24,0},{28,4},{1,25},{... | collective-permute-start | bytes 589832 | tf_op jit(solution)/shard_map/ppermute | solution.py:46
  39.2 15.1 %collective-permute-start.7 = (bf16[192,512]{1,0:T(8,128)(2,1)S(1)}, bf16[192,512]{1,0:T(8,128)(2,1)S(1)}, u32[]{:S(2)}, u32[]{:S(2)}) collective-permute-start(bf16[192,512]{1,0:T(8,128)(2,1)S(1)} %get-tuple-element.74.refs_0_), channel_id=1, source_target_pairs={{0,16},{4,20},{8,24},{12,28},{16,0},{20,4},{24,8},{28,12},{1,17},{... | collective-permute-start | bytes 589832 | tf_op jit(solution)/shard_map/ppermute | solution.py:46
  40.7 13.6 %collective-permute-start.6 = (bf16[192,512]{1,0:T(8,128)(2,1)S(1)}, bf16[192,512]{1,0:T(8,128)(2,1)S(1)}, u32[]{:S(2)}, u32[]{:S(2)}) collective-permute-start(bf16[192,512]{1,0:T(8,128)(2,1)S(1)} %get-tuple-element.74.refs_0_), channel_id=1, source_target_pairs={{0,8},{4,12},{8,0},{12,4},{16,24},{20,28},{24,16},{28,20},{1,9},{5... | collective-permute-start | bytes 589832 | tf_op jit(solution)/shard_map/ppermute | solution.py:46
  41.3 15.5 %copy-start.2 = (bf16[4,80,1536]{2,1,0:T(8,128)(2,1)}, bf16[4,80,1536]{2,1,0:T(8,128)(2,1)S(1)}, u32[]{:S(2)}) copy-start(bf16[4,80,1536]{2,1,0:T(8,128)(2,1)S(1)} %collective-permute-done.5.odd_ref.uodd_ref.refs_9_) | copy-start | bytes 2949124
  52.0 0.6 copy-start.27
  52.6 23.7 %copy-start.11 = (f32[16,1536]{1,0:T(8,128)}, f32[16,1536]{1,0:T(8,128)S(1)}, u32[]{:S(2)}) copy-start(f32[16,1536]{1,0:T(8,128)S(1)} %get-tuple-element.73.upb_ref) | copy-start | bytes 294916
  52.6 23.7 %copy-start.14 = (f32[16,512]{1,0:T(8,128)}, f32[16,512]{1,0:T(8,128)S(1)}, u32[]{:S(2)}) copy-start(f32[16,512]{1,0:T(8,128)S(1)} %get-tuple-element.72.vec_ref.refs_6_.refs_7_) | copy-start | bytes 98308
  52.6 23.7 %copy-start.17 = (f32[16,512]{1,0:T(8,128)}, f32[16,512]{1,0:T(8,128)S(1)}, u32[]{:S(2)}) copy-start(f32[16,512]{1,0:T(8,128)S(1)} %get-tuple-element.75.refs_4_.taps_ref.refs_6_) | copy-start | bytes 98308
  54.4 2.4 collective-permute-start.9
  56.7 0.9 copy-start.13
  143.2 4.8 %collective-permute-start.10 = (bf16[4,576,512]{2,1,0:T(8,128)(2,1)}, bf16[4,576,512]{2,1,0:T(8,128)(2,1)S(1)}, u32[]{:S(2)}, u32[]{:S(2)}) collective-permute-start(bf16[4,576,512]{2,1,0:T(8,128)(2,1)} %get-tuple-element.86), channel_id=1, source_target_pairs={{0,4},{4,0},{8,12},{12,8},{16,20},{20,16},{24,28},{28,24},{1,5},{5... | collective-permute-start | bytes 7077896 | tf_op jit(solution)/shard_map/ppermute | solution.py:46
  148.0 1.7 copy-start.4
  149.7 4.1 %copy-start.15 = (f32[16,512]{1,0:T(8,128)S(1)}, f32[16,512]{1,0:T(8,128)}, u32[]{:S(2)}) copy-start(f32[16,512]{1,0:T(8,128)} %copy-done.14) | copy-start | bytes 98308
  149.7 4.1 %copy-start.21 = (s32[4,1]{1,0:T(4,128)S(1)}, s32[4,1]{1,0:T(4,128)}, u32[]{:S(2)}) copy-start(s32[4,1]{1,0:T(4,128)} %copy-done.20) | copy-start | bytes 52
  150.2 25.2 %collective-permute-start.12 = (bf16[576,512]{1,0:T(8,128)(2,1)S(1)}, bf16[576,512]{1,0:T(8,128)(2,1)S(1)}, u32[]{:S(2)}, u32[]{:S(2)}) collective-permute-start(bf16[576,512]{1,0:T(8,128)(2,1)S(1)} %get-tuple-element.93), channel_id=1, source_target_pairs={{0,8},{4,12},{8,0},{12,4},{16,24},{20,28},{24,16},{28,20},{1,9},{5... | collective-permute-start | bytes 1769480 | tf_op jit(solution)/shard_map/ppermute | solution.py:46
  152.1 27.7 %collective-permute-start.13 = (bf16[576,512]{1,0:T(8,128)(2,1)S(1)}, bf16[576,512]{1,0:T(8,128)(2,1)S(1)}, u32[]{:S(2)}, u32[]{:S(2)}) collective-permute-start(bf16[576,512]{1,0:T(8,128)(2,1)S(1)} %get-tuple-element.94), channel_id=1, source_target_pairs={{0,16},{4,20},{8,24},{12,28},{16,0},{20,4},{24,8},{28,12},{1,17},{... | collective-permute-start | bytes 1769480 | tf_op jit(solution)/shard_map/ppermute | solution.py:46
  153.4 26.4 %collective-permute-start.14 = (bf16[576,512]{1,0:T(8,128)(2,1)S(1)}, bf16[576,512]{1,0:T(8,128)(2,1)S(1)}, u32[]{:S(2)}, u32[]{:S(2)}) collective-permute-start(bf16[576,512]{1,0:T(8,128)(2,1)S(1)} %get-tuple-element.95), channel_id=1, source_target_pairs={{0,24},{4,28},{8,16},{12,20},{16,8},{20,12},{24,0},{28,4},{1,25},{... | collective-permute-start | bytes 1769480 | tf_op jit(solution)/shard_map/ppermute | solution.py:46
  173.7 1.2 copy-start.8
  174.8 0.6 copy-start.24
  175.4 5.5 %collective-permute-start.11 = (bf16[4,384,512]{2,1,0:T(8,128)(2,1)}, bf16[4,384,512]{2,1,0:T(8,128)(2,1)}, u32[]{:S(2)}, u32[]{:S(2)}) collective-permute-start(bf16[4,384,512]{2,1,0:T(8,128)(2,1)} %get-tuple-element.92), channel_id=1, source_target_pairs={{0,4},{4,0},{8,12},{12,8},{16,20},{20,16},{24,28},{28,24},{1,5},{5... | collective-permute-start | bytes 4718600 | tf_op jit(solution)/shard_map/ppermute | solution.py:46
  181.0 8.9 %copy-start.1 = (bf16[4,80,1536]{2,1,0:T(8,128)(2,1)S(1)}, bf16[4,80,1536]{2,1,0:T(8,128)(2,1)}, u32[]{:S(2)}) copy-start(bf16[4,80,1536]{2,1,0:T(8,128)(2,1)} %copy-done) | copy-start | bytes 2949124
  181.0 8.9 %copy-start.3 = (bf16[4,80,1536]{2,1,0:T(8,128)(2,1)S(1)}, bf16[4,80,1536]{2,1,0:T(8,128)(2,1)}, u32[]{:S(2)}) copy-start(bf16[4,80,1536]{2,1,0:T(8,128)(2,1)} %copy-done.2) | copy-start | bytes 2949124
  181.0 1.5 copy-start.9
  182.5 7.4 %copy-start.22 = (s32[4,1]{1,0:T(4,128)S(1)}, s32[4,1]{1,0:T(4,128)}, u32[]{:S(2)}) copy-start(s32[4,1]{1,0:T(4,128)} %copy-done.20) | copy-start | bytes 52
  184.9 0.8 copy-start.28
  185.6 0.7 copy-start.29
  186.4 54.1 %all-reduce.2.cloned.1.call-start = ((), (), s32[]{:S(2)}) async-start(), calls=%async_computation | async-start | bytes 1179648 | tf_op jit(solution)/shard_map/psum | solution.py:1063
  186.4 23.7 %collective-permute-start.15 = (bf16[384,512]{1,0:T(8,128)(2,1)}, bf16[384,512]{1,0:T(8,128)(2,1)S(1)}, u32[]{:S(2)}, u32[]{:S(2)}) collective-permute-start(bf16[384,512]{1,0:T(8,128)(2,1)} %get-tuple-element.99), channel_id=1, source_target_pairs={{0,8},{4,12},{8,0},{12,4},{16,24},{20,28},{24,16},{28,20},{1,9},{5... | collective-permute-start | bytes 1179656 | tf_op jit(solution)/shard_map/ppermute | solution.py:46
  187.4 22.7 %collective-permute-start.16 = (bf16[384,512]{1,0:T(8,128)(2,1)}, bf16[384,512]{1,0:T(8,128)(2,1)S(1)}, u32[]{:S(2)}, u32[]{:S(2)}) collective-permute-start(bf16[384,512]{1,0:T(8,128)(2,1)} %copy-done.29), channel_id=1, source_target_pairs={{0,16},{4,20},{8,24},{12,28},{16,0},{20,4},{24,8},{28,12},{1,17},{... | collective-permute-start | bytes 1179656 | tf_op jit(solution)/shard_map/ppermute | solution.py:46
  188.1 22.0 %collective-permute-start.17 = (bf16[384,512]{1,0:T(8,128)(2,1)}, bf16[384,512]{1,0:T(8,128)(2,1)}, u32[]{:S(2)}, u32[]{:S(2)}) collective-permute-start(bf16[384,512]{1,0:T(8,128)(2,1)} %copy-done.28), channel_id=1, source_target_pairs={{0,24},{4,28},{8,16},{12,20},{16,8},{20,12},{24,0},{28,4},{1,25},{... | collective-permute-start | bytes 1179656 | tf_op jit(solution)/shard_map/ppermute | solution.py:46
  189.9 0.8 copy-start.16
  190.7 0.8 copy-start.18
  191.4 18.6 %copy-start.23 = (f32[16,512]{1,0:T(8,128)S(1)}, f32[16,512]{1,0:T(8,128)}, u32[]{:S(2)}) copy-start(f32[16,512]{1,0:T(8,128)} %get-tuple-element.104.mid_ref) | copy-start | bytes 98308
  191.4 18.6 %copy-start.25 = (f32[8,512]{1,0:T(8,128)S(1)}, f32[8,512]{1,0:T(8,128)}, u32[]{:S(2)}) copy-start(f32[8,512]{1,0:T(8,128)} %copy-done.24) | copy-start | bytes 49156
  191.4 18.6 %copy-start.26 = (f32[1,1536]{1,0:T(1,128)S(1)}, f32[1,1536]{1,0:T(1,128)}, u32[]{:S(2)}) copy-start(f32[1,1536]{1,0:T(1,128)} %get-tuple-element.105.bias1_ref) | copy-start | bytes 18436
  211.4 15.2 %collective-permute-start.18 = (bf16[96,512]{1,0:T(8,128)(2,1)S(1)}, bf16[96,512]{1,0:T(8,128)(2,1)S(1)}, u32[]{:S(2)}, u32[]{:S(2)}) collective-permute-start(bf16[96,512]{1,0:T(8,128)(2,1)S(1)} %get-tuple-element.107), channel_id=1, source_target_pairs={{0,1},{1,0},{2,3},{3,2},{4,5},{5,4},{6,7},{7,6},{8,9},{9,8},{10,11... | collective-permute-start | bytes 294920 | tf_op jit(solution)/shard_map/ppermute | solution.py:46
  214.5 13.0 %collective-permute-start.19 = (bf16[96,512]{1,0:T(8,128)(2,1)S(1)}, bf16[96,512]{1,0:T(8,128)(2,1)S(1)}, u32[]{:S(2)}, u32[]{:S(2)}) collective-permute-start(bf16[96,512]{1,0:T(8,128)(2,1)S(1)} %get-tuple-element.108), channel_id=1, source_target_pairs={{0,2},{1,3},{2,0},{3,1},{4,6},{5,7},{6,4},{7,5},{8,10},{9,11},{10,... | collective-permute-start | bytes 294920 | tf_op jit(solution)/shard_map/ppermute | solution.py:46
  217.4 10.1 %collective-permute-start.20 = (bf16[96,512]{1,0:T(8,128)(2,1)S(1)}, bf16[96,512]{1,0:T(8,128)(2,1)S(1)}, u32[]{:S(2)}, u32[]{:S(2)}) collective-permute-start(bf16[96,512]{1,0:T(8,128)(2,1)S(1)} %get-tuple-element.109), channel_id=1, source_target_pairs={{0,3},{1,2},{2,1},{3,0},{4,7},{5,6},{6,5},{7,4},{8,11},{9,10},{10,... | collective-permute-start | bytes 294920 | tf_op jit(solution)/shard_map/ppermute | solution.py:46
  227.6 12.9 %collective-permute-start.23 = (bf16[128,512]{1,0:T(8,128)(2,1)S(1)}, bf16[128,512]{1,0:T(8,128)(2,1)S(1)}, u32[]{:S(2)}, u32[]{:S(2)}) collective-permute-start(bf16[128,512]{1,0:T(8,128)(2,1)S(1)} %over_seq.1.refs_0_), channel_id=1, source_target_pairs={{0,3},{1,2},{2,1},{3,0},{4,7},{5,6},{6,5},{7,4},{8,11},{9,10},{10,... | collective-permute-start | bytes 393224 | tf_op jit(solution)/shard_map/ppermute | solution.py:46
  230.6 13.8 %collective-permute-start.22 = (bf16[128,512]{1,0:T(8,128)(2,1)S(1)}, bf16[128,512]{1,0:T(8,128)(2,1)S(1)}, u32[]{:S(2)}, u32[]{:S(2)}) collective-permute-start(bf16[128,512]{1,0:T(8,128)(2,1)S(1)} %over_seq.1.refs_0_), channel_id=1, source_target_pairs={{0,2},{1,3},{2,0},{3,1},{4,6},{5,7},{6,4},{7,5},{8,10},{9,11},{10,... | collective-permute-start | bytes 393224 | tf_op jit(solution)/shard_map/ppermute | solution.py:46
  240.0 5.7 %collective-permute-start.21 = (bf16[128,512]{1,0:T(8,128)(2,1)S(1)}, bf16[128,512]{1,0:T(8,128)(2,1)S(1)}, u32[]{:S(2)}, u32[]{:S(2)}) collective-permute-start(bf16[128,512]{1,0:T(8,128)(2,1)S(1)} %over_seq.1.refs_0_), channel_id=1, source_target_pairs={{0,1},{1,0},{2,3},{3,2},{4,5},{5,4},{6,7},{7,6},{8,9},{9,8},{10,11... | collective-permute-start | bytes 393224 | tf_op jit(solution)/shard_map/ppermute | solution.py:46
  245.7 1.1 copy-start.10
Sparse Core Ops, SparseCore 0:
  10.5 54.0 all-gather.3
  190.1 49.5 all-reduce.1

commit v3 on v2

--- a/solution.py
+++ b/solution.py
@@ -98,7 +98,7 @@
         self.start = lax.axis_index("seq") * rows - HALO
         self.total = rows * lax.axis_size("seq")
         self.length = lengths_ref[pl.program_id(0), 0]
-        self.tiles = [(0, HALO)] + [(r, 32) for r in range(HALO, HALO + rows, 32)] + [(HALO + rows, HALO)]
+        self.tiles = [(0, HALO)] + [(r, 64) for r in range(HALO, HALO + rows, 64)] + [(HALO + rows, HALO)]
         self.half = self.ext // 2
 
     def at(self, r=0, n=None):
@@ -141,15 +141,20 @@
     ref[8 * i : 8 * i + 8] += fold(x)
 
 
-def assemble(even_ref, odd_ref, size, whole_ref, sems):
+def assemble(even_ref, odd_ref, base, size, whole_ref, sems):
     me = lax.axis_index("dp")
     copies = []
     for h in range(even_ref.shape[0]):
         for c, ref in enumerate((even_ref, odd_ref)):
             at = pl.multiple_of((me ^ (2 * h + c)) * size, size)
-            copies.append(
-                pltpu.make_async_copy(ref.at[h, pl.ds(0, size)], whole_ref.at[pl.ds(at, size)], sems.at[2 * h + c])
-            )
+            for g in range(whole_ref.shape[1] // HALF):
+                copies.append(
+                    pltpu.make_async_copy(
+                        ref.at[h, pl.ds(base + g * size, size)],
+                        whole_ref.at[pl.ds(at, size), pl.ds(g * HALF, HALF)],
+                        sems.at[2 * h + c, g],
+                    )
+                )
     return copies
 
 
@@ -189,7 +194,7 @@
     ins = ins + [(a, "any") for a in after]
     return pl.pallas_call(
         kernel,
-        out_shape=[(pltpu.HBM if kind == "rows" else jax.ShapeDtypeStruct)(tuple(s), d) for s, d, kind in outs],
+        out_shape=[(pltpu.HBM if kind == "rows" or len(s) == 3 else jax.ShapeDtypeStruct)(tuple(s), d) for s, d, kind in outs],
         grid_spec=pltpu.PrefetchScalarGridSpec(
             num_scalar_prefetch=1,
             grid=(grid,),
@@ -203,18 +208,18 @@
     )(lengths, *[in_hbm(a) if kind == "rows" and a.shape[1] != HALO else a for a, kind in ins])
 
 
-def simple_call(kernel, ins, outs, name, scratch=(), after=(), limit=16, us=0):
+def simple_call(kernel, ins, outs, name, scratch=(), after=(), limit=16, us=0, hbm=(), out_hbm=False):
     whole = pl.BlockSpec(memory_space=pltpu.VMEM)
     return pl.pallas_call(
         skipping(kernel, len(ins), len(after)),
-        out_shape=[jax.ShapeDtypeStruct(tuple(s), d) for s, d in outs],
+        out_shape=[(pltpu.HBM if out_hbm else jax.ShapeDtypeStruct)(tuple(s), d) for s, d in outs],
         in_specs=[whole] * len(ins) + [pl.BlockSpec(memory_space=pl.ANY)] * len(after),
         out_specs=[whole] * len(outs),
         scratch_shapes=list(scratch),
         compiler_params=pltpu.CompilerParams(vmem_limit_bytes=limit * MiB),
         cost_estimate=cost(us),
         name=name,
-    )(*ins, *after)
+    )(*[in_hbm(a) if i in hbm else a for i, a in enumerate(ins)], *after)
 
 
 def head_columns(x):
@@ -225,7 +230,7 @@
 
 def pack_kernel(
     first_ref, last_ref, gfirst_ref, glast_ref, dw_ref, gains_ref, biases_ref, upb_ref, hgain_ref, hshift_ref,
-    head_ref, up_ref, down_ref, first_out, last_out, up0_out, rest_out,
+    head_ref, up_ref, down_ref, first_out, last_out, small_out, rest_out,
 ):
     width = first_ref.shape[2]
     first_out[:, :, :width] = first_ref[...]
@@ -233,8 +238,7 @@
     last_out[:, :, :width] = last_ref[...]
     last_out[:, :, width:] = glast_ref[...].astype(low)
     own = up_ref.shape[1]
-    up0_out[0:own] = up_ref[0]
-    up0_out[own:] = jnp.zeros((16, up_ref.shape[2]), low)
+    small_out[...] = jnp.zeros(small_out.shape, low)
 
     def stack(parts):
         parts = [p.astype(f32) for p in parts]
@@ -245,11 +249,11 @@
         high = x.astype(low).astype(f32)
         return [high, x - high]
 
-    up0_out[own:, 0:own] = stack([dw_ref[:, 0, :], dw_ref[:, 1, :]])
-    up0_out[own:, 128 : 128 + own] = stack(
+    small_out[:, 0:own] = stack([dw_ref[:, 0, :], dw_ref[:, 1, :]])
+    small_out[:, 128 : 128 + own] = stack(
         [gains_ref[0], gains_ref[1], biases_ref[:, 0, :], biases_ref[:, 1, :]] + halves(hgain_ref[...]) + halves(hshift_ref[...])
     )
-    up0_out[own:, 256 : 256 + upb_ref.shape[1]] = stack([upb_ref[...]])
+    small_out[:, 256 : 256 + upb_ref.shape[1]] = stack([upb_ref[...]])
     size = down_ref.shape[1]
     base = up_ref.shape[2] // HALF * own
     for g in range(0, up_ref.shape[2], HALF):
@@ -321,7 +325,7 @@
 
 def conv_kernel(
     rows, own, units, lengths, before_ref, features_ref, after_ref, hbias_ref, even_ref, odd_ref,
-    normed_ref, unit_ref, inv_ref, taps_ref, vec_ref, upb_ref, bias_ref, small_ref, pad_ref, sems,
+    normed_ref, unit_ref, inv_ref, masked_ref, taps_ref, vec_ref, upb_ref, bias_ref, small_ref, pad_ref, sems,
 ):
     @pl.when(pl.program_id(0) == 0)
     def _():
@@ -331,7 +335,7 @@
         for d in range(count):
             ref = odd_ref if d % 2 else even_ref
             copies.append(
-                pltpu.make_async_copy(ref.at[d // 2, pl.ds(own, 16), pl.ds(0, small_ref.shape[2])], small_ref.at[d], sems.at[d])
+                pltpu.make_async_copy(ref.at[d // 2], small_ref.at[d], sems.at[d])
             )
         run_copies(copies)
 
@@ -354,37 +358,52 @@
 
     frames = Frames(rows, lengths)
     put_padded(pad_ref, frames, functools.partial(feature_tile, frames, before_ref, features_ref, after_ref))
+    masked_ref[0] = pad_ref[8 : 8 + frames.ext].astype(low)
     conv_norm(frames, pad_ref, taps_ref, 0, vec_ref, 0, unit_ref.at[0], inv_ref.at[0], normed_ref.at[0])
 
 
-def up_gelu(frames, normed_at, weight_ref, bias, act_at, slope_at, chunk=256):
+def gelu_rows(normed, weight_ref, bias, act_at, slope_at, rows, chunk=256):
+    for c in range(0, weight_ref.shape[1], chunk):
+        pre = jnp.dot(normed, weight_ref[:, c : c + chunk], preferred_element_type=f32) + bias[:, c : c + chunk]
+        act, slope = gelu_parts(pre.astype(low))
+        act_at[rows, c : c + chunk] = act
+        slope_at[rows, c : c + chunk] = slope
+
+
+def up_gelu(frames, normed_at, weight_ref, bias, act_at, slope_at):
     for r0, _ in frames.parts():
-        normed = normed_at[r0 : r0 + frames.half]
-        for c in range(0, weight_ref.shape[1], chunk):
-            pre = jnp.dot(normed, weight_ref[:, c : c + chunk], preferred_element_type=f32) + bias[:, c : c + chunk]
-            act, slope = gelu_parts(pre.astype(low))
-            act_at[r0 : r0 + frames.half, c : c + chunk] = act
-            slope_at[r0 : r0 + frames.half, c : c + chunk] = slope
+        part = slice(r0, r0 + frames.half)
+        gelu_rows(normed_at[part], weight_ref, bias, act_at, slope_at, part)
 
 
 def forward_kernel(
-    rows, own, size, lengths, before_ref, features_ref, after_ref, normed_ref, vec_ref, upb_ref,
-    ueven_ref, uodd_ref, deven_ref, dodd_ref, hidden_ref, act_ref, slope_ref, branch_ref, up_ref, down_ref, sems, sems2,
+    own, size, lengths, masked_ref, normed_ref, vec_ref, upb_ref, even_ref, odd_ref,
+    hidden_ref, act_ref, slope_ref, branch_ref, up_ref, down_ref, sems, sems2,
 ):
-    @pl.when(pl.program_id(0) == 0)
+    first = pl.program_id(0) == 0
+    ups = assemble(even_ref, odd_ref, 0, own, up_ref, sems)
+    downs = assemble(even_ref, odd_ref, up_ref.shape[1] // HALF * own, size, down_ref, sems2)
+
+    @pl.when(first)
     def _():
-        run_copies(assemble(ueven_ref, uodd_ref, own, up_ref, sems) + assemble(deven_ref, dodd_ref, size, down_ref, sems2))
-
-    frames = Frames(rows, lengths)
+        for copy in ups + downs:
+            copy.start()
+        for copy in ups:
+            copy.wait()
+
     act_at = act_ref.at[0]
-    up_gelu(frames, normed_ref.at[0], up_ref, row(upb_ref, 0), act_at, slope_ref.at[0])
-    for r0, tiles in frames.parts():
-        product = jnp.dot(act_at[r0 : r0 + frames.half], down_ref[...], preferred_element_type=f32)
-        for r in tiles:
-            branch = product[r - r0 : r - r0 + 16] + bias_row(vec_ref, 0, 2)
-            branch_ref[0, r : r + 16] = branch.astype(low)
-            h = feature_tile(frames, before_ref, features_ref, after_ref, r, 16)
-            hidden_ref[0, r : r + 16] = h + gain_row(vec_ref, 0, 1) * branch
+    gelu_rows(normed_ref[0], up_ref, row(upb_ref, 0), act_at, slope_ref.at[0], slice(0, act_at.shape[0]))
+
+    @pl.when(first)
+    def _():
+        for copy in downs:
+            copy.wait()
+
+    product = jnp.dot(act_at[...], down_ref[...], preferred_element_type=f32)
+    for r in range(0, product.shape[0], 16):
+        branch = product[r : r + 16] + bias_row(vec_ref, 0, 2)
+        branch_ref[0, r : r + 16] = branch.astype(low)
+        hidden_ref[0, r : r + 16] = masked_ref[0, r : r + 16].astype(f32) + gain_row(vec_ref, 0, 1) * branch
 
 
 def split_rows(total_at, size, keep_at, send_at, pieces):
@@ -418,7 +437,7 @@
         add_to(sums_ref, at + 1, bgrad.astype(f32))
 
 
-def back_down(frames, bgrad_at, act_at, slope_at, weight_ref, total_ref, pgrad_at, bsums_ref, chunk=512):
+def back_down(frames, bgrad_at, act_at, slope_at, weight_ref, total_ref, pgrad_at, chunk=512):
     own = frames.own
     for c in range(0, weight_ref.shape[0], chunk):
         part = slice(c, c + chunk)
@@ -427,15 +446,10 @@
             for r in tiles:
                 grad = (act_grad[r - r0 : r - r0 + 16] * slope_at[r : r + 16, part].astype(f32)).astype(low)
                 pgrad_at[r : r + 16, part] = grad
-                if frames.owns(r):
-                    bsums_ref[:, part] += fold(grad.astype(f32))
         total_ref[part] += lax.dot_general(act_at[own, part], bgrad_at[own], rows_dims, preferred_element_type=f32)
 
 
-def back_up_norm(frames, pgrad_at, unit_at, inv_at, gain, weight_ref, pad_ref, sums_ref):
-    zeros = jnp.zeros((8, pad_ref.shape[1]), f32)
-    pad_ref[0:8] = zeros
-    pad_ref[frames.ext + 8 :] = zeros
+def back_up_norm(frames, pgrad_at, unit_at, inv_at, gain, weight_ref, put, sums_ref):
     for r0, tiles in frames.parts():
         product = lax.dot_general(pgrad_at[r0 : r0 + frames.half], weight_ref[...], cols_dims, preferred_element_type=f32)
         for r in tiles:
@@ -449,7 +463,7 @@
                 add_to(sums_ref, 9, normed_grad)
             else:
                 conv_grad = jnp.where(frames.inside(r, 16), conv_grad, 0.0).astype(low).astype(f32)
-            pad_ref[8 + r : 8 + r + 16] = conv_grad
+            put(r, conv_grad)
 
 
 def conv_back_tile(frames, r, n, pad_ref, block_in_of, hgrad, taps_ref, base, sums_ref):
@@ -472,36 +486,39 @@
 def middle_kernel(
     rows, own, size, lengths, h_ref, tgrad_ref, recip_ref, taps_ref, vec_ref, upb_ref, bias_ref,
     table_hbm, rest_ref,
-    audio_ref, hgrad_ref, keep_ref, send_ref, small_ref, sbias_ref,
+    audio_ref, hgrad_ref, cgrad_ref, keep_ref, send_ref, small_ref, sbias_ref,
     table_ref, up_ref, down_ref, head_ref, head_total, up_total, down_total, act_ref, slope_ref,
-    pad_ref, cpad_ref, frame_ref, unit1_ref, unit2_ref, inv1_ref, inv2_ref, normed1_ref, normed2_ref, turned_ref,
-    branch_ref, bgrad_ref, spectrum_ref, lgrad_ref, sums_ref, bsums_ref, hsums_ref, sems,
+    pad_ref, frame_ref, unit1_ref, unit2_ref, inv1_ref, inv2_ref, normed1_ref, normed2_ref, turned_ref,
+    branch_ref, bgrad_ref, spectrum_ref, lgrad_ref, sums_ref, sems,
 ):
     step = pl.program_id(0)
 
+    copies = []
+    groups = up_ref.shape[1] // HALF
+    width = up_ref.shape[0]
+    places = [(g * own, own, up_ref, g * HALF, HALF) for g in range(groups)]
+    places.append((groups * own, size, down_ref, 0, HALF))
+    base = groups * own + size
+    places += [(base + g * own, own, head_ref, g * HALF, lanes) for g, lanes in enumerate((HALF, HALF, EXTRA))]
+    for j in range(rest_ref.shape[0]):
+        for i, (at, many, ref, lane, lanes) in enumerate(places):
+            copy = pltpu.make_async_copy(
+                rest_ref.at[j, pl.ds(at, many), pl.ds(0, lanes)],
+                ref.at[pl.ds(j * many, many), pl.ds(lane, lanes)],
+                sems.at[j, i],
+            )
+            copies.append((copy, i))
+    copies.append((pltpu.make_async_copy(table_hbm, table_ref, sems.at[0, len(places)]), len(places)))
+    copies.sort(key=lambda pair: pair[1])
+
     @pl.when(step == 0)
     def _():
-        copies = []
-        groups = up_ref.shape[1] // HALF
-        places = [(g * own, own, up_ref, g * HALF, HALF) for g in range(groups)]
-        places.append((groups * own, size, down_ref, 0, HALF))
-        base = groups * own + size
-        places += [(base + g * own, own, head_ref, g * HALF, lanes) for g, lanes in enumerate((HALF, HALF, EXTRA))]
-        for j in range(rest_ref.shape[0]):
-            for i, (at, many, ref, lane, lanes) in enumerate(places):
-                copies.append(
-                    pltpu.make_async_copy(
-                        rest_ref.at[j, pl.ds(at, many), pl.ds(0, lanes)],
-                        ref.at[pl.ds(j * many, many), pl.ds(lane, lanes)],
-                        sems.at[j, i],
-                    )
-                )
-        copies.append(pltpu.make_async_copy(table_hbm, table_ref, sems.at[0, len(places)]))
-        for copy in copies:
+        for copy, _ in copies:
             copy.start()
-        for ref in (head_total, up_total, down_total, sums_ref, bsums_ref, hsums_ref):
+        for ref in (head_total, up_total, down_total, sums_ref):
             ref[...] = jnp.zeros_like(ref)
-        for copy in copies:
+        turned_ref[width:] = jnp.ones((16, rows), low)
+        for copy, _ in copies:
             copy.wait()
 
     frames = Frames(rows, lengths)
@@ -553,8 +570,6 @@
             for g, grad in enumerate(grads):
                 part = slice(g * HALF, g * HALF + grad.shape[1])
                 lgrad_ref[r : r + 16, part] = grad.astype(low)
-                if frames.owns(r):
-                    hsums_ref[:, part] += fold(grad)
 
     for r0, tiles in frames.parts():
         product = jnp.dot(spectrum_ref[r0 : r0 + half], table_ref[...], preferred_element_type=f32)
@@ -593,7 +608,7 @@
             put(part, product)
 
     own_tiles = [tile for tile in frames.tiles if frames.owns(tile[0])]
-    turned_ref[...] = normed2_ref[mine].T
+    turned_ref[:width] = normed2_ref[mine].T
 
     def put_head(part, product):
         head_total[:, part] += product
@@ -606,35 +621,25 @@
         audio_tile,
     )
 
-    back_down(frames, bgrad_ref, act_ref, slope_ref, down_ref, down_total, slope_ref, bsums_ref)
-    back_up_norm(frames, slope_ref, unit1_ref, inv1_ref, gain_row(vec_ref, 1, 0), up_ref, cpad_ref, sums_ref)
-    turned_ref[...] = normed1_ref[mine].T
-
-    def put_up(part, product):
-        up_total[:, part] += product
-
-    def conv_back(r, n):
-        hgrad_at[r : r + n] = conv_back_tile(
-            frames, r, n, cpad_ref, lambda r, n: pad_ref[8 + r : 8 + r + n], hgrad_at[r : r + n], taps_ref, KERNEL, sums_ref
-        )
-
-    beside(
-        [slice(c, c + 256) for c in range(0, up_total.shape[1], 256)],
-        frames.tiles,
-        lambda part: jnp.dot(turned_ref[...], slope_ref[mine, part], preferred_element_type=f32),
-        put_up,
-        conv_back,
-    )
+    back_down(frames, bgrad_ref, act_ref, slope_ref, down_ref, down_total, slope_ref)
+    def put_conv(r, grad):
+        cgrad_ref[0, r : r + 16] = grad.astype(low)
+
+    back_up_norm(frames, slope_ref, unit1_ref, inv1_ref, gain_row(vec_ref, 1, 0), up_ref, put_conv, sums_ref)
+    turned_ref[:width] = normed1_ref[mine].T
+
+    for c in range(0, up_total.shape[1], 256):
+        up_total[:, c : c + 256] += jnp.dot(turned_ref[...], slope_ref[mine, c : c + 256], preferred_element_type=f32)
 
     @pl.when(step == pl.num_programs(0) - 1)
     def _():
         close_sums(sums_ref, small_ref)
-        sbias_ref[...] = total_rows(bsums_ref[...])
+        sbias_ref[...] = up_total[width : width + 1]
         groups = up_ref.shape[1] // HALF * own
         split_columns(up_total, 0, own, keep_ref, send_ref)
         split_columns(down_total, groups, size, keep_ref, send_ref)
         base = groups + size
-        bias = total_rows(hsums_ref[...])
+        bias = head_total[width : width + 1]
         block = jnp.concatenate([bias[:, g : g + 384] for g in (0, 384, 768)] + [jnp.zeros((13, 384), f32)], axis=0)
         for h in range(keep_ref.shape[0]):
             for ref in (keep_ref, send_ref):
@@ -644,32 +649,44 @@
 
 
 def back_down_kernel(
-    rows, own, size, lengths, hgrad_ref, branch_ref, act_ref, slope_ref, normed_ref, vec_ref, even_ref, odd_ref,
-    pgrad_ref, keep_ref, send_ref, small_ref, sbias_ref, weight_ref, down_total, up_total, bgrad_ref, sums_ref, bsums_ref, sems,
+    rows, own, size, lengths, head_ref, cgrad_ref, h_ref, taps_ref, branch_ref, act_ref, slope_ref, normed_ref, vec_ref,
+    even_ref, odd_ref, pgrad_ref, hgrad_ref, keep_ref, send_ref, small_ref, sbias_ref, weight_ref, down_total, up_total, bgrad_ref, turned_ref, pad_ref, sums_ref, sems,
 ):
     step = pl.program_id(0)
 
     @pl.when(step == 0)
     def _():
-        copies = assemble(even_ref, odd_ref, size, weight_ref, sems)
+        copies = assemble(even_ref, odd_ref, up_total.shape[1] // HALF * own, size, weight_ref, sems)
         for copy in copies:
             copy.start()
-        for ref in (down_total, up_total, sums_ref, bsums_ref):
+        for ref in (down_total, up_total, sums_ref):
             ref[...] = jnp.zeros_like(ref)
+        turned_ref[normed_ref.shape[2] :] = jnp.ones((16, rows), low)
         for copy in copies:
             copy.wait()
 
     frames = Frames(rows, lengths)
     mine = frames.own
+    put_padded(pad_ref, frames, lambda r, n: cgrad_ref[0, r : r + n].astype(f32))
+
+    def block_in_tile(r, n):
+        return jnp.where(frames.inside(r, n), h_ref[0, r : r + n], 0.0).astype(low).astype(f32)
+
+    for r, n in frames.tiles:
+        hgrad_ref[0, r : r + n] = conv_back_tile(
+            frames, r, n, pad_ref, block_in_tile, head_ref[0, r : r + n], taps_ref, KERNEL, sums_ref
+        )
     for r in range(0, frames.ext, 16):
-        branch_tile(frames, r, hgrad_ref[0, r : r + 16], branch_ref[0, r : r + 16], gain_row(vec_ref, 0, 1), bgrad_ref, sums_ref, 0)
-    back_down(frames, bgrad_ref, act_ref.at[0], slope_ref.at[0], weight_ref, down_total, pgrad_ref.at[0], bsums_ref)
-    up_total[...] += lax.dot_general(normed_ref[0, mine], pgrad_ref[0, mine], rows_dims, preferred_element_type=f32)
+        branch_tile(frames, r, hgrad_ref[0, r : r + 16], branch_ref[0, r : r + 16], gain_row(vec_ref, 0, 1), bgrad_ref, sums_ref, 8)
+    back_down(frames, bgrad_ref, act_ref.at[0], slope_ref.at[0], weight_ref, down_total, pgrad_ref.at[0])
+    width = normed_ref.shape[2]
+    turned_ref[:width] = normed_ref[0, mine].T
+    up_total[...] += jnp.dot(turned_ref[...], pgrad_ref[0, mine], preferred_element_type=f32)
 
     @pl.when(step == pl.num_programs(0) - 1)
     def _():
         close_sums(sums_ref, small_ref)
-        sbias_ref[...] = total_rows(bsums_ref[...])
+        sbias_ref[...] = up_total[width : width + 1]
         split_columns(up_total, 0, own, keep_ref, send_ref)
         split_columns(down_total, up_total.shape[1] // HALF * own, size, keep_ref, send_ref)
 
@@ -683,11 +700,18 @@
     @pl.when(step == 0)
     def _():
         sums_ref[...] = jnp.zeros_like(sums_ref)
-        run_copies(assemble(even_ref, odd_ref, own, weight_ref, sems))
+        run_copies(assemble(even_ref, odd_ref, 0, own, weight_ref, sems))
 
     frames = Frames(rows, lengths)
+    zeros = jnp.zeros((8, pad_ref.shape[1]), f32)
+    pad_ref[0:8] = zeros
+    pad_ref[frames.ext + 8 :] = zeros
+
+    def put_conv(r, grad):
+        pad_ref[8 + r : 8 + r + 16] = grad
+
     back_up_norm(
-        frames, pgrad_ref.at[0], unit_ref.at[0], inv_ref.at[0], gain_row(vec_ref, 0, 0), weight_ref, pad_ref, sums_ref
+        frames, pgrad_ref.at[0], unit_ref.at[0], inv_ref.at[0], gain_row(vec_ref, 0, 0), weight_ref, put_conv, sums_ref
     )
 
     def block_in_tile(r, n):
@@ -707,9 +731,9 @@
     width = out_ref.shape[1]
     groups = [r[:, g : g + width] for r in (bias0_ref, bias1_ref) for g in range(0, r.shape[1], width)]
     rows = [
-        conv0_ref[0:7], mid_ref[0:7],
-        conv0_ref[8:9], down0_ref[0:1], mid_ref[8:9], mid_ref[10:11],
-        conv0_ref[7:8], conv0_ref[9:10], down0_ref[1:2], mid_ref[7:8], mid_ref[9:10], mid_ref[11:12],
+        conv0_ref[0:7], down0_ref[0:7],
+        conv0_ref[8:9], down0_ref[8:9], mid_ref[8:9], mid_ref[10:11],
+        conv0_ref[7:8], conv0_ref[9:10], down0_ref[9:10], mid_ref[7:8], mid_ref[9:10], mid_ref[11:12],
         mid_ref[12:14],
     ] + groups
     filled = 26 + len(groups)
@@ -717,11 +741,19 @@
     out_ref[...] = jnp.concatenate(rows, axis=0).astype(low)
 
 
-def gather_kernel(pieces, at, *refs):
-    for h in range(pieces):
-        refs[-1 if len(refs) == pieces + 1 else pieces + 1][h] = refs[h][...]
-    if len(refs) > pieces + 1:
-        refs[-1][...] = refs[pieces][at]
+def gather_kernel(*refs):
+    for h, ref in enumerate(refs[:-1]):
+        refs[-1][h] = ref[...]
+
+
+def gather_first_kernel(*refs):
+    up_ref, down_ref, stack_ref, piece_ref = refs[-4:]
+    for h, ref in enumerate(refs[:-4]):
+        stack_ref[h] = ref[...]
+    own = up_ref.shape[1]
+    for g in range(0, up_ref.shape[2], HALF):
+        piece_ref[g // HALF * own : (g // HALF + 1) * own] = up_ref[0, :, g : g + HALF]
+    piece_ref[up_ref.shape[2] // HALF * own :] = down_ref[0]
 
 
 def final_kernel(
@@ -822,7 +854,7 @@
 def pair_stage(keep, recv, name, after=()):
     piece = keep.shape[1:]
     kept, *sent = simple_call(
-        pair_kernel, [keep, recv], [(piece, f32)] + [(piece, low)] * (keep.shape[0] - 1), name, after=after
+        pair_kernel, [keep, recv], [(piece, f32)] + [(piece, low)] * (keep.shape[0] - 1), name, after=after, hbm=(0,), out_hbm=True
     )
     return kept, [swap(x, "dp", 2 * (h + 1)) for h, x in enumerate(sent)]
 
@@ -883,14 +915,14 @@
     packed_outs = [
         (micro, HALO, width + HOP),
         (micro, HALO, width + HOP),
-        (own + 16, units),
+        (16, HALF),
         (units // HALF * own + size + 3 * own, HALF),
     ]
 
     def whole_block(dims):
         return pl.BlockSpec(tuple(dims), lambda i: (0,) * len(dims))
 
-    first, last, up0_piece, rest_piece = pl.pallas_call(
+    first, last, small_piece, rest_piece = pl.pallas_call(
         pack_kernel,
         grid=(1,),
         in_specs=[edge(width, 0), edge(width, last_at), edge(HOP, 0), edge(HOP, last_at)]
@@ -916,17 +948,17 @@
     def across(x):
         return [x] + [swap(x, "dp", d) for d in range(2, count, 2)]
 
-    def stacked(pieces, name, after, following=None):
-        piece = pieces[0].shape
-        ins = pieces + ([] if following is None else [following[0]])
-        outs = [((pairs,) + piece, low)] + ([] if following is None else [(following[0].shape[1:], low)])
-        if following is None:
-            (even,) = simple_call(functools.partial(gather_kernel, pairs, 0), ins, outs, name, after=after)
-            return (even, swap(even, "dp", 1)), None
-        even, piece = simple_call(functools.partial(gather_kernel, pairs, following[1]), ins, outs, name, after=after)
-        return (even, swap(even, "dp", 1)), piece
-
-    up0_pieces = across(up0_piece)
+    grouped = units // HALF * own
+    small_pieces = across(small_piece)
+    small_even, block0_piece = simple_call(
+        gather_first_kernel,
+        small_pieces + [up_weight, down_weight],
+        [((pairs, 16, HALF), low), ((grouped + size, HALF), low)],
+        "stack_small",
+        after=[before, after],
+    )
+    small_odd = swap(small_even, "dp", 1)
+    block0_pieces = across(block0_piece)
     table_grad, recip = run(
         functools.partial(dft_kernel, rows),
         ins=[(before, "rows"), (audio_grad, "rows"), (after, "rows"), (squared, "all"), (tables, "all")],
@@ -935,15 +967,15 @@
         us=20,
         name="dft",
     )
-    up0, down0_piece = stacked(up0_pieces, "stack_up0", [recip], (down_weight, 0))
-    down0_pieces = across(down0_piece)
-    normed, unit, inv_std, taps, vec, upb, bias_row_all = run(
+    normed, unit, inv_std, masked, taps, vec, upb, bias_row_all = run(
         functools.partial(conv_kernel, rows, own, units),
-        ins=[(before, "rows"), (features, "rows"), (after, "rows"), (head_bias[None], "all"), (up0[0], "any"), (up0[1], "any")],
+        ins=[(before, "rows"), (features, "rows"), (after, "rows"), (head_bias[None], "all"), (small_even, "any"), (small_odd, "any")],
+        after=[recip],
         outs=[
             (shape(width), low, "rows"),
             (shape(width), low, "rows"),
             (shape(1), f32, "rows"),
+            (shape(width), low, "rows"),
             ((16, width), f32, "all"),
             ((16, width), f32, "all"),
             ((16, units), f32, "all"),
@@ -952,28 +984,34 @@
         scratch=[pltpu.VMEM((count, 16, 512), low), pltpu.VMEM((ext + 16, width), f32), dma()],
         name="conv",
     )
-    down0, _ = stacked(down0_pieces, "stack_down0", [taps])
-    hidden, act, slope, branch = run(
-        functools.partial(forward_kernel, rows, own, size),
+    (block0_even,) = simple_call(
+        gather_kernel, block0_pieces, [((pairs, grouped + size, HALF), low)], "stack_block0", after=[taps]
+    )
+    block0 = [(block0_even, "any"), (swap(block0_even, "dp", 1), "any")]
+    halves = (2 * micro, ext // 2)
+    hidden, act, slope, branch = call(
+        functools.partial(forward_kernel, own, size),
+        2 * micro,
+        lengths,
         ins=[
-            (before, "rows"),
-            (features, "rows"),
-            (after, "rows"),
-            (normed, "rows"),
+            (masked.reshape(halves + (width,)), "rows"),
+            (normed.reshape(halves + (width,)), "rows"),
             (vec, "all"),
             (upb, "all"),
-            (up0[0], "any"),
-            (up0[1], "any"),
-            (down0[0], "any"),
-            (down0[1], "any"),
+        ]
+        + block0,
+        outs=[
+            (halves + (width,), f32, "rows"),
+            (halves + (units,), low, "rows"),
+            (halves + (units,), low, "rows"),
+            (halves + (width,), low, "rows"),
         ],
-        outs=[(shape(width), f32, "rows"), (shape(units), low, "rows"), (shape(units), low, "rows"), (shape(width), low, "rows")],
-        scratch=[pltpu.VMEM((width, units), low), pltpu.VMEM((units, width), low), dma(), dma()],
+        scratch=[pltpu.VMEM((width, units), low), pltpu.VMEM((units, width), low), dma(count, units // HALF), dma(count, 1)],
         name="forward",
     )
-    grouped = units // HALF * own
+    hidden, act, slope, branch = (x.reshape(micro, ext, -1) for x in (hidden, act, slope, branch))
     packed = 3 * own + size + grouped
-    audio, incoming, keep1, send1, small_mid, sbias1 = run(
+    audio, head_grad_rows, conv_grad1, keep1, send1, small_mid, sbias1 = run(
         functools.partial(middle_kernel, rows, own, size),
         ins=[
             (hidden, "rows"),
@@ -989,6 +1027,7 @@
         outs=[
             ((micro, rows, HOP), f32, "rows"),
             (shape(width), f32, "rows"),
+            (shape(width), low, "rows"),
             ((pairs, packed, HALF), low, "all"),
             ((pairs, packed, HALF), low, "all"),
             ((16, width), f32, "all"),
@@ -999,12 +1038,11 @@
             pltpu.VMEM((width, units), low),
             pltpu.VMEM((units, width), low),
             pltpu.VMEM((width, columns), low),
-            pltpu.VMEM((width, columns), f32),
-            pltpu.VMEM((width, units), f32),
+            pltpu.VMEM((width + 16, columns), f32),
+            pltpu.VMEM((width + 16, units), f32),
             pltpu.VMEM((units, width), f32),
             pltpu.VMEM((ext, units), low),
             pltpu.VMEM((ext, units), low),
-            pltpu.VMEM((ext + 16, width), f32),
             pltpu.VMEM((ext + 16, width), f32),
             pltpu.VMEM((ext + 16, NFFT), f32),
             pltpu.VMEM((ext, width), f32),
@@ -1013,47 +1051,49 @@
             pltpu.VMEM((ext, 1), f32),
             pltpu.VMEM((ext, width), low),
             pltpu.VMEM((ext, width), low),
-            pltpu.VMEM((width, rows), low),
+            pltpu.VMEM((width + 16, rows), low),
             pltpu.VMEM((ext, width), low),
             pltpu.VMEM((ext, width), low),
             pltpu.VMEM((ext, NFFT), low),
             pltpu.VMEM((ext, columns), low),
             pltpu.VMEM((128, width), f32),
-            pltpu.VMEM((8, units), f32),
-            pltpu.VMEM((8, columns), f32),
             dma(count, 5 + units // HALF),
         ],
         name="middle",
         limit=56,
     )
     kept1, recvs1 = pair_stage(keep1, swap(send1, "dp", 1), "late_pair")
-    pre_grad, keep, send, small_down, sbias0 = run(
+    pre_grad, incoming, keep, send, small_down, sbias0 = run(
         functools.partial(back_down_kernel, rows, own, size),
         ins=[
-            (incoming, "rows"),
+            (head_grad_rows, "rows"),
+            (conv_grad1, "rows"),
+            (hidden, "rows"),
+            (taps, "all"),
             (branch, "rows"),
             (act, "rows"),
             (slope, "rows"),
             (normed, "rows"),
             (vec, "all"),
-            (down0[0], "any"),
-            (down0[1], "any"),
-        ],
+        ]
+        + block0,
         outs=[
             (shape(units), low, "rows"),
+            (shape(width), f32, "rows"),
             ((pairs, grouped + size, width), low, "all"),
             ((pairs, grouped + size, width), low, "all"),
-            ((8, width), f32, "all"),
+            ((16, width), f32, "all"),
             ((1, units), f32, "all"),
         ],
         scratch=[
             pltpu.VMEM((units, width), low),
             pltpu.VMEM((units, width), f32),
-            pltpu.VMEM((width, units), f32),
+            pltpu.VMEM((width + 16, units), f32),
             pltpu.VMEM((ext, width), low),
-            pltpu.VMEM((64, width), f32),
-            pltpu.VMEM((8, units), f32),
-            dma(),
+            pltpu.VMEM((width + 16, rows), low),
+            pltpu.VMEM((ext + 16, width), f32),
+            pltpu.VMEM((128, width), f32),
+            dma(count, 1),
         ],
         after=[kept1],
         us=20,
@@ -1072,11 +1112,10 @@
             (incoming, "rows"),
             (taps, "all"),
             (vec, "all"),
-            (up0[0], "any"),
-            (up0[1], "any"),
-        ],
+        ]
+        + block0,
         outs=[((micro, rows, width), f32, "rows"), ((16, width), f32, "all")],
-        scratch=[pltpu.VMEM((width, units), low), pltpu.VMEM((ext + 16, width), f32), pltpu.VMEM((128, width), f32), dma()],
+        scratch=[pltpu.VMEM((width, units), low), pltpu.VMEM((ext + 16, width), f32), pltpu.VMEM((128, width), f32), dma(count, units // HALF)],
         after=[kept],
         name="back_up",
     )

time: 257 us -> 250 us (0.973)
  waiting for transfers between devices: 27.3 us -> 20.1 us
    ppermute x22, waiting for transfers between devices: 25.5 us -> 20.1 us  [swap(): lax.ppermute(x, axis, [(i, i ^ d) for i in range(lax.axis_size(axis))])]
    unnamed x67 -> x57, local copies, waits for them, and re-layouts: 10.7 us -> 8.93 us
  transfers between devices with their start and end apart: 26 -> 26, of which waited for: 10 -> 9; matrix products, arithmetic and copies ran while one was open for 0% -> 0% of each run, Pallas kernels for 31% -> 34%
where the time goes in v3:
time: 250 us
  Pallas kernels  156 us (62%)
  starting transfers between devices  40.3 us (16%)
  waiting for transfers between devices  20.1 us (8%)
  between operations  14.4 us (6%)
  blocking collectives  9.27 us (4%)
  local copies, waits for them, and re-layouts  8.93 us (4%)
    pallas_call x6, Pallas kernels, call(): pl.pallas_call(kernel, out_shape=[(pltpu.HBM if kind == 'rows' or len(s)...  143 us
    ppermute x22, starting transfers between devices, swap(): lax.ppermute(x, axis, [(i, i ^ d) for i in range(lax.axis_size(axis))])  34.1 us
    ppermute x22, waiting for transfers between devices, swap(): lax.ppermute(x, axis, [(i, i ^ d) for i in range(lax.axis_size(axis))])  20.1 us
    pallas_call x9, Pallas kernels, simple_call(): pl.pallas_call(skipping(kernel, len(ins), len(after)), out_shape=[(pltpu....  10.5 us
    all_gather x1, blocking collectives, per_device(): small_all = lax.all_gather(smalls, 'dp', axis=0)  9.27 us
    unnamed x57, local copies, waits for them, and re-layouts  8.93 us
  transfers between devices with their start and end apart: 26, of which 9 were waited for; matrix products, arithmetic and copies ran while one was open for 0% of the time, Pallas kernels for 34%

profile of v3, /device:TPU:0, one launch (start us, length us, event | category | flops | bytes accessed | tf_op | source)
XLA Modules:
  0.0 249.7 jit_solution(8184776546176007294)
XLA Ops:
  7.2 0.0 all-gather.4.cloned.1.call-start
  7.3 0.0 copy-start.4
  7.3 0.0 copy-start.25
  7.3 2.4 pack.1
  9.7 0.0 all-gather.4.cloned.1.call-update
  9.8 4.9 %collective-permute-start = (bf16[4,16,768]{2,1,0:T(8,128)(2,1)}, bf16[4,16,768]{2,1,0:T(8,128)(2,1)S(1)}, u32[]{:S(2)}, u32[]{:S(2)}) collective-permute-start(bf16[4,16,768]{2,1,0:T(8,128)(2,1)} %get-tuple-element.69), channel_id=1, source_target_pairs={{0,1},{1,2},{2,3},{4,5},{5,6},{6,7},{8,9},{9,10},{10,11},{12,13},{... | collective-permute-start | bytes 294920 | tf_op jit(solution)/shard_map/ppermute | solution.py:936
  14.7 1.3 collective-permute-start.1
  16.0 2.5 %collective-permute-start.4 = (bf16[16,512]{1,0:T(8,128)(2,1)}, bf16[16,512]{1,0:T(8,128)(2,1)S(1)}, u32[]{:S(2)}, u32[]{:S(2)}) collective-permute-start(bf16[16,512]{1,0:T(8,128)(2,1)} %get-tuple-element.71.refs_0_), channel_id=1, source_target_pairs={{0,24},{4,28},{8,16},{12,20},{16,8},{20,12},{24,0},{28,4},{1,25},{... | collective-permute-start | bytes 49160 | tf_op jit(solution)/shard_map/ppermute | solution.py:46
  18.5 0.5 collective-permute-start.3
  19.0 0.5 collective-permute-start.2
  19.6 0.1 copy.30.lengths.refs_0_
  19.7 1.3 collective-permute-done.4.refs_3_
  20.9 1.5 collective-permute-done.3.refs_2_
  22.5 0.5 collective-permute-done.2.refs_1_
  23.0 0.0 copy-start.21
  23.0 0.7 copy-done.21
  23.7 1.6 collective-permute-start.8
  25.3 0.5 collective-permute-start.7
  25.8 1.5 collective-permute-start.6
  27.3 8.7 %dft.1 = (bf16[4,544,1024]{2,1,0:T(8,128)(2,1)}, f32[544,256]{1,0:T(8,128)S(1)}) custom-call(s32[4,1]{1,0:T(4,128)S(1)} %copy.30.lengths.refs_0_, bf16[4,16,768]{2,1,0:T(8,128)(2,1)S(1)} %collective-permute-done.refs_6_.before_ref.refs_1_, f32[4,512,256]{2,1,0:T(8,128)} %bitcast.31, bf16[4,16,768]{2,1,0:T(8,128)(2,1)S(1)} %collective-permute-done.1.refs_7_.after_ref.refs_3_, ...), custom_call_target="tpu_custom_call" | custom-call | flops 20000000000 | bytes 1000 | tf_op jit(solution)/shard_map/dft/pallas_call | solution.py:195
  36.1 10.8 %conv.1 = (bf16[4,544,512]{2,1,0:T(8,128)(2,1)}, bf16[4,544,512]{2,1,0:T(8,128)(2,1)}, f32[4,544,1]{2,1,0:T(8,128)}, bf16[4,544,512]{2,1,0:T(8,128)(2,1)}, f32[1...) custom-call(s32[4,1]{1,0:T(4,128)S(1)} %copy.30.lengths.refs_0_, ...), custom_call_target="tpu_custom_call" | custom-call | flops 1000 | bytes 1000 | tf_op jit(solution)/shard_map/conv/pallas_call | solution.py:195
  46.9 0.6 copy-done.23
  47.5 0.1 stack_block0.1.even_ref.refs_10_.refs_8_
  47.6 0.6 collective-permute-start.9
  48.2 3.3 %collective-permute-done.9.odd_ref.refs_11_.refs_9_ = bf16[4,384,512]{2,1,0:T(8,128)(2,1)S(1)} collective-permute-done((bf16[4,384,512]{2,1,0:T(8,128)(2,1)S(1)}, bf16[4,384,512]{2,1,0:T(8,128)(2,1)S(1)}, u32[]{:S(2)}, u32[]{:S(2)}) %collective-permute-start.9) | collective-permute-done | bytes 1572896 | tf_op jit(solution)/shard_map/ppermute | solution.py:46
  51.5 18.0 %forward.1 = (f32[8,272,512]{2,1,0:T(8,128)}, bf16[8,272,1536]{2,1,0:T(8,128)(2,1)}, bf16[8,272,1536]{2,1,0:T(8,128)(2,1)}, bf16[8,272,512]{2,1,0:T(8,128)(2,1)}) custom-call(s32[4,1]{1,0:T(4,128)S(1)} %copy.30.lengths.refs_0_, bf16[8,272,512]{2,1,0:T(8,128)(2,1)} %bitcast.36, bf16[8,272,512]{2,1,0:T(8,128)(2,1)} %bitcast.35, ...), custom_call_target="tpu_custom_call" | custom-call | flops 1000 | bytes 1000 | tf_op jit(solution)/shard_map/forward/pallas_call | solution.py:195
  69.5 0.0 all-gather.4.cloned.1.call-done
  69.6 61.0 %middle.1 = (f32[4,512,256]{2,1,0:T(8,128)}, f32[4,544,512]{2,1,0:T(8,128)}, bf16[4,544,512]{2,1,0:T(8,128)(2,1)}, bf16[4,576,512]{2,1,0:T(8,128)(2,1)}, bf16[4,...) custom-call(s32[4,1]{1,0:T(4,128)} %copy-done.15, f32[4,544,512]{2,1,0:T(8,128)} %bitcast.33, ...), custom_call_target="tpu_custom_call" | custom-call | flops 1000 | bytes 1000 | tf_op jit(solution)/shard_map/middle/pallas_call | solution.py:195
  130.6 0.3 collective-permute-start.10
  130.9 4.5 %collective-permute-done.10.recv_ref = bf16[4,576,512]{2,1,0:T(8,128)(2,1)S(1)} collective-permute-done((bf16[4,576,512]{2,1,0:T(8,128)(2,1)}, bf16[4,576,512]{2,1,0:T(8,128)(2,1)S(1)}, u32[]{:S(2)}, u32[]{:S(2)}) %collective-permute-start.10) | collective-permute-done | bytes 2359328 | tf_op jit(solution)/shard_map/ppermute | solution.py:46
  135.4 3.4 %late_pair.1 = (f32[576,512]{1,0:T(8,128)}, bf16[576,512]{1,0:T(8,128)(2,1)}, bf16[576,512]{1,0:T(8,128)(2,1)}, bf16[576,512]{1,0:T(8,128)(2,1)}) custom-call(bf16[4,576,512]{2,1,0:T(8,128)(2,1)} %get-tuple-element.90.keep_ref, bf16[4,576,512]{2,1,0:T(8,128)(2,1)S(1)} %collective-permute-done.10.recv_ref), custom_call_target="tpu_custom_call" | custom-call | flops 1000 | bytes 1000 | tf_op jit(solution)/shard_map/late_pair/pallas_call | solution.py:213
  138.8 1.8 collective-permute-start.12
  140.6 1.6 collective-permute-start.13
  142.2 0.1 collective-permute-start.14
  142.3 1.3 copy-done.24
  143.6 27.8 %back_down.1 = (bf16[4,544,1536]{2,1,0:T(8,128)(2,1)}, f32[4,544,512]{2,1,0:T(8,128)}, bf16[4,384,512]{2,1,0:T(8,128)(2,1)}, bf16[4,384,512]{2,1,0:T(8,128)(2,1)...) custom-call(s32[4,1]{1,0:T(4,128)S(1)} %copy-done.16, f32[4,544,512]{2,1,0:T(8,128)} %get-tuple-element.85.refs_1_, ...), custom_call_target="tpu_custom_call" | custom-call | flops 20000000000 | bytes 1000 | tf_op jit(solution)/shard_map/back_down/pallas_call | solution.py:195
  171.4 0.6 copy-done.19
  172.0 0.3 late_cross.1.refs_2_
  172.3 0.8 copy-done.1
  173.1 2.6 %collective-permute-done.11.refs_1_ = bf16[4,384,512]{2,1,0:T(8,128)(2,1)} collective-permute-done((bf16[4,384,512]{2,1,0:T(8,128)(2,1)}, bf16[4,384,512]{2,1,0:T(8,128)(2,1)}, u32[]{:S(2)}, u32[]{:S(2)}) %collective-permute-start.11) | collective-permute-done | bytes 1572896 | tf_op jit(solution)/shard_map/ppermute | solution.py:46
  175.7 1.1 copy-done.2
  176.8 3.2 %pair.1 = (f32[384,512]{1,0:T(8,128)}, bf16[384,512]{1,0:T(8,128)(2,1)}, bf16[384,512]{1,0:T(8,128)(2,1)}, bf16[384,512]{1,0:T(8,128)(2,1)}) custom-call(bf16[4,384,512]{2,1,0:T(8,128)(2,1)} %get-tuple-element.97.refs_0_, bf16[4,384,512]{2,1,0:T(8,128)(2,1)} %collective-permute-done.11.refs_1_, bf16[576,512]{1,0:T(8,128)(2,1)S(1)} %copy-done.2), custom_call_target="tpu_custom_call" | custom-call | flops 1000 | bytes 1000 | tf_op jit(solution)/shard_map/pair/pallas_call | solution.py:213
  180.0 1.8 collective-permute-start.15
  181.8 1.6 collective-permute-start.16
  183.4 0.1 collective-permute-start.17
  183.5 0.0 all-reduce.2.cloned.1.call-update
  183.6 1.1 copy-done
  184.7 0.8 copy-done.11
  185.5 0.8 copy-done.14
  186.2 16.8 %back_up.1 = (f32[4,512,512]{2,1,0:T(8,128)}, f32[16,512]{1,0:T(8,128)S(1)}) custom-call(s32[4,1]{1,0:T(4,128)S(1)} %copy-done.17, bf16[4,544,1536]{2,1,0:T(8,128)(2,1)} %get-tuple-element.93.refs_1_, bf16[4,544,512]{2,1,0:T(8,128)(2,1)} %get-tuple-element.94.refs_2_, f32[4,544,1]{2,1,0:T(8,128)} %get-tuple-element.95.refs_3_, ...), custom_call_target="tpu_custom_call" | custom-call | flops 1000 | bytes 1000 | tf_op jit(solution)/shard_map/back_up/pallas_call | solution.py:195
  203.1 1.4 cross.1
  204.5 2.6 %collective-permute-start.18 = (bf16[96,512]{1,0:T(8,128)(2,1)S(1)}, bf16[96,512]{1,0:T(8,128)(2,1)S(1)}, u32[]{:S(2)}, u32[]{:S(2)}) collective-permute-start(bf16[96,512]{1,0:T(8,128)(2,1)S(1)} %get-tuple-element.113), channel_id=1, source_target_pairs={{0,1},{1,0},{2,3},{3,2},{4,5},{5,4},{6,7},{7,6},{8,9},{9,8},{10,11... | collective-permute-start | bytes 294920 | tf_op jit(solution)/shard_map/ppermute | solution.py:46
  207.1 2.6 %collective-permute-start.19 = (bf16[96,512]{1,0:T(8,128)(2,1)S(1)}, bf16[96,512]{1,0:T(8,128)(2,1)S(1)}, u32[]{:S(2)}, u32[]{:S(2)}) collective-permute-start(bf16[96,512]{1,0:T(8,128)(2,1)S(1)} %get-tuple-element.114), channel_id=1, source_target_pairs={{0,2},{1,3},{2,0},{3,1},{4,6},{5,7},{6,4},{7,5},{8,10},{9,11},{10,... | collective-permute-start | bytes 294920 | tf_op jit(solution)/shard_map/ppermute | solution.py:46
  209.7 9.3 %all-gather.1 = bf16[256,512]{1,0:T(8,128)(2,1)S(1)} all-gather(bf16[32,512]{1,0:T(8,128)(2,1)S(1)} %small.1.refs_4_), channel_id=3, replica_groups=mesh['dp'=8,'seq'=4] {'dp'}, dimensions={0}, use_global_device_ids=true | all-gather | bytes 294912 | tf_op jit(solution)/shard_map/all_gather | solution.py:1126
  218.9 1.1 collective-permute-done.19.refs_2_
  220.1 0.1 over_seq.1.refs_0_
  220.2 3.6 %collective-permute-start.23 = (bf16[128,512]{1,0:T(8,128)(2,1)S(1)}, bf16[128,512]{1,0:T(8,128)(2,1)S(1)}, u32[]{:S(2)}, u32[]{:S(2)}) collective-permute-start(bf16[128,512]{1,0:T(8,128)(2,1)S(1)} %over_seq.1.refs_0_), channel_id=1, source_target_pairs={{0,3},{1,2},{2,1},{3,0},{4,7},{5,6},{6,5},{7,4},{8,11},{9,10},{10,... | collective-permute-start | bytes 393224 | tf_op jit(solution)/shard_map/ppermute | solution.py:46
  223.8 9.8 %collective-permute-start.22 = (bf16[128,512]{1,0:T(8,128)(2,1)S(1)}, bf16[128,512]{1,0:T(8,128)(2,1)S(1)}, u32[]{:S(2)}, u32[]{:S(2)}) collective-permute-start(bf16[128,512]{1,0:T(8,128)(2,1)S(1)} %over_seq.1.refs_0_), channel_id=1, source_target_pairs={{0,2},{1,3},{2,0},{3,1},{4,6},{5,7},{6,4},{7,5},{8,10},{9,11},{10,... | collective-permute-start | bytes 393224 | tf_op jit(solution)/shard_map/ppermute | solution.py:46
  233.6 0.5 collective-permute-start.21
  234.1 3.9 %collective-permute-done.22.refs_2_ = bf16[128,512]{1,0:T(8,128)(2,1)S(1)} collective-permute-done((bf16[128,512]{1,0:T(8,128)(2,1)S(1)}, bf16[128,512]{1,0:T(8,128)(2,1)S(1)}, u32[]{:S(2)}, u32[]{:S(2)}) %collective-permute-start.22) | collective-permute-done | bytes 131104 | tf_op jit(solution)/shard_map/ppermute | solution.py:46
  238.0 1.3 collective-permute-done.21.refs_1_
  239.3 1.1 copy-done.7
  240.4 1.9 final.1
  242.2 0.6 reduce
  (66 shorter events, 0.2 us)
Async XLA Ops:
  7.2 62.4 %all-gather.4.cloned.1.call-start = ((), (), s32[]{:S(2)}) async-start(), calls=%async_computation.1 | async-start | bytes 5308416 | tf_op jit(solution)/shard_map/all_gather | solution.py:938
  7.2 12.3 %copy-start.27 = (s32[4,1]{0,1:T(1,128)S(1)}, s32[4,1]{0,1:T(1,128)}, u32[]{:S(2)}) copy-start(s32[4,1]{0,1:T(1,128)} %param.16) | copy-start | bytes 52
  7.2 12.4 %copy-start.26 = (f32[1026]{0:T(1024)S(1)}, f32[1026]{0:T(1024)}, u32[]{:S(2)}) copy-start(f32[1026]{0:T(1024)} %param.26) | copy-start | bytes 12316
  7.2 15.7 %copy-start.5 = (bf16[2,64,1536]{2,1,0:T(8,128)(2,1)S(1)}, bf16[2,64,1536]{2,1,0:T(8,128)(2,1)}, u32[]{:S(2)}) copy-start(bf16[2,64,1536]{2,1,0:T(8,128)(2,1)} %refs_4_.1) | copy-start | bytes 1179652
  7.3 15.7 %copy-start.6 = (bf16[2,192,512]{2,1,0:T(8,128)(2,1)S(1)}, bf16[2,192,512]{2,1,0:T(8,128)(2,1)}, u32[]{:S(2)}) copy-start(bf16[2,192,512]{2,1,0:T(8,128)(2,1)} %refs_5_.1) | copy-start | bytes 1179652
  7.3 20.0 %copy-start.4 = (bf16[1024,1024]{1,0:T(8,128)(2,1)S(1)}, bf16[1024,1024]{1,0:T(8,128)(2,1)}, u32[]{:S(2)}) copy-start(bf16[1024,1024]{1,0:T(8,128)(2,1)} %constant.5.clone.table_ref.table_hbm) | copy-start | bytes 6291460
  7.3 20.0 %copy-start.25 = (f32[4,256]{1,0:T(4,128)S(1)}, f32[4,256]{1,0:T(4,128)}, u32[]{:S(2)}) copy-start(f32[4,256]{1,0:T(4,128)} %constant.4.clone.squared_ref) | copy-start | bytes 12292
  9.8 13.2 %collective-permute-start = (bf16[4,16,768]{2,1,0:T(8,128)(2,1)}, bf16[4,16,768]{2,1,0:T(8,128)(2,1)S(1)}, u32[]{:S(2)}, u32[]{:S(2)}) collective-permute-start(bf16[4,16,768]{2,1,0:T(8,128)(2,1)} %get-tuple-element.69), channel_id=1, source_target_pairs={{0,1},{1,2},{2,3},{4,5},{5,6},{6,7},{8,9},{9,10},{10,11},{12,13},{... | collective-permute-start | bytes 294920 | tf_op jit(solution)/shard_map/ppermute | solution.py:936
  14.7 8.3 %collective-permute-start.1 = (bf16[4,16,768]{2,1,0:T(8,128)(2,1)}, bf16[4,16,768]{2,1,0:T(8,128)(2,1)S(1)}, u32[]{:S(2)}, u32[]{:S(2)}) collective-permute-start(bf16[4,16,768]{2,1,0:T(8,128)(2,1)} %get-tuple-element.70), channel_id=1, source_target_pairs={{1,0},{2,1},{3,2},{5,4},{6,5},{7,6},{9,8},{10,9},{11,10},{13,12},{... | collective-permute-start | bytes 294920 | tf_op jit(solution)/shard_map/ppermute | solution.py:937
  16.0 4.9 %collective-permute-start.4 = (bf16[16,512]{1,0:T(8,128)(2,1)}, bf16[16,512]{1,0:T(8,128)(2,1)S(1)}, u32[]{:S(2)}, u32[]{:S(2)}) collective-permute-start(bf16[16,512]{1,0:T(8,128)(2,1)} %get-tuple-element.71.refs_0_), channel_id=1, source_target_pairs={{0,24},{4,28},{8,16},{12,20},{16,8},{20,12},{24,0},{28,4},{1,25},{... | collective-permute-start | bytes 49160 | tf_op jit(solution)/shard_map/ppermute | solution.py:46
  18.5 4.0 %collective-permute-start.3 = (bf16[16,512]{1,0:T(8,128)(2,1)}, bf16[16,512]{1,0:T(8,128)(2,1)S(1)}, u32[]{:S(2)}, u32[]{:S(2)}) collective-permute-start(bf16[16,512]{1,0:T(8,128)(2,1)} %get-tuple-element.71.refs_0_), channel_id=1, source_target_pairs={{0,16},{4,20},{8,24},{12,28},{16,0},{20,4},{24,8},{28,12},{1,17},{... | collective-permute-start | bytes 49160 | tf_op jit(solution)/shard_map/ppermute | solution.py:46
  19.0 3.9 %collective-permute-start.2 = (bf16[16,512]{1,0:T(8,128)(2,1)}, bf16[16,512]{1,0:T(8,128)(2,1)S(1)}, u32[]{:S(2)}, u32[]{:S(2)}) collective-permute-start(bf16[16,512]{1,0:T(8,128)(2,1)} %get-tuple-element.71.refs_0_), channel_id=1, source_target_pairs={{0,8},{4,12},{8,0},{12,4},{16,24},{20,28},{24,16},{28,20},{1,9},{5... | collective-permute-start | bytes 49160 | tf_op jit(solution)/shard_map/ppermute | solution.py:46
  19.7 31.8 %copy-start.15 = (s32[4,1]{1,0:T(4,128)}, s32[4,1]{1,0:T(4,128)S(1)}, u32[]{:S(2)}) copy-start(s32[4,1]{1,0:T(4,128)S(1)} %copy.30.lengths.refs_0_) | copy-start | bytes 52
  23.0 0.7 copy-start.21
  23.7 23.7 %collective-permute-start.8 = (bf16[384,512]{1,0:T(8,128)(2,1)S(1)}, bf16[384,512]{1,0:T(8,128)(2,1)S(1)}, u32[]{:S(2)}, u32[]{:S(2)}) collective-permute-start(bf16[384,512]{1,0:T(8,128)(2,1)S(1)} %get-tuple-element.78.refs_0_), channel_id=1, source_target_pairs={{0,24},{4,28},{8,16},{12,20},{16,8},{20,12},{24,0},{28,4},{1,25},{... | collective-permute-start | bytes 1179656 | tf_op jit(solution)/shard_map/ppermute | solution.py:46
  25.3 22.2 %collective-permute-start.7 = (bf16[384,512]{1,0:T(8,128)(2,1)S(1)}, bf16[384,512]{1,0:T(8,128)(2,1)S(1)}, u32[]{:S(2)}, u32[]{:S(2)}) collective-permute-start(bf16[384,512]{1,0:T(8,128)(2,1)S(1)} %get-tuple-element.78.refs_0_), channel_id=1, source_target_pairs={{0,16},{4,20},{8,24},{12,28},{16,0},{20,4},{24,8},{28,12},{1,17},{... | collective-permute-start | bytes 1179656 | tf_op jit(solution)/shard_map/ppermute | solution.py:46
  25.8 21.7 %collective-permute-start.6 = (bf16[384,512]{1,0:T(8,128)(2,1)S(1)}, bf16[384,512]{1,0:T(8,128)(2,1)S(1)}, u32[]{:S(2)}, u32[]{:S(2)}) collective-permute-start(bf16[384,512]{1,0:T(8,128)(2,1)S(1)} %get-tuple-element.78.refs_0_), channel_id=1, source_target_pairs={{0,8},{4,12},{8,0},{12,4},{16,24},{20,28},{24,16},{28,20},{1,9},{5... | collective-permute-start | bytes 1179656 | tf_op jit(solution)/shard_map/ppermute | solution.py:46
  27.3 8.8 %collective-permute-start.5 = (bf16[4,16,512]{2,1,0:T(8,128)(2,1)S(1)}, bf16[4,16,512]{2,1,0:T(8,128)(2,1)S(1)}, u32[]{:S(2)}, u32[]{:S(2)}) collective-permute-start(bf16[4,16,512]{2,1,0:T(8,128)(2,1)S(1)} %get-tuple-element.72.refs_5_), channel_id=1, source_target_pairs={{0,4},{4,0},{8,12},{12,8},{16,20},{20,16},{24,28},{28,24},{1,5},{5... | collective-permute-start | bytes 196616 | tf_op jit(solution)/shard_map/ppermute | solution.py:46
  36.0 11.6 %copy-start.3 = (f32[544,256]{1,0:T(8,128)}, f32[544,256]{1,0:T(8,128)S(1)}, u32[]{:S(2)}) copy-start(f32[544,256]{1,0:T(8,128)S(1)} %get-tuple-element.73.refs_7_.recip_ref) | copy-start | bytes 1671172
  46.9 0.6 copy-start.23
  47.5 22.0 %copy-start.8 = (f32[16,1536]{1,0:T(8,128)}, f32[16,1536]{1,0:T(8,128)S(1)}, u32[]{:S(2)}) copy-start(f32[16,1536]{1,0:T(8,128)S(1)} %get-tuple-element.77.upb_ref) | copy-start | bytes 294916
  47.5 22.0 %copy-start.9 = (f32[16,512]{1,0:T(8,128)}, f32[16,512]{1,0:T(8,128)S(1)}, u32[]{:S(2)}) copy-start(f32[16,512]{1,0:T(8,128)S(1)} %get-tuple-element.79.refs_4_.taps_ref.refs_6_) | copy-start | bytes 98308
  47.5 22.0 %copy-start.12 = (f32[16,512]{1,0:T(8,128)}, f32[16,512]{1,0:T(8,128)S(1)}, u32[]{:S(2)}) copy-start(f32[16,512]{1,0:T(8,128)S(1)} %get-tuple-element.76.vec_ref.refs_9_.refs_7_) | copy-start | bytes 98308
  47.6 3.9 %collective-permute-start.9 = (bf16[4,384,512]{2,1,0:T(8,128)(2,1)S(1)}, bf16[4,384,512]{2,1,0:T(8,128)(2,1)S(1)}, u32[]{:S(2)}, u32[]{:S(2)}) collective-permute-start(bf16[4,384,512]{2,1,0:T(8,128)(2,1)S(1)} %stack_block0.1.even_ref.refs_10_.refs_8_), channel_id=1, source_target_pairs={{0,4},{4,0},{8,12},{12,8},{16,20},{20,16},{24,28},{28,24},{1,5},{5... | collective-permute-start | bytes 4718600 | tf_op jit(solution)/shard_map/ppermute | solution.py:46
  130.6 4.8 %collective-permute-start.10 = (bf16[4,576,512]{2,1,0:T(8,128)(2,1)}, bf16[4,576,512]{2,1,0:T(8,128)(2,1)S(1)}, u32[]{:S(2)}, u32[]{:S(2)}) collective-permute-start(bf16[4,576,512]{2,1,0:T(8,128)(2,1)} %get-tuple-element.91), channel_id=1, source_target_pairs={{0,4},{4,0},{8,12},{12,8},{16,20},{20,16},{24,28},{28,24},{1,5},{5... | collective-permute-start | bytes 7077896 | tf_op jit(solution)/shard_map/ppermute | solution.py:46
  135.4 6.9 %copy-start.10 = (f32[16,512]{1,0:T(8,128)S(1)}, f32[16,512]{1,0:T(8,128)}, u32[]{:S(2)}) copy-start(f32[16,512]{1,0:T(8,128)} %copy-done.9) | copy-start | bytes 98308
  135.4 6.9 %copy-start.13 = (f32[16,512]{1,0:T(8,128)S(1)}, f32[16,512]{1,0:T(8,128)}, u32[]{:S(2)}) copy-start(f32[16,512]{1,0:T(8,128)} %copy-done.12) | copy-start | bytes 98308
  135.4 6.9 %copy-start.16 = (s32[4,1]{1,0:T(4,128)S(1)}, s32[4,1]{1,0:T(4,128)}, u32[]{:S(2)}) copy-start(s32[4,1]{1,0:T(4,128)} %copy-done.15) | copy-start | bytes 52
  138.8 33.2 %collective-permute-start.12 = (bf16[576,512]{1,0:T(8,128)(2,1)}, bf16[576,512]{1,0:T(8,128)(2,1)S(1)}, u32[]{:S(2)}, u32[]{:S(2)}) collective-permute-start(bf16[576,512]{1,0:T(8,128)(2,1)} %get-tuple-element.99), channel_id=1, source_target_pairs={{0,8},{4,12},{8,0},{12,4},{16,24},{20,28},{24,16},{28,20},{1,9},{5... | collective-permute-start | bytes 1769480 | tf_op jit(solution)/shard_map/ppermute | solution.py:46
  140.6 31.4 %collective-permute-start.13 = (bf16[576,512]{1,0:T(8,128)(2,1)}, bf16[576,512]{1,0:T(8,128)(2,1)S(1)}, u32[]{:S(2)}, u32[]{:S(2)}) collective-permute-start(bf16[576,512]{1,0:T(8,128)(2,1)} %get-tuple-element.100), channel_id=1, source_target_pairs={{0,16},{4,20},{8,24},{12,28},{16,0},{20,4},{24,8},{28,12},{1,17},{... | collective-permute-start | bytes 1769480 | tf_op jit(solution)/shard_map/ppermute | solution.py:46
  142.2 29.8 %collective-permute-start.14 = (bf16[576,512]{1,0:T(8,128)(2,1)}, bf16[576,512]{1,0:T(8,128)(2,1)S(1)}, u32[]{:S(2)}, u32[]{:S(2)}) collective-permute-start(bf16[576,512]{1,0:T(8,128)(2,1)} %get-tuple-element.101), channel_id=1, source_target_pairs={{0,24},{4,28},{8,16},{12,20},{16,8},{20,12},{24,0},{28,4},{1,25},{... | collective-permute-start | bytes 1769480 | tf_op jit(solution)/shard_map/ppermute | solution.py:46
  142.3 1.3 copy-start.24
  171.4 0.6 copy-start.19
  172.0 3.8 %collective-permute-start.11 = (bf16[4,384,512]{2,1,0:T(8,128)(2,1)}, bf16[4,384,512]{2,1,0:T(8,128)(2,1)}, u32[]{:S(2)}, u32[]{:S(2)}) collective-permute-start(bf16[4,384,512]{2,1,0:T(8,128)(2,1)} %get-tuple-element.98), channel_id=1, source_target_pairs={{0,4},{4,0},{8,12},{12,8},{16,20},{20,16},{24,28},{28,24},{1,5},{5... | collective-permute-start | bytes 4718600 | tf_op jit(solution)/shard_map/ppermute | solution.py:46
  172.3 0.8 copy-start.1
  173.1 10.4 %copy-start.17 = (s32[4,1]{1,0:T(4,128)S(1)}, s32[4,1]{1,0:T(4,128)}, u32[]{:S(2)}) copy-start(s32[4,1]{1,0:T(4,128)} %copy-done.15) | copy-start | bytes 52
  175.7 1.1 copy-start.2
  180.0 54.1 %all-reduce.2.cloned.1.call-start = ((), (), s32[]{:S(2)}) async-start(), calls=%async_computation | async-start | bytes 1179648 | tf_op jit(solution)/shard_map/psum | solution.py:1103
  180.0 23.0 %collective-permute-start.15 = (bf16[384,512]{1,0:T(8,128)(2,1)}, bf16[384,512]{1,0:T(8,128)(2,1)S(1)}, u32[]{:S(2)}, u32[]{:S(2)}) collective-permute-start(bf16[384,512]{1,0:T(8,128)(2,1)} %get-tuple-element.105), channel_id=1, source_target_pairs={{0,8},{4,12},{8,0},{12,4},{16,24},{20,28},{24,16},{28,20},{1,9},{5... | collective-permute-start | bytes 1179656 | tf_op jit(solution)/shard_map/ppermute | solution.py:46
  181.8 21.3 %collective-permute-start.16 = (bf16[384,512]{1,0:T(8,128)(2,1)}, bf16[384,512]{1,0:T(8,128)(2,1)}, u32[]{:S(2)}, u32[]{:S(2)}) collective-permute-start(bf16[384,512]{1,0:T(8,128)(2,1)} %get-tuple-element.106), channel_id=1, source_target_pairs={{0,16},{4,20},{8,24},{12,28},{16,0},{20,4},{24,8},{28,12},{1,17},{... | collective-permute-start | bytes 1179656 | tf_op jit(solution)/shard_map/ppermute | solution.py:46
  183.4 19.7 %collective-permute-start.17 = (bf16[384,512]{1,0:T(8,128)(2,1)}, bf16[384,512]{1,0:T(8,128)(2,1)}, u32[]{:S(2)}, u32[]{:S(2)}) collective-permute-start(bf16[384,512]{1,0:T(8,128)(2,1)} %get-tuple-element.107), channel_id=1, source_target_pairs={{0,24},{4,28},{8,16},{12,20},{16,8},{20,12},{24,0},{28,4},{1,25},{... | collective-permute-start | bytes 1179656 | tf_op jit(solution)/shard_map/ppermute | solution.py:46
  183.6 1.1 copy-start
  184.7 0.8 copy-start.11
  185.5 0.8 copy-start.14
  186.2 16.8 %copy-start.18 = (f32[16,512]{1,0:T(8,128)S(1)}, f32[16,512]{1,0:T(8,128)}, u32[]{:S(2)}) copy-start(f32[16,512]{1,0:T(8,128)} %get-tuple-element.110.mid_ref) | copy-start | bytes 98308
  186.2 16.8 %copy-start.20 = (f32[16,512]{1,0:T(8,128)S(1)}, f32[16,512]{1,0:T(8,128)}, u32[]{:S(2)}) copy-start(f32[16,512]{1,0:T(8,128)} %copy-done.19) | copy-start | bytes 98308
  186.2 16.8 %copy-start.22 = (f32[1,1536]{1,0:T(1,128)S(1)}, f32[1,1536]{1,0:T(1,128)}, u32[]{:S(2)}) copy-start(f32[1,1536]{1,0:T(1,128)} %get-tuple-element.111.bias1_ref) | copy-start | bytes 18436
  204.5 14.4 %collective-permute-start.18 = (bf16[96,512]{1,0:T(8,128)(2,1)S(1)}, bf16[96,512]{1,0:T(8,128)(2,1)S(1)}, u32[]{:S(2)}, u32[]{:S(2)}) collective-permute-start(bf16[96,512]{1,0:T(8,128)(2,1)S(1)} %get-tuple-element.113), channel_id=1, source_target_pairs={{0,1},{1,0},{2,3},{3,2},{4,5},{5,4},{6,7},{7,6},{8,9},{9,8},{10,11... | collective-permute-start | bytes 294920 | tf_op jit(solution)/shard_map/ppermute | solution.py:46
  207.1 13.0 %collective-permute-start.19 = (bf16[96,512]{1,0:T(8,128)(2,1)S(1)}, bf16[96,512]{1,0:T(8,128)(2,1)S(1)}, u32[]{:S(2)}, u32[]{:S(2)}) collective-permute-start(bf16[96,512]{1,0:T(8,128)(2,1)S(1)} %get-tuple-element.114), channel_id=1, source_target_pairs={{0,2},{1,3},{2,0},{3,1},{4,6},{5,7},{6,4},{7,5},{8,10},{9,11},{10,... | collective-permute-start | bytes 294920 | tf_op jit(solution)/shard_map/ppermute | solution.py:46
  209.7 10.4 %collective-permute-start.20 = (bf16[96,512]{1,0:T(8,128)(2,1)S(1)}, bf16[96,512]{1,0:T(8,128)(2,1)S(1)}, u32[]{:S(2)}, u32[]{:S(2)}) collective-permute-start(bf16[96,512]{1,0:T(8,128)(2,1)S(1)} %get-tuple-element.115), channel_id=1, source_target_pairs={{0,3},{1,2},{2,1},{3,0},{4,7},{5,6},{6,5},{7,4},{8,11},{9,10},{10,... | collective-permute-start | bytes 294920 | tf_op jit(solution)/shard_map/ppermute | solution.py:46
  220.2 14.0 %collective-permute-start.23 = (bf16[128,512]{1,0:T(8,128)(2,1)S(1)}, bf16[128,512]{1,0:T(8,128)(2,1)S(1)}, u32[]{:S(2)}, u32[]{:S(2)}) collective-permute-start(bf16[128,512]{1,0:T(8,128)(2,1)S(1)} %over_seq.1.refs_0_), channel_id=1, source_target_pairs={{0,3},{1,2},{2,1},{3,0},{4,7},{5,6},{6,5},{7,4},{8,11},{9,10},{10,... | collective-permute-start | bytes 393224 | tf_op jit(solution)/shard_map/ppermute | solution.py:46
  223.8 14.2 %collective-permute-start.22 = (bf16[128,512]{1,0:T(8,128)(2,1)S(1)}, bf16[128,512]{1,0:T(8,128)(2,1)S(1)}, u32[]{:S(2)}, u32[]{:S(2)}) collective-permute-start(bf16[128,512]{1,0:T(8,128)(2,1)S(1)} %over_seq.1.refs_0_), channel_id=1, source_target_pairs={{0,2},{1,3},{2,0},{3,1},{4,6},{5,7},{6,4},{7,5},{8,10},{9,11},{10,... | collective-permute-start | bytes 393224 | tf_op jit(solution)/shard_map/ppermute | solution.py:46
  233.6 5.7 %collective-permute-start.21 = (bf16[128,512]{1,0:T(8,128)(2,1)S(1)}, bf16[128,512]{1,0:T(8,128)(2,1)S(1)}, u32[]{:S(2)}, u32[]{:S(2)}) collective-permute-start(bf16[128,512]{1,0:T(8,128)(2,1)S(1)} %over_seq.1.refs_0_), channel_id=1, source_target_pairs={{0,1},{1,0},{2,3},{3,2},{4,5},{5,4},{6,7},{7,6},{8,9},{9,8},{10,11... | collective-permute-start | bytes 393224 | tf_op jit(solution)/shard_map/ppermute | solution.py:46
  239.3 1.1 copy-start.7
Sparse Core Ops, SparseCore 0:
  10.5 53.3 all-gather.3
  183.8 49.4 all-reduce.1

commit v4 on v3

--- a/solution.py
+++ b/solution.py
@@ -25,8 +25,8 @@
 cols_dims = (((1,), (1,)), ((), ()))
 MiB = 2**20
 GELU = (0.7978202661111929, 0.03654664812915587, -0.00019444764679970054, -1.3688682486738934e-05)
-SIN = (6.283184921107194, -41.34159015596926, 81.59997289449204, -76.61480381354174, 41.34439732745281, -12.473668162531846)
-COS = (0.9999992215705861, -19.738982516102407, 64.92872660899411, -85.27239689575316, 58.79403819232432, -21.076781286284348)
+SIN = (3.1415902835876266, -5.16740769757772, 2.544020809221036, -0.5594899050493729)
+COS = (1.9999999069332557, -9.869585717340266, 8.116823828128622, -2.6637603211811274, 0.43939359457288596)
 
 
 def window_values():
@@ -87,7 +87,8 @@
     r = x * (1.0 / (2.0 * math.pi))
     r = r - jnp.floor(r + 0.5)
     z = r * r
-    return poly(z, COS), r * poly(z, SIN)
+    half = r * poly(z, SIN)
+    return 1.0 - 2.0 * (half * half), half * poly(z, COS)
 
 
 class Frames:
@@ -205,7 +206,7 @@
         compiler_params=pltpu.CompilerParams(vmem_limit_bytes=limit * MiB, dimension_semantics=("arbitrary",)),
         cost_estimate=cost(us),
         name=name,
-    )(lengths, *[in_hbm(a) if kind == "rows" and a.shape[1] != HALO else a for a, kind in ins])
+    )(lengths, *[a if kind == "any" or a.shape[1] == HALO else in_hbm(a) for a, kind in ins])
 
 
 def simple_call(kernel, ins, outs, name, scratch=(), after=(), limit=16, us=0, hbm=(), out_hbm=False):
@@ -557,13 +558,15 @@
             top = jnp.exp(jnp.where(lane == 0, last, 0.0))
             top_re = top * cos
             top_im = top * sin
-            spectrum_ref[r : r + 16, :HALF] = re.astype(low)
+            re = re.astype(low)
+            spectrum_ref[r : r + 16, :HALF] = re
             spectrum_ref[r : r + 16, HALF : HALF + EXTRA] = jnp.where(lane == 0, top_re, im[:, :EXTRA]).astype(low)
-            spectrum_ref[r : r + 16, HALF + EXTRA :] = im[:, EXTRA:].astype(low)
-            tgrad = tgrad_ref[0, r : r + 16].astype(f32)
-            re_grad = tgrad[:, :HALF]
-            top_grad = tgrad[:, HALF : HALF + EXTRA]
-            im_grad = jnp.concatenate([jnp.where(lane == 0, 0.0, top_grad), tgrad[:, HALF + EXTRA :]], axis=1)
+            im = im.astype(low)
+            spectrum_ref[r : r + 16, HALF + EXTRA :] = im[:, EXTRA:]
+            re_grad = tgrad_ref[0, r : r + 16, :HALF]
+            top_grad = tgrad_ref[0, r : r + 16, HALF : HALF + EXTRA].astype(f32)
+            im_first = jnp.where(lane == 0, 0.0, top_grad).astype(low)
+            im_grad = jnp.concatenate([im_first, tgrad_ref[0, r : r + 16, HALF + EXTRA :]], axis=1)
             log_last = jnp.where(lane == 0, top_grad * top_re, 0.0)
             phase_last = jnp.where(lane == 1, pltpu.roll(top_grad * top_im, 1, 1), 0.0)
             grads = (re_grad * re + im_grad * im, im_grad * re - re_grad * im, log_last - phase_last)
@@ -1008,6 +1011,7 @@
         ],
         scratch=[pltpu.VMEM((width, units), low), pltpu.VMEM((units, width), low), dma(count, units // HALF), dma(count, 1)],
         name="forward",
+        limit=60,
     )
     hidden, act, slope, branch = (x.reshape(micro, ext, -1) for x in (hidden, act, slope, branch))
     packed = 3 * own + size + grouped
@@ -1098,6 +1102,7 @@
         after=[kept1],
         us=20,
         name="back_down",
+        limit=60,
     )
     shard1 = add_all([kept1] + recvs1, low, "late_cross", after=[sbias0], us=200)
     late = lax.psum(shard1, "seq")
@@ -1118,6 +1123,7 @@
         scratch=[pltpu.VMEM((width, units), low), pltpu.VMEM((ext + 16, width), f32), pltpu.VMEM((128, width), f32), dma(count, units // HALF)],
         after=[kept],
         name="back_up",
+        limit=60,
     )
     (smalls,) = simple_call(
         small_kernel, [small_conv, small_down, sbias0, small_mid, sbias1], [((SMALL, width), low)], "small"

time: 250 us -> 246 us (0.984)
  local copies, waits for them, and re-layouts: 8.93 us -> 5.14 us
    unnamed x57 -> x45, local copies, waits for them, and re-layouts: 8.93 us -> 4.54 us
  transfers between devices with their start and end apart: 26 -> 26, of which waited for: 9 -> 9; matrix products, arithmetic and copies ran while one was open for 0% -> 0% of each run, Pallas kernels for 34% -> 35%
where the time goes in v4:
time: 246 us; the launch traced here: 245 us
  Pallas kernels  157 us (64%)
  starting transfers between devices  38.8 us (16%)
  waiting for transfers between devices  20 us (8%)
  between operations  14.5 us (6%)
  blocking collectives  9.3 us (4%)
  local copies, waits for them, and re-layouts  5.14 us (2%)
    pallas_call x6, Pallas kernels, call(): pl.pallas_call(kernel, out_shape=[(pltpu.HBM if kind == 'rows' or len(s)...  145 us
    ppermute x22, starting transfers between devices, swap(): lax.ppermute(x, axis, [(i, i ^ d) for i in range(lax.axis_size(axis))])  32.5 us
    ppermute x22, waiting for transfers between devices, swap(): lax.ppermute(x, axis, [(i, i ^ d) for i in range(lax.axis_size(axis))])  19 us
    pallas_call x9, Pallas kernels, simple_call(): pl.pallas_call(skipping(kernel, len(ins), len(after)), out_shape=[(pltpu....  10.2 us
    all_gather x1, blocking collectives, per_device(): small_all = lax.all_gather(smalls, 'dp', axis=0)  9.3 us
    ppermute x1, starting transfers between devices, per_device(): lax.ppermute(last, 'seq', [(i, i + 1) for i in range(seq_count - 1)])  4.93 us
  transfers between devices with their start and end apart: 26, of which 9 were waited for; matrix products, arithmetic and copies ran while one was open for 0% of the time, Pallas kernels for 35%

profile of v4, /device:TPU:0, one launch (start us, length us, event | category | flops | bytes accessed | tf_op | source)
XLA Modules:
  0.0 245.4 jit_solution(12543503433742027985)
XLA Ops:
  7.2 0.0 all-gather.4.cloned.1.call-start
  7.3 2.4 pack.1
  9.7 0.0 all-gather.4.cloned.1.call-update
  9.7 4.9 %collective-permute-start = (bf16[4,16,768]{2,1,0:T(8,128)(2,1)}, bf16[4,16,768]{2,1,0:T(8,128)(2,1)S(1)}, u32[]{:S(2)}, u32[]{:S(2)}) collective-permute-start(bf16[4,16,768]{2,1,0:T(8,128)(2,1)} %get-tuple-element.69), channel_id=1, source_target_pairs={{0,1},{1,2},{2,3},{4,5},{5,6},{6,7},{8,9},{9,10},{10,11},{12,13},{... | collective-permute-start | bytes 294920 | tf_op jit(solution)/shard_map/ppermute | solution.py:939
  14.6 1.3 collective-permute-start.1
  15.9 2.5 %collective-permute-start.4 = (bf16[16,512]{1,0:T(8,128)(2,1)}, bf16[16,512]{1,0:T(8,128)(2,1)S(1)}, u32[]{:S(2)}, u32[]{:S(2)}) collective-permute-start(bf16[16,512]{1,0:T(8,128)(2,1)} %get-tuple-element.71.refs_0_), channel_id=1, source_target_pairs={{0,24},{4,28},{8,16},{12,20},{16,8},{20,12},{24,0},{28,4},{1,25},{... | collective-permute-start | bytes 49160 | tf_op jit(solution)/shard_map/ppermute | solution.py:46
  18.4 0.5 collective-permute-start.3
  19.0 0.5 collective-permute-start.2
  19.5 0.1 copy.30.lengths.refs_0_
  19.6 0.6 broadcast_in_dim.17.refs_4_
  20.2 0.7 collective-permute-done.4.refs_3_
  20.9 1.5 collective-permute-done.3.refs_2_
  22.4 0.5 collective-permute-done.2.refs_1_
  22.9 0.0 copy-start.13
  22.9 0.7 copy-done.13
  23.7 1.6 collective-permute-start.8
  25.2 0.5 collective-permute-start.7
  25.7 1.5 collective-permute-start.6
  27.2 9.5 %dft.1 = (bf16[4,544,1024]{2,1,0:T(8,128)(2,1)}, f32[544,256]{1,0:T(8,128)S(1)}) custom-call(s32[4,1]{1,0:T(4,128)S(1)} %copy.30.lengths.refs_0_, bf16[4,16,768]{2,1,0:T(8,128)(2,1)S(1)} %collective-permute-done.refs_6_.before_ref.refs_1_, f32[4,512,256]{2,1,0:T(8,128)} %bitcast.31, bf16[4,16,768]{2,1,0:T(8,128)(2,1)S(1)} %collective-permute-done.1.refs_7_.after_ref.refs_3_, ...), custom_call_target="tpu_custom_call" | custom-call | flops 20000000000 | bytes 1000 | tf_op jit(solution)/shard_map/dft/pallas_call | solution.py:196
  36.7 10.8 %conv.1 = (bf16[4,544,512]{2,1,0:T(8,128)(2,1)}, bf16[4,544,512]{2,1,0:T(8,128)(2,1)}, f32[4,544,1]{2,1,0:T(8,128)}, bf16[4,544,512]{2,1,0:T(8,128)(2,1)}, f32[1...) custom-call(s32[4,1]{1,0:T(4,128)S(1)} %copy.30.lengths.refs_0_, ...), custom_call_target="tpu_custom_call" | custom-call | flops 1000 | bytes 1000 | tf_op jit(solution)/shard_map/conv/pallas_call | solution.py:196
  47.6 0.0 copy-start.6
  47.6 0.0 copy-start.17
  47.6 0.1 stack_block0.1.even_ref.refs_10_.refs_8_
  47.8 0.6 collective-permute-start.9
  48.3 3.2 %collective-permute-done.9.odd_ref.refs_11_.refs_9_ = bf16[4,384,512]{2,1,0:T(8,128)(2,1)S(1)} collective-permute-done((bf16[4,384,512]{2,1,0:T(8,128)(2,1)S(1)}, bf16[4,384,512]{2,1,0:T(8,128)(2,1)S(1)}, u32[]{:S(2)}, u32[]{:S(2)}) %collective-permute-start.9) | collective-permute-done | bytes 1572896 | tf_op jit(solution)/shard_map/ppermute | solution.py:46
  51.6 1.1 copy-done.19
  52.7 17.6 %forward.1 = (f32[8,272,512]{2,1,0:T(8,128)}, bf16[8,272,1536]{2,1,0:T(8,128)(2,1)}, bf16[8,272,1536]{2,1,0:T(8,128)(2,1)}, bf16[8,272,512]{2,1,0:T(8,128)(2,1)}) custom-call(s32[4,1]{1,0:T(4,128)} %copy-done.9, bf16[8,272,512]{2,1,0:T(8,128)(2,1)} %bitcast.36, bf16[8,272,512]{2,1,0:T(8,128)(2,1)} %bitcast.35, f32[16,512]{1,0:T(8,128)} %copy-done.8, ...), custom_call_target="tpu_custom_call" | custom-call | flops 1000 | bytes 1000 | tf_op jit(solution)/shard_map/forward/pallas_call | solution.py:196
  70.4 0.0 all-gather.4.cloned.1.call-done
  70.4 60.4 %middle.1 = (f32[4,512,256]{2,1,0:T(8,128)}, f32[4,544,512]{2,1,0:T(8,128)}, bf16[4,544,512]{2,1,0:T(8,128)(2,1)}, bf16[4,576,512]{2,1,0:T(8,128)(2,1)}, bf16[4,...) custom-call(s32[4,1]{1,0:T(4,128)} %copy-done.9, f32[4,544,512]{2,1,0:T(8,128)} %bitcast.33, ...), custom_call_target="tpu_custom_call" | custom-call | flops 1000 | bytes 1000 | tf_op jit(solution)/shard_map/middle/pallas_call | solution.py:196
  130.8 0.2 collective-permute-start.10
  131.0 4.6 %collective-permute-done.10.recv_ref = bf16[4,576,512]{2,1,0:T(8,128)(2,1)S(1)} collective-permute-done((bf16[4,576,512]{2,1,0:T(8,128)(2,1)}, bf16[4,576,512]{2,1,0:T(8,128)(2,1)S(1)}, u32[]{:S(2)}, u32[]{:S(2)}) %collective-permute-start.10) | collective-permute-done | bytes 2359328 | tf_op jit(solution)/shard_map/ppermute | solution.py:46
  135.6 3.4 %late_pair.1 = (f32[576,512]{1,0:T(8,128)}, bf16[576,512]{1,0:T(8,128)(2,1)}, bf16[576,512]{1,0:T(8,128)(2,1)}, bf16[576,512]{1,0:T(8,128)(2,1)}) custom-call(bf16[4,576,512]{2,1,0:T(8,128)(2,1)} %get-tuple-element.90.keep_ref, bf16[4,576,512]{2,1,0:T(8,128)(2,1)S(1)} %collective-permute-done.10.recv_ref), custom_call_target="tpu_custom_call" | custom-call | flops 1000 | bytes 1000 | tf_op jit(solution)/shard_map/late_pair/pallas_call | solution.py:214
  139.0 1.7 collective-permute-start.12
  140.7 1.5 collective-permute-start.13
  142.2 0.3 collective-permute-start.14
  142.5 27.9 %back_down.1 = (bf16[4,544,1536]{2,1,0:T(8,128)(2,1)}, f32[4,544,512]{2,1,0:T(8,128)}, bf16[4,384,512]{2,1,0:T(8,128)(2,1)}, bf16[4,384,512]{2,1,0:T(8,128)(2,1)}, f32[16,512]{1,0:T(8,128)}, /*index=5*/f32[1,1536]{1,0:T(1,128)}) custom-call(s32[4,1]{1,0:T(4,128)} %copy-done.9, f32[4,544,512]{2,1,0:T(8,128)} %get-tuple-element.85.refs_1_, ...), custom_call_target="tpu_custom_call" | custom-call | flops 20000000000 | bytes 1000 | tf_op jit(solution)/shard_map/back_down/pallas_call | solution.py:196
  170.4 0.1 collective-permute-start.11
  170.5 0.0 copy-start.15
  170.6 0.7 copy-done.15
  171.2 1.1 late_cross.1.refs_2_
  172.3 1.9 collective-permute-done.11.refs_1_
  174.2 3.3 %pair.1 = (f32[384,512]{1,0:T(8,128)}, bf16[384,512]{1,0:T(8,128)(2,1)}, bf16[384,512]{1,0:T(8,128)(2,1)}, bf16[384,512]{1,0:T(8,128)(2,1)}) custom-call(bf16[4,384,512]{2,1,0:T(8,128)(2,1)} %get-tuple-element.97.refs_0_, bf16[4,384,512]{2,1,0:T(8,128)(2,1)} %collective-permute-done.11.refs_1_, bf16[576,512]{1,0:T(8,128)(2,1)} %late_cross.1.refs_2_), custom_call_target="tpu_custom_call" | custom-call | flops 1000 | bytes 1000 | tf_op jit(solution)/shard_map/pair/pallas_call | solution.py:214
  177.5 1.7 collective-permute-start.15
  179.2 1.5 collective-permute-start.16
  180.7 0.3 collective-permute-start.17
  181.0 0.0 all-reduce.2.cloned.1.call-update
  181.0 0.0 copy-start.11
  181.0 0.0 copy-start.14
  181.1 18.3 %back_up.1 = (f32[4,512,512]{2,1,0:T(8,128)}, f32[16,512]{1,0:T(8,128)}) custom-call(s32[4,1]{1,0:T(4,128)} %copy-done.9, bf16[4,544,1536]{2,1,0:T(8,128)(2,1)} %get-tuple-element.93.refs_1_, bf16[4,544,512]{2,1,0:T(8,128)(2,1)} %get-tuple-element.94.refs_2_, f32[4,544,1]{2,1,0:T(8,128)} %get-tuple-element.95.refs_3_, bf16[4,512,512]{2,1,0:T(8,128)(2,1)} %bitcast.28, ...), custom_call_target="tpu_custom_call" | custom-call | flops 1000 | bytes 1000 | tf_op jit(solution)/shard_map/back_up/pallas_call | solution.py:196
  199.5 0.7 copy-done.12
  200.3 0.3 cross.1
  200.6 2.7 %collective-permute-start.18 = (bf16[96,512]{1,0:T(8,128)(2,1)S(1)}, bf16[96,512]{1,0:T(8,128)(2,1)S(1)}, u32[]{:S(2)}, u32[]{:S(2)}) collective-permute-start(bf16[96,512]{1,0:T(8,128)(2,1)S(1)} %get-tuple-element.113), channel_id=1, source_target_pairs={{0,1},{1,0},{2,3},{3,2},{4,5},{5,4},{6,7},{7,6},{8,9},{9,8},{10,11... | collective-permute-start | bytes 294920 | tf_op jit(solution)/shard_map/ppermute | solution.py:46
  203.3 2.5 %collective-permute-start.19 = (bf16[96,512]{1,0:T(8,128)(2,1)S(1)}, bf16[96,512]{1,0:T(8,128)(2,1)S(1)}, u32[]{:S(2)}, u32[]{:S(2)}) collective-permute-start(bf16[96,512]{1,0:T(8,128)(2,1)S(1)} %get-tuple-element.114), channel_id=1, source_target_pairs={{0,2},{1,3},{2,0},{3,1},{4,6},{5,7},{6,4},{7,5},{8,10},{9,11},{10,... | collective-permute-start | bytes 294920 | tf_op jit(solution)/shard_map/ppermute | solution.py:46
  205.8 9.3 %all-gather.1 = bf16[256,512]{1,0:T(8,128)(2,1)S(1)} all-gather(bf16[32,512]{1,0:T(8,128)(2,1)S(1)} %small.1.refs_4_), channel_id=3, replica_groups=mesh['dp'=8,'seq'=4] {'dp'}, dimensions={0}, use_global_device_ids=true | all-gather | bytes 294912 | tf_op jit(solution)/shard_map/all_gather | solution.py:1132
  215.1 1.0 collective-permute-done.19.refs_2_
  216.1 0.1 over_seq.1.refs_0_
  216.2 3.8 %collective-permute-start.23 = (bf16[128,512]{1,0:T(8,128)(2,1)S(1)}, bf16[128,512]{1,0:T(8,128)(2,1)S(1)}, u32[]{:S(2)}, u32[]{:S(2)}) collective-permute-start(bf16[128,512]{1,0:T(8,128)(2,1)S(1)} %over_seq.1.refs_0_), channel_id=1, source_target_pairs={{0,3},{1,2},{2,1},{3,0},{4,7},{5,6},{6,5},{7,4},{8,11},{9,10},{10,... | collective-permute-start | bytes 393224 | tf_op jit(solution)/shard_map/ppermute | solution.py:46
  220.0 8.1 %collective-permute-start.22 = (bf16[128,512]{1,0:T(8,128)(2,1)S(1)}, bf16[128,512]{1,0:T(8,128)(2,1)S(1)}, u32[]{:S(2)}, u32[]{:S(2)}) collective-permute-start(bf16[128,512]{1,0:T(8,128)(2,1)S(1)} %over_seq.1.refs_0_), channel_id=1, source_target_pairs={{0,2},{1,3},{2,0},{3,1},{4,6},{5,7},{6,4},{7,5},{8,10},{9,11},{10,... | collective-permute-start | bytes 393224 | tf_op jit(solution)/shard_map/ppermute | solution.py:46
  228.1 0.5 collective-permute-start.21
  228.6 0.9 all-reduce.2.cloned.1.call-done.late_ref
  229.5 5.5 %collective-permute-done.22.refs_2_ = bf16[128,512]{1,0:T(8,128)(2,1)S(1)} collective-permute-done((bf16[128,512]{1,0:T(8,128)(2,1)S(1)}, bf16[128,512]{1,0:T(8,128)(2,1)S(1)}, u32[]{:S(2)}, u32[]{:S(2)}) %collective-permute-start.22) | collective-permute-done | bytes 131104 | tf_op jit(solution)/shard_map/ppermute | solution.py:46
  235.0 1.1 copy-done.5
  236.0 1.9 final.1
  237.9 0.6 reduce
  (54 shorter events, 0.2 us)
Async XLA Ops:
  7.2 63.2 %all-gather.4.cloned.1.call-start = ((), (), s32[]{:S(2)}) async-start(), calls=%async_computation.1 | async-start | bytes 5308416 | tf_op jit(solution)/shard_map/all_gather | solution.py:941
  7.2 12.3 %copy-start.21 = (s32[4,1]{0,1:T(1,128)S(1)}, s32[4,1]{0,1:T(1,128)}, u32[]{:S(2)}) copy-start(s32[4,1]{0,1:T(1,128)} %param.16) | copy-start | bytes 52
  7.2 12.3 %copy-start.20 = (f32[1026]{0:T(1024)S(1)}, f32[1026]{0:T(1024)}, u32[]{:S(2)}) copy-start(f32[1026]{0:T(1024)} %param.26) | copy-start | bytes 12316
  7.2 15.7 %copy-start.3 = (bf16[2,64,1536]{2,1,0:T(8,128)(2,1)S(1)}, bf16[2,64,1536]{2,1,0:T(8,128)(2,1)}, u32[]{:S(2)}) copy-start(bf16[2,64,1536]{2,1,0:T(8,128)(2,1)} %refs_4_.1) | copy-start | bytes 1179652
  7.3 15.7 %copy-start.4 = (bf16[2,192,512]{2,1,0:T(8,128)(2,1)S(1)}, bf16[2,192,512]{2,1,0:T(8,128)(2,1)}, u32[]{:S(2)}) copy-start(bf16[2,192,512]{2,1,0:T(8,128)(2,1)} %refs_5_.1) | copy-start | bytes 1179652
  9.7 13.2 %collective-permute-start = (bf16[4,16,768]{2,1,0:T(8,128)(2,1)}, bf16[4,16,768]{2,1,0:T(8,128)(2,1)S(1)}, u32[]{:S(2)}, u32[]{:S(2)}) collective-permute-start(bf16[4,16,768]{2,1,0:T(8,128)(2,1)} %get-tuple-element.69), channel_id=1, source_target_pairs={{0,1},{1,2},{2,3},{4,5},{5,6},{6,7},{8,9},{9,10},{10,11},{12,13},{... | collective-permute-start | bytes 294920 | tf_op jit(solution)/shard_map/ppermute | solution.py:939
  14.6 8.3 %collective-permute-start.1 = (bf16[4,16,768]{2,1,0:T(8,128)(2,1)}, bf16[4,16,768]{2,1,0:T(8,128)(2,1)S(1)}, u32[]{:S(2)}, u32[]{:S(2)}) collective-permute-start(bf16[4,16,768]{2,1,0:T(8,128)(2,1)} %get-tuple-element.70), channel_id=1, source_target_pairs={{1,0},{2,1},{3,2},{5,4},{6,5},{7,6},{9,8},{10,9},{11,10},{13,12},{... | collective-permute-start | bytes 294920 | tf_op jit(solution)/shard_map/ppermute | solution.py:940
  15.9 4.9 %collective-permute-start.4 = (bf16[16,512]{1,0:T(8,128)(2,1)}, bf16[16,512]{1,0:T(8,128)(2,1)S(1)}, u32[]{:S(2)}, u32[]{:S(2)}) collective-permute-start(bf16[16,512]{1,0:T(8,128)(2,1)} %get-tuple-element.71.refs_0_), channel_id=1, source_target_pairs={{0,24},{4,28},{8,16},{12,20},{16,8},{20,12},{24,0},{28,4},{1,25},{... | collective-permute-start | bytes 49160 | tf_op jit(solution)/shard_map/ppermute | solution.py:46
  18.4 3.9 %collective-permute-start.3 = (bf16[16,512]{1,0:T(8,128)(2,1)}, bf16[16,512]{1,0:T(8,128)(2,1)S(1)}, u32[]{:S(2)}, u32[]{:S(2)}) collective-permute-start(bf16[16,512]{1,0:T(8,128)(2,1)} %get-tuple-element.71.refs_0_), channel_id=1, source_target_pairs={{0,16},{4,20},{8,24},{12,28},{16,0},{20,4},{24,8},{28,12},{1,17},{... | collective-permute-start | bytes 49160 | tf_op jit(solution)/shard_map/ppermute | solution.py:46
  19.0 3.9 %collective-permute-start.2 = (bf16[16,512]{1,0:T(8,128)(2,1)}, bf16[16,512]{1,0:T(8,128)(2,1)S(1)}, u32[]{:S(2)}, u32[]{:S(2)}) collective-permute-start(bf16[16,512]{1,0:T(8,128)(2,1)} %get-tuple-element.71.refs_0_), channel_id=1, source_target_pairs={{0,8},{4,12},{8,0},{12,4},{16,24},{20,28},{24,16},{28,20},{1,9},{5... | collective-permute-start | bytes 49160 | tf_op jit(solution)/shard_map/ppermute | solution.py:46
  19.6 17.1 %copy-start.9 = (s32[4,1]{1,0:T(4,128)}, s32[4,1]{1,0:T(4,128)S(1)}, u32[]{:S(2)}) copy-start(s32[4,1]{1,0:T(4,128)S(1)} %copy.30.lengths.refs_0_) | copy-start | bytes 52
  22.9 0.7 copy-start.13
  23.7 23.9 %collective-permute-start.8 = (bf16[384,512]{1,0:T(8,128)(2,1)S(1)}, bf16[384,512]{1,0:T(8,128)(2,1)S(1)}, u32[]{:S(2)}, u32[]{:S(2)}) collective-permute-start(bf16[384,512]{1,0:T(8,128)(2,1)S(1)} %get-tuple-element.78.refs_0_), channel_id=1, source_target_pairs={{0,24},{4,28},{8,16},{12,20},{16,8},{20,12},{24,0},{28,4},{1,25},{... | collective-permute-start | bytes 1179656 | tf_op jit(solution)/shard_map/ppermute | solution.py:46
  25.2 22.4 %collective-permute-start.7 = (bf16[384,512]{1,0:T(8,128)(2,1)S(1)}, bf16[384,512]{1,0:T(8,128)(2,1)S(1)}, u32[]{:S(2)}, u32[]{:S(2)}) collective-permute-start(bf16[384,512]{1,0:T(8,128)(2,1)S(1)} %get-tuple-element.78.refs_0_), channel_id=1, source_target_pairs={{0,16},{4,20},{8,24},{12,28},{16,0},{20,4},{24,8},{28,12},{1,17},{... | collective-permute-start | bytes 1179656 | tf_op jit(solution)/shard_map/ppermute | solution.py:46
  25.7 21.9 %collective-permute-start.6 = (bf16[384,512]{1,0:T(8,128)(2,1)S(1)}, bf16[384,512]{1,0:T(8,128)(2,1)S(1)}, u32[]{:S(2)}, u32[]{:S(2)}) collective-permute-start(bf16[384,512]{1,0:T(8,128)(2,1)S(1)} %get-tuple-element.78.refs_0_), channel_id=1, source_target_pairs={{0,8},{4,12},{8,0},{12,4},{16,24},{20,28},{24,16},{28,20},{1,9},{5... | collective-permute-start | bytes 1179656 | tf_op jit(solution)/shard_map/ppermute | solution.py:46
  27.2 9.5 %collective-permute-start.5 = (bf16[4,16,512]{2,1,0:T(8,128)(2,1)S(1)}, bf16[4,16,512]{2,1,0:T(8,128)(2,1)S(1)}, u32[]{:S(2)}, u32[]{:S(2)}) collective-permute-start(bf16[4,16,512]{2,1,0:T(8,128)(2,1)S(1)} %get-tuple-element.72.refs_5_), channel_id=1, source_target_pairs={{0,4},{4,0},{8,12},{12,8},{16,20},{20,16},{24,28},{28,24},{1,5},{5... | collective-permute-start | bytes 196616 | tf_op jit(solution)/shard_map/ppermute | solution.py:46
  36.7 11.0 %copy-start.2 = (f32[544,256]{1,0:T(8,128)}, f32[544,256]{1,0:T(8,128)S(1)}, u32[]{:S(2)}) copy-start(f32[544,256]{1,0:T(8,128)S(1)} %get-tuple-element.73.refs_7_.recip_ref) | copy-start | bytes 1671172
  47.6 4.0 %copy-start.6 = (f32[16,1536]{1,0:T(8,128)}, f32[16,1536]{1,0:T(8,128)S(1)}, u32[]{:S(2)}) copy-start(f32[16,1536]{1,0:T(8,128)S(1)} %get-tuple-element.77.upb_ref) | copy-start | bytes 294916
  47.6 4.0 %copy-start.8 = (f32[16,512]{1,0:T(8,128)}, f32[16,512]{1,0:T(8,128)S(1)}, u32[]{:S(2)}) copy-start(f32[16,512]{1,0:T(8,128)S(1)} %get-tuple-element.76.vec_ref.refs_9_.refs_7_) | copy-start | bytes 98308
  47.6 4.0 %copy-start.17 = (f32[1,1152]{1,0:T(1,128)}, f32[1,1152]{1,0:T(1,128)S(1)}, u32[]{:S(2)}) copy-start(f32[1,1152]{1,0:T(1,128)S(1)} %get-tuple-element.82.bias_ref) | copy-start | bytes 13828
  47.6 22.8 %copy-start.7 = (f32[16,512]{1,0:T(8,128)}, f32[16,512]{1,0:T(8,128)S(1)}, u32[]{:S(2)}) copy-start(f32[16,512]{1,0:T(8,128)S(1)} %get-tuple-element.79.refs_4_.taps_ref.refs_6_) | copy-start | bytes 98308
  47.7 5.0 %copy-start = (bf16[4,384,512]{2,1,0:T(8,128)(2,1)}, bf16[4,384,512]{2,1,0:T(8,128)(2,1)S(1)}, u32[]{:S(2)}) copy-start(bf16[4,384,512]{2,1,0:T(8,128)(2,1)S(1)} %stack_block0.1.even_ref.refs_10_.refs_8_) | copy-start | bytes 4718596
  47.8 3.8 %collective-permute-start.9 = (bf16[4,384,512]{2,1,0:T(8,128)(2,1)S(1)}, bf16[4,384,512]{2,1,0:T(8,128)(2,1)S(1)}, u32[]{:S(2)}, u32[]{:S(2)}) collective-permute-start(bf16[4,384,512]{2,1,0:T(8,128)(2,1)S(1)} %stack_block0.1.even_ref.refs_10_.refs_8_), channel_id=1, source_target_pairs={{0,4},{4,0},{8,12},{12,8},{16,20},{20,16},{24,28},{28,24},{1,5},{5... | collective-permute-start | bytes 4718600 | tf_op jit(solution)/shard_map/ppermute | solution.py:46
  51.6 1.2 copy-start.19
  130.8 4.8 %collective-permute-start.10 = (bf16[4,576,512]{2,1,0:T(8,128)(2,1)}, bf16[4,576,512]{2,1,0:T(8,128)(2,1)S(1)}, u32[]{:S(2)}, u32[]{:S(2)}) collective-permute-start(bf16[4,576,512]{2,1,0:T(8,128)(2,1)} %get-tuple-element.91), channel_id=1, source_target_pairs={{0,4},{4,0},{8,12},{12,8},{16,20},{20,16},{24,28},{28,24},{1,5},{5... | collective-permute-start | bytes 7077896 | tf_op jit(solution)/shard_map/ppermute | solution.py:46
  139.0 31.5 %collective-permute-start.12 = (bf16[576,512]{1,0:T(8,128)(2,1)}, bf16[576,512]{1,0:T(8,128)(2,1)S(1)}, u32[]{:S(2)}, u32[]{:S(2)}) collective-permute-start(bf16[576,512]{1,0:T(8,128)(2,1)} %get-tuple-element.99), channel_id=1, source_target_pairs={{0,8},{4,12},{8,0},{12,4},{16,24},{20,28},{24,16},{28,20},{1,9},{5... | collective-permute-start | bytes 1769480 | tf_op jit(solution)/shard_map/ppermute | solution.py:46
  140.7 29.8 %collective-permute-start.13 = (bf16[576,512]{1,0:T(8,128)(2,1)}, bf16[576,512]{1,0:T(8,128)(2,1)S(1)}, u32[]{:S(2)}, u32[]{:S(2)}) collective-permute-start(bf16[576,512]{1,0:T(8,128)(2,1)} %get-tuple-element.100), channel_id=1, source_target_pairs={{0,16},{4,20},{8,24},{12,28},{16,0},{20,4},{24,8},{28,12},{1,17},{... | collective-permute-start | bytes 1769480 | tf_op jit(solution)/shard_map/ppermute | solution.py:46
  142.2 28.3 %collective-permute-start.14 = (bf16[576,512]{1,0:T(8,128)(2,1)}, bf16[576,512]{1,0:T(8,128)(2,1)S(1)}, u32[]{:S(2)}, u32[]{:S(2)}) collective-permute-start(bf16[576,512]{1,0:T(8,128)(2,1)} %get-tuple-element.101), channel_id=1, source_target_pairs={{0,24},{4,28},{8,16},{12,20},{16,8},{20,12},{24,0},{28,4},{1,25},{... | collective-permute-start | bytes 1769480 | tf_op jit(solution)/shard_map/ppermute | solution.py:46
  142.5 28.0 %copy-start.18 = (f32[576,512]{1,0:T(8,128)S(1)}, f32[576,512]{1,0:T(8,128)}, u32[]{:S(2)}) copy-start(f32[576,512]{1,0:T(8,128)} %get-tuple-element.92.refs_12_.refs_0_) | copy-start | bytes 3538948
  170.4 3.8 %collective-permute-start.11 = (bf16[4,384,512]{2,1,0:T(8,128)(2,1)}, bf16[4,384,512]{2,1,0:T(8,128)(2,1)}, u32[]{:S(2)}, u32[]{:S(2)}) collective-permute-start(bf16[4,384,512]{2,1,0:T(8,128)(2,1)} %get-tuple-element.98), channel_id=1, source_target_pairs={{0,4},{4,0},{8,12},{12,8},{16,20},{20,16},{24,28},{28,24},{1,5},{5... | collective-permute-start | bytes 4718600 | tf_op jit(solution)/shard_map/ppermute | solution.py:46
  170.5 0.7 copy-start.15
  177.5 52.0 %all-reduce.2.cloned.1.call-start = ((), (), s32[]{:S(2)}) async-start(), calls=%async_computation | async-start | bytes 1179648 | tf_op jit(solution)/shard_map/psum | solution.py:1108
  177.5 22.7 %collective-permute-start.15 = (bf16[384,512]{1,0:T(8,128)(2,1)}, bf16[384,512]{1,0:T(8,128)(2,1)S(1)}, u32[]{:S(2)}, u32[]{:S(2)}) collective-permute-start(bf16[384,512]{1,0:T(8,128)(2,1)} %get-tuple-element.105), channel_id=1, source_target_pairs={{0,8},{4,12},{8,0},{12,4},{16,24},{20,28},{24,16},{28,20},{1,9},{5... | collective-permute-start | bytes 1179656 | tf_op jit(solution)/shard_map/ppermute | solution.py:46
  179.2 21.0 %collective-permute-start.16 = (bf16[384,512]{1,0:T(8,128)(2,1)}, bf16[384,512]{1,0:T(8,128)(2,1)S(1)}, u32[]{:S(2)}, u32[]{:S(2)}) collective-permute-start(bf16[384,512]{1,0:T(8,128)(2,1)} %get-tuple-element.106), channel_id=1, source_target_pairs={{0,16},{4,20},{8,24},{12,28},{16,0},{20,4},{24,8},{28,12},{1,17},{... | collective-permute-start | bytes 1179656 | tf_op jit(solution)/shard_map/ppermute | solution.py:46
  180.7 19.6 %collective-permute-start.17 = (bf16[384,512]{1,0:T(8,128)(2,1)}, bf16[384,512]{1,0:T(8,128)(2,1)S(1)}, u32[]{:S(2)}, u32[]{:S(2)}) collective-permute-start(bf16[384,512]{1,0:T(8,128)(2,1)} %get-tuple-element.107), channel_id=1, source_target_pairs={{0,24},{4,28},{8,16},{12,20},{16,8},{20,12},{24,0},{28,4},{1,25},{... | collective-permute-start | bytes 1179656 | tf_op jit(solution)/shard_map/ppermute | solution.py:46
  181.0 18.4 %copy-start.10 = (f32[16,512]{1,0:T(8,128)S(1)}, f32[16,512]{1,0:T(8,128)}, u32[]{:S(2)}) copy-start(f32[16,512]{1,0:T(8,128)} %get-tuple-element.110.mid_ref) | copy-start | bytes 98308
  181.0 18.4 %copy-start.11 = (f32[16,512]{1,0:T(8,128)S(1)}, f32[16,512]{1,0:T(8,128)}, u32[]{:S(2)}) copy-start(f32[16,512]{1,0:T(8,128)} %get-tuple-element.109.down0_ref) | copy-start | bytes 98308
  181.0 18.4 %copy-start.14 = (f32[1,1536]{1,0:T(1,128)S(1)}, f32[1,1536]{1,0:T(1,128)}, u32[]{:S(2)}) copy-start(f32[1,1536]{1,0:T(1,128)} %get-tuple-element.111.bias1_ref) | copy-start | bytes 18436
  181.1 18.4 %copy-start.16 = (f32[1,1536]{1,0:T(1,128)S(1)}, f32[1,1536]{1,0:T(1,128)}, u32[]{:S(2)}) copy-start(f32[1,1536]{1,0:T(1,128)} %get-tuple-element.102.refs_4_.bias0_ref) | copy-start | bytes 18436
  181.1 19.2 %copy-start.1 = (f32[384,512]{1,0:T(8,128)S(1)}, f32[384,512]{1,0:T(8,128)}, u32[]{:S(2)}) copy-start(f32[384,512]{1,0:T(8,128)} %get-tuple-element.103.refs_10_.refs_0_) | copy-start | bytes 2359300
  199.5 0.8 copy-start.12
  200.6 14.5 %collective-permute-start.18 = (bf16[96,512]{1,0:T(8,128)(2,1)S(1)}, bf16[96,512]{1,0:T(8,128)(2,1)S(1)}, u32[]{:S(2)}, u32[]{:S(2)}) collective-permute-start(bf16[96,512]{1,0:T(8,128)(2,1)S(1)} %get-tuple-element.113), channel_id=1, source_target_pairs={{0,1},{1,0},{2,3},{3,2},{4,5},{5,4},{6,7},{7,6},{8,9},{9,8},{10,11... | collective-permute-start | bytes 294920 | tf_op jit(solution)/shard_map/ppermute | solution.py:46
  203.3 12.8 %collective-permute-start.19 = (bf16[96,512]{1,0:T(8,128)(2,1)S(1)}, bf16[96,512]{1,0:T(8,128)(2,1)S(1)}, u32[]{:S(2)}, u32[]{:S(2)}) collective-permute-start(bf16[96,512]{1,0:T(8,128)(2,1)S(1)} %get-tuple-element.114), channel_id=1, source_target_pairs={{0,2},{1,3},{2,0},{3,1},{4,6},{5,7},{6,4},{7,5},{8,10},{9,11},{10,... | collective-permute-start | bytes 294920 | tf_op jit(solution)/shard_map/ppermute | solution.py:46
  205.8 10.3 %collective-permute-start.20 = (bf16[96,512]{1,0:T(8,128)(2,1)S(1)}, bf16[96,512]{1,0:T(8,128)(2,1)S(1)}, u32[]{:S(2)}, u32[]{:S(2)}) collective-permute-start(bf16[96,512]{1,0:T(8,128)(2,1)S(1)} %get-tuple-element.115), channel_id=1, source_target_pairs={{0,3},{1,2},{2,1},{3,0},{4,7},{5,6},{6,5},{7,4},{8,11},{9,10},{10,... | collective-permute-start | bytes 294920 | tf_op jit(solution)/shard_map/ppermute | solution.py:46
  216.2 13.3 %collective-permute-start.23 = (bf16[128,512]{1,0:T(8,128)(2,1)S(1)}, bf16[128,512]{1,0:T(8,128)(2,1)S(1)}, u32[]{:S(2)}, u32[]{:S(2)}) collective-permute-start(bf16[128,512]{1,0:T(8,128)(2,1)S(1)} %over_seq.1.refs_0_), channel_id=1, source_target_pairs={{0,3},{1,2},{2,1},{3,0},{4,7},{5,6},{6,5},{7,4},{8,11},{9,10},{10,... | collective-permute-start | bytes 393224 | tf_op jit(solution)/shard_map/ppermute | solution.py:46
  220.0 15.0 %collective-permute-start.22 = (bf16[128,512]{1,0:T(8,128)(2,1)S(1)}, bf16[128,512]{1,0:T(8,128)(2,1)S(1)}, u32[]{:S(2)}, u32[]{:S(2)}) collective-permute-start(bf16[128,512]{1,0:T(8,128)(2,1)S(1)} %over_seq.1.refs_0_), channel_id=1, source_target_pairs={{0,2},{1,3},{2,0},{3,1},{4,6},{5,7},{6,4},{7,5},{8,10},{9,11},{10,... | collective-permute-start | bytes 393224 | tf_op jit(solution)/shard_map/ppermute | solution.py:46
  228.1 6.9 %collective-permute-start.21 = (bf16[128,512]{1,0:T(8,128)(2,1)S(1)}, bf16[128,512]{1,0:T(8,128)(2,1)S(1)}, u32[]{:S(2)}, u32[]{:S(2)}) collective-permute-start(bf16[128,512]{1,0:T(8,128)(2,1)S(1)} %over_seq.1.refs_0_), channel_id=1, source_target_pairs={{0,1},{1,0},{2,3},{3,2},{4,5},{5,4},{6,7},{7,6},{8,9},{9,8},{10,11... | collective-permute-start | bytes 393224 | tf_op jit(solution)/shard_map/ppermute | solution.py:46
  235.0 1.1 copy-start.5
Sparse Core Ops, SparseCore 0:
  10.5 53.4 all-gather.3
  181.3 48.2 all-reduce.1
